TPU v7x, 32 devices: a whole 2x2x4 slice. The times are simulated.
32 devices in a mesh: parts: 2 (over x), vocab: 16 (over z, y, core).
Axes of the slice: x: 2, y: 2, z: 4, core: 2. Of those that a mesh axis runs over, the one named last changes fastest.
Arguments:
- emission: bfloat16 [8192, 4096], P(None, 'vocab'), may hold values from 0 to 0.9765625
- transition: bfloat16 [8192, 8192], P(None, 'vocab'), may hold values from 0 to 0.30517578
- beta_start: float32 [8192, 16], replicated, may hold values from 0.1 to 1
- allow_list: int32 [16, 8], replicated, may hold values from 0 to 15, as said below
- trans_table: int32 [16, 16], replicated, may hold values from 0 to 15
- last_token: int32 [32], P('parts'), parts along dimension 0, may hold values from 0 to 4095, as said below
- prompt_state: int32 [32], P('parts'), parts along dimension 0, may hold values from 0 to 15
- prior_msg: float32 [32, 8192], P(('parts', 'vocab')), parts along dimension 0, may hold values from 0 to 125
- lm_logits: bfloat16 [32, 4096], P('parts', 'vocab'), parts along dimension 0, may hold values from -12 to 275
Outputs:
- beta_end: float32 [16384, 16], P(('parts', 'vocab')), parts along dimension 0
- constrained: float32 [32, 4096], P('parts', 'vocab'), parts along dimension 0
There are 2 independent parts, one for each index of `parts`. A program takes and returns all parts, laid end to end along the dimension named above; an argument that names none is the same for every part. Nothing has to cross between parts.
Inputs may be any that keep to these rules, and one draw needn't show every extreme that they name: `allow_list`: each row lists 8 different blocks. `last_token`: each prompt's last token may be any token of the vocabulary.
All inputs are finite; a program needn't handle non-finite values.
Results may differ from a plain program's by a relative error of at most 0.00052.
Values may be sent and summed in bfloat16 or wider, within the bound.
No kernel may reach another device: no remote copies, remote signals or barrier semaphores. Data moves between devices by JAX's collectives and lax.ppermute only.
A program may use at most 64 MiB of HBM per device.

v0:
```python
import functools

import jax
import jax.numpy as jnp
from jax import lax
from jax.experimental import pallas as pl
from jax.experimental.pallas import tpu as pltpu
from jax.sharding import PartitionSpec as P

BLK = 256
STEPS = 3
LIMIT = 16 * 1024 * 1024
VMEM = pl.BlockSpec(memory_space=pltpu.VMEM)
SMEM = pl.BlockSpec(memory_space=pltpu.SMEM)
ANY = pl.BlockSpec(memory_space=pl.ANY)
PARAMS = pltpu.CompilerParams(vmem_limit_bytes=LIMIT)


def exchange(blocks):
    return lax.all_to_all(blocks, "vocab", split_axis=0, concat_axis=0, tiled=True)


def spread(own, devices):
    return exchange(jnp.broadcast_to(own[None], (devices,) + own.shape))


def basis(count):
    return [1, 3, 4] + [(1 << bit) | 1 for bit in range(3, count)]


def swap(block, offset, devices):
    pairs = [(i, i ^ offset) for i in range(devices)]
    return lax.ppermute(block, "vocab", pairs)


def split_wide(wide):
    high = wide.astype(jnp.bfloat16)
    low = (wide - high.astype(jnp.float32)).astype(jnp.bfloat16)
    return high, low


def split_outside(wide):
    high = lax.reduce_precision(wide, exponent_bits=8, mantissa_bits=7)
    return high.astype(jnp.bfloat16), (wide - high).astype(jnp.bfloat16)


def split_three(wide):
    high = wide.astype(jnp.bfloat16)
    rest = wide - high.astype(jnp.float32)
    middle = rest.astype(jnp.bfloat16)
    low = (rest - middle.astype(jnp.float32)).astype(jnp.bfloat16)
    return high, middle, low


def dot_rows(left, right):
    return lax.dot_general(left, right, (((1,), (1,)), ((), ())), preferred_element_type=jnp.float32)


def partner_of(bits, count):
    partner = 0
    for bit, offset in zip(bits, basis(count)):
        partner ^= bit * offset
    return partner


def all_bits(count):
    return [tuple((k >> (count - 1 - b)) & 1 for b in range(count)) for k in range(1 << count)]


def square_partners(count):
    return [partner_of((0,) + bits, count) for bits in all_bits(2)]


def far_partners(count):
    return [partner_of((0, 0, 0) + bits, count) for bits in all_bits(count - 3)]


def half_places(count, first):
    return [
        ((q, h), first ^ near ^ far)
        for q, near in enumerate(square_partners(count))
        for h, far in enumerate(far_partners(count))
    ]


def partner_rows(i, rows):
    owner = lax.axis_index("vocab") ^ i
    return pl.ds(pl.multiple_of(owner * rows, rows), rows)


def pack(blocks, wide, extra):
    rows = blocks.reshape(-1, blocks.shape[-1])
    parts = split_outside(rows) if wide else (rows.astype(jnp.bfloat16),)
    return jnp.concatenate(parts + extra, axis=0)


def unpack(packed, shape, wide):
    size = shape[0] * shape[1]
    rows = packed[:size].astype(jnp.float32)
    if wide:
        rows += packed[size : 2 * size].astype(jnp.float32)
    return rows.reshape(shape)


def reduce_blocks(kept, received, wide, devices, count, near_extra=(), far_extra=()):
    total = kept + received.astype(jnp.float32)
    near, extras = total[0], list(near_extra)
    for q, offset in enumerate(square_partners(count)):
        if q:
            packed = swap(pack(total[q], wide, near_extra), offset, devices)
            near += unpack(packed, total.shape[1:], wide)
            for extra in near_extra:
                extras.append(packed[-extra.shape[0] :])
    blocks = [near[0]]
    for h, offset in enumerate(far_partners(count)):
        if h:
            blocks.append(swap(pack(near[h], wide, far_extra), offset, devices))
    return blocks, extras


def gather_blocks(own, devices, count):
    far = jnp.stack([own] + [swap(own, offset, devices) for offset in far_partners(count)[1:]])
    near = jnp.stack([far] + [swap(far, offset, devices) for offset in square_partners(count)[1:]])
    return near, swap(near, 1, devices)


def column_of(scalars_ref, shape):
    row = lax.broadcasted_iota(jnp.int32, shape, 0)
    column = jnp.zeros(shape, jnp.int32)
    for k in range(shape[0]):
        column = jnp.where(row == k, scalars_ref[k], column)
    return column


def tables_kernel(
    count, state_ref, allow_ref, table_ref, emission_ref, sums_in_ref,
    route_ref, chooser_ref, sums_ref,
):
    device = lax.axis_index("vocab")
    devices = 1 << count
    states = table_ref.shape[0]
    sums_ref[...] = sums_in_ref[...]
    allow, table = allow_ref[...], table_ref[...]
    hits = [jnp.max((allow == b).astype(jnp.float32), axis=0, keepdims=True) for b in range(devices)]
    shape = (states, states)
    diagonal = [lax.broadcasted_iota(jnp.int32, shape, axis) for axis in (0, 1)]
    diagonal = (diagonal[0] == diagonal[1]).astype(jnp.bfloat16)
    hits = dot_rows(diagonal, jnp.concatenate(hits, axis=0).astype(jnp.bfloat16))
    ids = lax.broadcasted_iota(jnp.int32, shape, 1)
    own_step = jnp.zeros(shape, jnp.float32)
    for b in range(devices):
        step = jnp.where(table[:, b : b + 1] == ids, hits[:, b : b + 1], 0.0)
        own_step = jnp.where(device == b, step, own_step)
        step = step.astype(jnp.bfloat16)
        route_ref[pl.ds(b * states, states)] = jnp.concatenate([step] * 3, axis=1)
    shape = (states, devices)
    prompts = state_ref[...] == lax.broadcasted_iota(jnp.int32, shape, 0)
    chooser = lax.dot_general(
        prompts.astype(jnp.bfloat16),
        own_step.astype(jnp.bfloat16),
        (((0,), (0,)), ((), ())),
        preferred_element_type=jnp.float32,
    ).astype(jnp.bfloat16)
    chooser_ref[...] = jnp.concatenate([chooser] * 3, axis=1)


def tables(state, allow, table, emission, sums, count):
    devices, states = 1 << count, table.shape[0]
    return pl.pallas_call(
        functools.partial(tables_kernel, count),
        out_shape=[
            pltpu.VMEM((devices * states, 3 * states), jnp.bfloat16),
            pltpu.VMEM((devices, 3 * states), jnp.bfloat16),
            jax.ShapeDtypeStruct(sums.shape, sums.dtype),
        ],
        in_specs=[VMEM] * 5,
        out_specs=[VMEM] * 3,
        compiler_params=PARAMS,
        name="tables",
    )(state, allow, table, emission, sums)


def products_kernel(
    count, token_hbm, state_hbm, allow_hbm, table_hbm, start_hbm, emission_ref,
    sums_ref, kept_ref, sent_ref, state_ref, allow_ref, table_ref, messages_ref,
    token_ref, columns_ref, sems,
):
    device = lax.axis_index("vocab")
    devices = 1 << count
    rows = emission_ref.shape[0] >> count
    own = pl.ds(pl.multiple_of(device * rows, rows), rows)
    pairs = [
        (token_hbm, token_ref), (state_hbm, state_ref), (allow_hbm, allow_ref),
        (table_hbm, table_ref), (start_hbm.at[:, own], messages_ref),
    ]
    copies = [
        pltpu.make_async_copy(source, to, sems.at[k]) for k, (source, to) in enumerate(pairs)
    ]
    for copy in copies:
        copy.start()
    shape = (devices * devices // 2, devices * devices)
    to, source = (lax.broadcasted_iota(jnp.int32, shape, axis) for axis in (0, 1))
    same_block = (to & (devices - 1)) == (source >> count)
    orders = []
    for first in range(2):
        prompt = partner_at((to >> count) + first * (devices // 2), count)
        onehot = same_block & ((source & (devices - 1)) == prompt)
        orders.append(onehot.astype(jnp.bfloat16))
    copies[0].wait()
    shape = (devices, BLK)
    tokens = column_of(token_ref, shape) - device * BLK
    onehot = (tokens == lax.broadcasted_iota(jnp.int32, shape, 1)).astype(jnp.bfloat16)
    left = jnp.concatenate([onehot, jnp.ones((16, BLK), jnp.bfloat16)], axis=0)
    for k in range(devices):
        product = dot_rows(left, emission_ref[pl.ds(k * rows, rows)])
        columns_ref[pl.ds(k * devices, devices)] = product[:devices].astype(jnp.bfloat16)
        sums_ref[k] = product[devices : devices + 1]
    for order, out_ref in zip(orders, (kept_ref, sent_ref)):
        ordered = jnp.dot(order, columns_ref[...], preferred_element_type=jnp.float32)
        out_ref[...] = ordered.astype(jnp.bfloat16).reshape(out_ref.shape)
    for copy in copies[1:]:
        copy.wait()


def first_products(last_token, prompt_state, allow_list, trans_table, beta_start, emission, count):
    devices, rows = 1 << count, emission.shape[0] >> count
    half = pltpu.VMEM((4, devices // 8, devices, rows), jnp.bfloat16)
    small = (prompt_state[None], allow_list.T, trans_table)
    operands = (last_token,) + small + (beta_start.T,)
    return pl.pallas_call(
        functools.partial(products_kernel, count),
        out_shape=[jax.ShapeDtypeStruct((devices, 1, rows), jnp.float32), half, half]
        + [pltpu.VMEM(array.shape, array.dtype) for array in small]
        + [pltpu.VMEM((beta_start.shape[1], rows), jnp.float32)],
        in_specs=[ANY] * len(operands) + [VMEM],
        out_specs=[VMEM] * 7,
        scratch_shapes=[
            pltpu.SMEM(last_token.shape, jnp.int32),
            pltpu.VMEM((devices * devices, rows), jnp.bfloat16),
            pltpu.SemaphoreType.DMA((len(operands),)),
        ],
        compiler_params=PARAMS,
        name="first_products",
    )(*(in_hbm(operand) for operand in operands), emission)


def in_hbm(array):
    return pltpu.with_memory_space_constraint(array, pltpu.HBM)


def forward_kernel(prior_ref, *refs):
    blocks, out_ref = refs[:-1], refs[-1]
    devices, rows = out_ref.shape
    columns = blocks[0][-devices:]
    for block in blocks[1:]:
        columns += block[-devices:].astype(jnp.float32)
    prior = jnp.concatenate([prior_ref[:, pl.ds(k * rows, rows)] for k in range(devices)], axis=0)
    unnormal = prior * columns
    out_ref[...] = (unnormal / jnp.sum(unnormal)).astype(jnp.bfloat16)


def forward_messages_here(prior, blocks, devices):
    return pl.pallas_call(
        forward_kernel,
        out_shape=pltpu.VMEM((devices, blocks[0].shape[1]), jnp.bfloat16),
        in_specs=[VMEM] * (1 + len(blocks)),
        out_specs=VMEM,
        compiler_params=PARAMS,
        name="forward_messages",
    )(prior, *blocks)


def partner_at(place, count):
    number = jnp.zeros_like(place)
    for bit, offset in enumerate(basis(count)):
        number = number ^ (((place >> (count - 1 - bit)) & 1) * offset)
    return lax.axis_index("vocab") ^ number


def order_kernel(count, near_ref, far_ref, out_ref):
    size = 1 << count
    shape = (size * size, size * size)
    to, source = (lax.broadcasted_iota(jnp.int32, shape, axis) for axis in (0, 1))
    same_block = partner_at(to >> count, count) == (source & (size - 1))
    same_prompt = (to & (size - 1)) == partner_at(source >> count, count)
    onehot = (same_block & same_prompt).astype(jnp.bfloat16)
    half = size * size // 2
    rows = out_ref.shape[1]
    near = near_ref[...].reshape(half, rows)
    far = far_ref[...].reshape(half, rows)
    ordered = jnp.dot(onehot[:, :half], near, preferred_element_type=jnp.float32)
    ordered += jnp.dot(onehot[:, half:], far, preferred_element_type=jnp.float32)
    out_ref[...] = ordered.astype(jnp.bfloat16)


def order_forward(near, far, count):
    rows = near.shape[-1]
    return pl.pallas_call(
        functools.partial(order_kernel, count),
        out_shape=pltpu.VMEM((1 << (2 * count), rows), jnp.bfloat16),
        in_specs=[VMEM] * 2,
        out_specs=VMEM,
        compiler_params=PARAMS,
        name="order_forward",
    )(near, far)


def last_kernel(*refs):
    blocks, out_ref = refs[:-2], refs[-1]
    states = out_ref.shape[0]
    messages = blocks[0][...]
    for block in blocks[1:]:
        for part in range(2):
            messages += block[pl.ds(part * states, states)].astype(jnp.float32)
    out_ref[...] = messages


def last_sum(blocks, after):
    return pl.pallas_call(
        last_kernel,
        out_shape=pltpu.VMEM(blocks[0].shape, jnp.float32),
        in_specs=[VMEM] * len(blocks) + [ANY],
        out_specs=VMEM,
        compiler_params=PARAMS,
        name="last_messages",
    )(*blocks, after)


def half_products(halves, transition_ref, out_ref, count, first):
    states = halves.shape[0] // 2
    rows = transition_ref.shape[0] >> count
    for place, partner in half_places(count, first):
        product = dot_rows(halves, transition_ref[partner_rows(partner, rows)])
        product = product[:states] + product[states:]
        out_ref[place + (pl.ds(0, states),)] = product.astype(out_ref.dtype)


def add_rows(out_ref, states, extra):
    for ref in extra:
        rows = pl.ds(states, ref.shape[2])
        for place in ((y, k) for y in range(ref.shape[0]) for k in range(ref.shape[1])):
            out_ref[place + (rows,)] = ref[place].astype(out_ref.dtype)


def send_kernel(count, number, transition_ref, route_ref, sums_ref, *refs):
    parts, extra, (halves_ref, out_ref) = refs[:number], refs[number:-2], refs[-2:]
    states = halves_ref.shape[0] // 2
    messages = parts[0][:states].astype(jnp.float32)
    for part in parts[1:]:
        messages += part[:states].astype(jnp.float32)
    selected = jnp.dot(
        route_ref[...],
        jnp.concatenate(split_three(messages), axis=0),
        preferred_element_type=jnp.float32,
    )
    emitted = selected[:states] * sums_ref[0]
    for b in range(1, 1 << count):
        emitted += selected[b * states : (b + 1) * states] * sums_ref[b]
    halves = jnp.concatenate(split_wide(emitted), axis=0)
    halves_ref[...] = halves
    half_products(halves, transition_ref, out_ref, count, 1)
    add_rows(out_ref, states, extra)


def keep_kernel(count, transition_ref, halves_ref, *refs):
    extra, out_ref = refs[:-1], refs[-1]
    half_products(halves_ref[...], transition_ref, out_ref, count, 0)
    add_rows(out_ref, halves_ref.shape[0] // 2, extra)


def step(transition, route, sums, parts, dtype, devices, count, kept_rows=(), sent_rows=()):
    states, rows = route.shape[0] // devices, parts[0].shape[1]
    total = states + sum(block.shape[2] for block in kept_rows)
    shape = (4, devices // 8, total, rows)
    halves, sent = pl.pallas_call(
        functools.partial(send_kernel, count, len(parts)),
        out_shape=[
            pltpu.VMEM((2 * states, rows), jnp.bfloat16),
            pltpu.VMEM(shape, dtype),
        ],
        in_specs=[VMEM] * (3 + len(parts) + len(sent_rows)),
        out_specs=[VMEM] * 2,
        compiler_params=PARAMS,
        name="step_sent_half",
    )(transition, route, sums, *parts, *sent_rows)
    received = swap(sent, 1, devices)
    kept = pl.pallas_call(
        functools.partial(keep_kernel, count),
        out_shape=pltpu.VMEM(shape, jnp.float32),
        in_specs=[VMEM] * (2 + len(kept_rows)),
        out_specs=VMEM,
        compiler_params=PARAMS,
        name="step_kept_half",
    )(transition, halves, *kept_rows)
    return kept, received


def weigh_half(emission_ref, forward_ref, chooser, parts_ref, count, first):
    rows = emission_ref.shape[0] >> count
    prompts = chooser.shape[0]
    weights = jnp.zeros((prompts, emission_ref.shape[1]), jnp.float32)
    for order, (place, partner) in enumerate(half_places(count, first)):
        pieces = jnp.concatenate(split_three(parts_ref[place]), axis=0)
        chosen = jnp.dot(chooser, pieces, preferred_element_type=jnp.float32)
        block = order + (first << (count - 1))
        forward = forward_ref[pl.ds(block * prompts, prompts)].astype(jnp.float32)
        scaled = (forward * chosen).astype(jnp.bfloat16)
        tile = emission_ref[partner_rows(partner, rows)]
        weights += jnp.dot(scaled, tile, preferred_element_type=jnp.float32)
    return weights


def near_kernel(count, emission_ref, forward_ref, chooser_ref, parts_ref, out_ref):
    out_ref[...] = weigh_half(emission_ref, forward_ref, chooser_ref[...], parts_ref, count, 0)


def far_kernel(count, emission_ref, forward_ref, chooser_ref, logits_ref, near_ref, parts_ref, raised_ref, pair_ref):
    chooser = chooser_ref[...]
    logits = logits_ref[...].astype(jnp.float32)
    top = jnp.max(logits, axis=1, keepdims=True)
    weights = near_ref[...] + weigh_half(emission_ref, forward_ref, chooser, parts_ref, count, 1)
    allowed = jnp.sum(chooser.astype(jnp.float32), axis=1, keepdims=True) > 0
    raised = jnp.where(allowed, jnp.exp(logits - top) * weights, 0.0)
    raised_ref[...] = raised
    total = jnp.sum(raised, axis=1, keepdims=True)
    lane = lax.broadcasted_iota(jnp.int32, pair_ref.shape, 1)
    pair_ref[...] = jnp.where(lane == 0, top, total)


def weigh(emission, forward, chooser, logits, near, far, count):
    half = pl.pallas_call(
        functools.partial(near_kernel, count),
        out_shape=pltpu.VMEM(logits.shape, jnp.float32),
        in_specs=[VMEM] * 4,
        out_specs=VMEM,
        compiler_params=PARAMS,
        name="weigh_near",
    )(emission, forward, chooser, near)
    return pl.pallas_call(
        functools.partial(far_kernel, count),
        out_shape=[
            pltpu.VMEM(logits.shape, jnp.float32),
            pltpu.VMEM((logits.shape[0], 128), jnp.float32),
        ],
        in_specs=[VMEM] * 6,
        out_specs=[VMEM] * 2,
        compiler_params=PARAMS,
        name="weigh_far",
    )(emission, forward, chooser, logits, half, far)


def normalise(raised, pair, devices):
    pairs = spread(pair[:, :2].T, devices)
    own_top = pair[:, :1]
    tops, totals = pairs[:, 0], pairs[:, 1]
    top = jnp.max(tops, axis=0)
    total = jnp.sum(totals * jnp.exp(tops - top), axis=0)
    return BLK * devices * (raised * jnp.exp(own_top - top[:, None])) / total[:, None]


def forward_messages(emission, last_token, prior_msg, devices, device):
    hidden = emission.shape[0]
    local_rows = prior_msg.shape[0]
    token_ids = jnp.arange(BLK, dtype=jnp.int32)
    tokens = last_token - device * BLK
    onehot = (tokens[:, None] == token_ids[None, :]).astype(jnp.bfloat16)
    owned = dot_rows(onehot, emission)
    owned = owned.astype(jnp.bfloat16).reshape(devices, local_rows, hidden)
    columns = jnp.sum(exchange(owned), axis=0, dtype=jnp.float32)
    unnormal = prior_msg * columns
    forward_msg = (unnormal / jnp.sum(unnormal, axis=1, keepdims=True)).astype(jnp.bfloat16)
    return spread(forward_msg, devices).reshape(devices * local_rows, hidden)


def per_device(
    emission,
    transition,
    beta_start,
    allow_list,
    trans_table,
    last_token,
    prompt_state,
    prior_msg,
    lm_logits,
):
    devices = lax.axis_size("vocab")
    device = lax.axis_index("vocab")
    hidden = emission.shape[0]
    states = beta_start.shape[1]
    own_rows = transition.shape[1]
    prompts = prompt_state.shape[0]
    count = devices.bit_length() - 1
    if devices == 1 << count and count > 2 and own_rows % 128 == 0 and prompts == devices:
        sums, columns, columns_out, state, allow, table, messages = first_products(
            last_token, prompt_state, allow_list, trans_table, beta_start, emission, count
        )
        route, chooser, sums = tables(state, allow, table, emission, sums, count)
        sums = exchange(sums)
        parts, kept_rows, sent_rows = [messages], (columns,), (columns_out,)
        for window_step in range(STEPS):
            wide = window_step == STEPS - 1
            dtype = jnp.float32 if wide else jnp.bfloat16
            kept, received = step(
                transition, route, sums, parts, dtype, devices, count, kept_rows, sent_rows
            )
            kept_rows, sent_rows, near_extra, far_extra = (), (), (), ()
            if window_step == 1:
                forward = forward_messages_here(prior_msg, parts, devices)
                far_extra = (forward,)
            if window_step == 2:
                near_extra = (forward,)
            parts, extras = reduce_blocks(
                kept, received, wide, devices, count, near_extra, far_extra
            )
            if window_step == 1:
                others = [part[-devices:] for part in parts[1:]]
                forward = jnp.concatenate([forward] + others, axis=0)
        near = jnp.stack(extras).reshape(4, devices // 8, devices, own_rows)
        forward = order_forward(near, swap(near, 1, devices), count)
        messages = last_sum(parts, forward)
        near, far = gather_blocks(messages, devices, count)
        raised, pair = weigh(emission, forward, chooser, lm_logits, near, far, count)
        return messages.T, normalise(raised, pair, devices)
    state_ids = jnp.arange(states, dtype=jnp.int32)
    block_ids = jnp.arange(devices, dtype=jnp.int32)
    allowed = jnp.any(allow_list[:, :, None] == block_ids, axis=1)
    dest_here = lax.dynamic_index_in_dim(trans_table, device, axis=1, keepdims=False)
    allow_here = jnp.any(allow_list == device, axis=1)
    dest_rows = jnp.sum(jnp.where(prompt_state[:, None] == state_ids, dest_here, 0), axis=1)
    allow_rows = jnp.any((prompt_state[:, None] == state_ids) & allow_here, axis=1)
    chooser = (dest_rows[:, None] == state_ids) & allow_rows[:, None]
    messages = lax.dynamic_slice_in_dim(beta_start, device * own_rows, own_rows, 0).T
    forward_all = forward_messages(emission, last_token, prior_msg, devices, device)
    own_sums = exchange(jnp.sum(emission, axis=1, dtype=jnp.float32).reshape(devices, own_rows))
    route = allowed.T[:, :, None] & (trans_table.T[:, :, None] == state_ids)
    route = route.astype(jnp.float32).reshape(devices * states, states)
    by_owner = transition.reshape(devices, own_rows, own_rows)
    for window_step in range(STEPS):
        selected = jnp.dot(route, messages, precision=lax.Precision.HIGHEST)
        selected = selected.reshape(devices, states, own_rows)
        emitted = jnp.sum(selected * own_sums[:, None, :], axis=0)
        halves = jnp.concatenate(split_outside(emitted), axis=0)
        partial = jnp.einsum("dzy,sy->dsz", by_owner, halves, preferred_element_type=jnp.float32)
        partial = partial[:, :states] + partial[:, states:]
        if window_step < STEPS - 1:
            partial = partial.astype(jnp.bfloat16)
        messages = jnp.sum(exchange(partial), axis=0, dtype=jnp.float32)
    everywhere = spread(messages, devices)
    chosen = jnp.einsum(
        "ps,dsz->pdz", chooser.astype(jnp.float32), everywhere, precision=lax.Precision.HIGHEST
    )
    forward_all = forward_all.reshape(prompts, devices, own_rows).astype(jnp.float32)
    scaled = (forward_all * chosen).astype(jnp.bfloat16).reshape(prompts, hidden)
    weights = jnp.dot(scaled, emission, preferred_element_type=jnp.float32)
    weights = jnp.where(allow_rows[:, None], weights, 0.0)
    logits = lm_logits.astype(jnp.float32)
    top_here = jnp.max(logits, axis=1)
    raised = jnp.exp(logits - top_here[:, None]) * weights
    pairs = spread(jnp.stack([top_here, jnp.sum(raised, axis=1)]), devices)
    tops, totals = pairs[:, 0], pairs[:, 1]
    top = jnp.max(tops, axis=0)
    total = jnp.sum(totals * jnp.exp(tops - top), axis=0)
    raised = raised * jnp.exp(top_here - top)[:, None]
    return (messages.T, BLK * devices * raised / total[:, None])


def solution(mesh):
    return jax.shard_map(
        per_device,
        mesh=mesh,
        in_specs=(
            P(None, "vocab"),
            P(None, "vocab"),
            P(),
            P(),
            P(),
            P("parts"),
            P("parts"),
            P(("parts", "vocab"), None),
            P("parts", "vocab"),
        ),
        out_specs=(P(("parts", "vocab"), None), P("parts", "vocab")),
        check_vma=False,
    )
```

profile of v0, /device:TPU:0, one launch (start us, length us, event | category | flops | bytes accessed | tf_op | source)
XLA Modules:
  0.0 90.2 jit_solution(2809910379178580093)
XLA Ops:
  0.7 2.3 %copy-done.1 = bf16[8192,256]{1,0:T(8,128)(2,1)S(1)} copy-done((bf16[8192,256]{1,0:T(8,128)(2,1)S(1)}, bf16[8192,256]{1,0:T(8,128)(2,1)}, u32[]{:S(2)}) %copy-start.1) | copy-done | bytes 4194328
  3.0 2.4 %first_products.1 = (f32[16,1,512]{2,1,0:T(1,128)S(1)}, bf16[4,2,16,512]{3,2,1,0:T(8,128)(2,1)S(1)}, bf16[4,2,16,512]{3,2,1,0:T(8,128)(2,1)S(1)}, s32[1,16]{1,0:...) custom-call(s32[16]{0:T(128)} %token_hbm.1, s32[1,16]{1,0:T(1,128)} %bitcast.123, ...), custom_call_target="tpu_custom_call" | custom-call | tf_op jit(solution)/shard_map/first_products/pallas_call | solution.py:230
  5.8 13.8 %all_to_all.10.sums_ref = f32[16,1,512]{2,1,0:T(1,128)S(1)} all-to-all(f32[16,1,512]{2,1,0:T(1,128)S(1)} %get-tuple-element.25), channel_id=1, replica_groups=mesh['parts'=2,'vocab'=16] {'vocab'}, dimensions={0} | all-to-all | bytes 65536 | tf_op jit(solution)/shard_map/all_to_all | solution.py:20
  19.6 1.5 %step_sent_half.3 = (bf16[32,512]{1,0:T(8,128)(2,1)S(1)}, bf16[4,2,32,512]{3,2,1,0:T(8,128)(2,1)S(1)}) custom-call(bf16[8192,512]{1,0:T(8,128)(2,1)S(1)} %copy-done, bf16[256,48]{1,0:T(8,128)(2,1)S(1)} %get-tuple-element.24.route_ref, f32[16,1,512]{2,1,0:T(1,128)S(1)} %all_to_all.10.sums_ref, f32[16,512]{1,0:T(8,128)S(1)} %get-tuple-element.26.refs_0_, ...), custom_call_target="tpu_custom_call" | custom-call | tf_op jit(solution)/shard_map/step_sent_half/pallas_call | solution.py:375
  21.1 1.3 %step_kept_half.3 = f32[4,2,32,512]{3,2,1,0:T(8,128)S(1)} custom-call(bf16[8192,512]{1,0:T(8,128)(2,1)S(1)} %copy-done, bf16[32,512]{1,0:T(8,128)(2,1)S(1)} %get-tuple-element.28.halves_ref, bf16[4,2,16,512]{3,2,1,0:T(8,128)(2,1)S(1)} %get-tuple-element.29.refs_0_), custom_call_target="tpu_custom_call" | custom-call | tf_op jit(solution)/shard_map/step_kept_half/pallas_call | solution.py:387
  23.1 1.4 %collective-permute-start.1 = (bf16[64,512]{1,0:T(8,128)(2,1)S(1)}, bf16[64,512]{1,0:T(8,128)(2,1)S(1)}, u32[]{:S(2)}, u32[]{:S(2)}) collective-permute-start(bf16[64,512]{1,0:T(8,128)(2,1)S(1)} %bitcast.109), channel_id=1, source_target_pairs={{0,4},{1,5},{2,6},{3,7},{4,0},{5,1},{6,2},{7,3},{8,12},{9,13},{10,... | collective-permute-start | bytes 196616 | tf_op jit(solution)/shard_map/ppermute | solution.py:33
  25.7 2.0 %collective-permute-done.3 = bf16[64,512]{1,0:T(8,128)(2,1)S(1)} collective-permute-done((bf16[64,512]{1,0:T(8,128)(2,1)S(1)}, bf16[64,512]{1,0:T(8,128)(2,1)S(1)}, u32[]{:S(2)}, u32[]{:S(2)}) %collective-permute-start.3) | collective-permute-done | bytes 65568 | tf_op jit(solution)/shard_map/ppermute | solution.py:33
  29.7 5.0 %collective-permute-done.4.refs_1_ = bf16[32,512]{1,0:T(8,128)(2,1)S(1)} collective-permute-done((bf16[32,512]{1,0:T(8,128)(2,1)S(1)}, bf16[32,512]{1,0:T(8,128)(2,1)S(1)}, u32[]{:S(2)}, u32[]{:S(2)}) %collective-permute-start.4) | collective-permute-done | bytes 32800 | tf_op jit(solution)/shard_map/ppermute | solution.py:33
  34.7 1.4 %step_sent_half.4 = (bf16[32,512]{1,0:T(8,128)(2,1)S(1)}, bf16[4,2,16,512]{3,2,1,0:T(8,128)(2,1)S(1)}) custom-call(bf16[8192,512]{1,0:T(8,128)(2,1)S(1)} %copy-done, bf16[256,48]{1,0:T(8,128)(2,1)S(1)} %get-tuple-element.24.route_ref, f32[16,1,512]{2,1,0:T(1,128)S(1)} %all_to_all.10.sums_ref, f32[32,512]{1,0:T(8,128)S(1)} %slice_bitcast_fusion.3.refs_0_, ...), custom_call_target="tpu_custom_call" | custom-call | tf_op jit(solution)/shard_map/step_sent_half/pallas_call | solution.py:375
  36.2 1.3 %step_kept_half.4 = f32[4,2,16,512]{3,2,1,0:T(8,128)S(1)} custom-call(bf16[8192,512]{1,0:T(8,128)(2,1)S(1)} %copy-done, bf16[32,512]{1,0:T(8,128)(2,1)S(1)} %get-tuple-element.31.halves_ref), custom_call_target="tpu_custom_call" | custom-call | tf_op jit(solution)/shard_map/step_kept_half/pallas_call | solution.py:387
  37.7 2.4 %collective-permute-start.6 = (bf16[32,512]{1,0:T(8,128)(2,1)S(1)}, bf16[32,512]{1,0:T(8,128)(2,1)S(1)}, u32[]{:S(2)}, u32[]{:S(2)}) collective-permute-start(bf16[32,512]{1,0:T(8,128)(2,1)S(1)} %bitcast.119), channel_id=1, source_target_pairs={{0,4},{1,5},{2,6},{3,7},{4,0},{5,1},{6,2},{7,3},{8,12},{9,13},{10,... | collective-permute-start | bytes 98312 | tf_op jit(solution)/shard_map/ppermute | solution.py:33
  42.5 1.3 %collective-permute-done.7 = bf16[32,512]{1,0:T(8,128)(2,1)S(1)} collective-permute-done((bf16[32,512]{1,0:T(8,128)(2,1)S(1)}, bf16[32,512]{1,0:T(8,128)(2,1)S(1)}, u32[]{:S(2)}, u32[]{:S(2)}) %collective-permute-start.7) | collective-permute-done | bytes 32800 | tf_op jit(solution)/shard_map/ppermute | solution.py:33
  43.9 4.9 %collective-permute-done.9.refs_1_ = bf16[32,512]{1,0:T(8,128)(2,1)S(1)} collective-permute-done((bf16[32,512]{1,0:T(8,128)(2,1)S(1)}, bf16[32,512]{1,0:T(8,128)(2,1)S(1)}, u32[]{:S(2)}, u32[]{:S(2)}) %collective-permute-start.9) | collective-permute-done | bytes 32800 | tf_op jit(solution)/shard_map/ppermute | solution.py:33
  48.9 1.4 %step_sent_half.5 = (bf16[32,512]{1,0:T(8,128)(2,1)S(1)}, f32[4,2,16,512]{3,2,1,0:T(8,128)S(1)}) custom-call(bf16[8192,512]{1,0:T(8,128)(2,1)S(1)} %copy-done, bf16[256,48]{1,0:T(8,128)(2,1)S(1)} %get-tuple-element.24.route_ref, f32[16,1,512]{2,1,0:T(1,128)S(1)} %all_to_all.10.sums_ref, f32[16,512]{1,0:T(8,128)S(1)} %slice_bitcast_fusion.6.refs_0_, ...), custom_call_target="tpu_custom_call" | custom-call | tf_op jit(solution)/shard_map/step_sent_half/pallas_call | solution.py:375
  53.1 2.2 %collective-permute-start.13 = (bf16[96,512]{1,0:T(8,128)(2,1)S(1)}, bf16[96,512]{1,0:T(8,128)(2,1)S(1)}, u32[]{:S(2)}, u32[]{:S(2)}) collective-permute-start(bf16[96,512]{1,0:T(8,128)(2,1)S(1)} %get-tuple-element.63), channel_id=1, source_target_pairs={{0,7},{1,6},{2,5},{3,4},{4,3},{5,2},{6,1},{7,0},{8,15},{9,14},{10,... | collective-permute-start | bytes 294920 | tf_op jit(solution)/shard_map/ppermute | solution.py:33
  55.3 2.3 %collective-permute-done.11 = bf16[96,512]{1,0:T(8,128)(2,1)S(1)} collective-permute-done((bf16[96,512]{1,0:T(8,128)(2,1)S(1)}, bf16[96,512]{1,0:T(8,128)(2,1)S(1)}, u32[]{:S(2)}, u32[]{:S(2)}) %collective-permute-start.11) | collective-permute-done | bytes 98336 | tf_op jit(solution)/shard_map/ppermute | solution.py:33
  57.7 1.4 %collective-permute-done.13 = bf16[96,512]{1,0:T(8,128)(2,1)S(1)} collective-permute-done((bf16[96,512]{1,0:T(8,128)(2,1)S(1)}, bf16[96,512]{1,0:T(8,128)(2,1)S(1)}, u32[]{:S(2)}, u32[]{:S(2)}) %collective-permute-start.13) | collective-permute-done | bytes 98336 | tf_op jit(solution)/shard_map/ppermute | solution.py:33
  61.1 2.4 %collective-permute-done.14.refs_1_ = bf16[32,512]{1,0:T(8,128)(2,1)S(1)} collective-permute-done((bf16[32,512]{1,0:T(8,128)(2,1)S(1)}, bf16[32,512]{1,0:T(8,128)(2,1)S(1)}, u32[]{:S(2)}, u32[]{:S(2)}) %collective-permute-start.14) | collective-permute-done | bytes 32800 | tf_op jit(solution)/shard_map/ppermute | solution.py:33
  63.8 4.0 %collective-permute-done.16 = f32[16,512]{1,0:T(8,128)S(1)} collective-permute-done((f32[16,512]{1,0:T(8,128)S(1)}, f32[16,512]{1,0:T(8,128)S(1)}, u32[]{:S(2)}, u32[]{:S(2)}) %collective-permute-start.16) | collective-permute-done | bytes 32800 | tf_op jit(solution)/shard_map/ppermute | solution.py:33
  68.9 2.0 %collective-permute-start.17 = (f32[2,16,512]{2,1,0:T(8,128)S(1)}, f32[2,16,512]{2,1,0:T(8,128)S(1)}, u32[]{:S(2)}, u32[]{:S(2)}) collective-permute-start(f32[2,16,512]{2,1,0:T(8,128)S(1)} %get-tuple-element.52), channel_id=1, source_target_pairs={{0,4},{1,5},{2,6},{3,7},{4,0},{5,1},{6,2},{7,3},{8,12},{9,13},{10,... | collective-permute-start | bytes 196616 | tf_op jit(solution)/shard_map/ppermute | solution.py:33
  71.7 1.8 %collective-permute-done.17 = f32[2,16,512]{2,1,0:T(8,128)S(1)} collective-permute-done((f32[2,16,512]{2,1,0:T(8,128)S(1)}, f32[2,16,512]{2,1,0:T(8,128)S(1)}, u32[]{:S(2)}, u32[]{:S(2)}) %collective-permute-start.17) | collective-permute-done | bytes 65568 | tf_op jit(solution)/shard_map/ppermute | solution.py:33
  73.5 2.4 %collective-permute-done.19 = f32[2,16,512]{2,1,0:T(8,128)S(1)} collective-permute-done((f32[2,16,512]{2,1,0:T(8,128)S(1)}, f32[2,16,512]{2,1,0:T(8,128)S(1)}, u32[]{:S(2)}, u32[]{:S(2)}) %collective-permute-start.19) | collective-permute-done | bytes 65568 | tf_op jit(solution)/shard_map/ppermute | solution.py:33
  79.3 3.5 %all-to-all-start.1 = ((f32[16,2,16]{2,1,0:T(2,128)}), f32[16,2,16]{2,1,0:T(2,128)S(1)}, u32[]{:S(2)}, u32[]{:S(2)}) async-start(f32[16,2,16]{2,1,0:T(2,128)} %broadcast_in_dim.7), calls=%async_computation.1 | async-start | bytes 32768 | tf_op jit(solution)/shard_map/all_to_all | solution.py:20
  83.4 5.8 %all-to-all-done.1 = f32[16,2,16]{2,1,0:T(2,128)S(1)} async-done(((f32[16,2,16]{2,1,0:T(2,128)}), f32[16,2,16]{2,1,0:T(2,128)S(1)}, u32[]{:S(2)}, u32[]{:S(2)}) %all-to-all-start.1) | async-done | bytes 2080 | tf_op jit(solution)/shard_map/all_to_all | solution.py:20
  (85 shorter events, 18.9 us)
Async XLA Ops:
  21.1 1.6 %collective-permute-start = (bf16[4,2,32,512]{3,2,1,0:T(8,128)(2,1)S(1)}, bf16[4,2,32,512]{3,2,1,0:T(8,128)(2,1)S(1)}, u32[]{:S(2)}, u32[]{:S(2)}) collective-permute-start(bf16[4,2,32,512]{3,2,1,0:T(8,128)(2,1)S(1)} %get-tuple-element.30), channel_id=1, source_target_pairs={{0,1},{1,0},{2,3},{3,2},{4,5},{5,4},{6,7},{7,6},{8,9},{9,8},{10,11... | collective-permute-start | bytes 786440 | tf_op jit(solution)/shard_map/ppermute | solution.py:33
  22.8 5.0 %collective-permute-start.3 = (bf16[64,512]{1,0:T(8,128)(2,1)S(1)}, bf16[64,512]{1,0:T(8,128)(2,1)S(1)}, u32[]{:S(2)}, u32[]{:S(2)}) collective-permute-start(bf16[64,512]{1,0:T(8,128)(2,1)S(1)} %bitcast.110), channel_id=1, source_target_pairs={{0,7},{1,6},{2,5},{3,4},{4,3},{5,2},{6,1},{7,0},{8,15},{9,14},{10,... | collective-permute-start | bytes 196616 | tf_op jit(solution)/shard_map/ppermute | solution.py:33
  23.1 5.3 %collective-permute-start.1 = (bf16[64,512]{1,0:T(8,128)(2,1)S(1)}, bf16[64,512]{1,0:T(8,128)(2,1)S(1)}, u32[]{:S(2)}, u32[]{:S(2)}) collective-permute-start(bf16[64,512]{1,0:T(8,128)(2,1)S(1)} %bitcast.109), channel_id=1, source_target_pairs={{0,4},{1,5},{2,6},{3,7},{4,0},{5,1},{6,2},{7,3},{8,12},{9,13},{10,... | collective-permute-start | bytes 196616 | tf_op jit(solution)/shard_map/ppermute | solution.py:33
  24.5 5.0 %collective-permute-start.2 = (bf16[64,512]{1,0:T(8,128)(2,1)S(1)}, bf16[64,512]{1,0:T(8,128)(2,1)S(1)}, u32[]{:S(2)}, u32[]{:S(2)}) collective-permute-start(bf16[64,512]{1,0:T(8,128)(2,1)S(1)} %bitcast.108), channel_id=1, source_target_pairs={{0,3},{1,2},{2,1},{3,0},{4,7},{5,6},{6,5},{7,4},{8,11},{9,10},{10,... | collective-permute-start | bytes 196616 | tf_op jit(solution)/shard_map/ppermute | solution.py:33
  29.5 5.1 %collective-permute-start.4 = (bf16[32,512]{1,0:T(8,128)(2,1)S(1)}, bf16[32,512]{1,0:T(8,128)(2,1)S(1)}, u32[]{:S(2)}, u32[]{:S(2)}) collective-permute-start(bf16[32,512]{1,0:T(8,128)(2,1)S(1)} %fusion.13), channel_id=1, source_target_pairs={{0,9},{1,8},{2,11},{3,10},{4,13},{5,12},{6,15},{7,14},{8,1},{9,0},... | collective-permute-start | bytes 98312 | tf_op jit(solution)/shard_map/ppermute | solution.py:33
  36.1 1.4 %collective-permute-start.5 = (bf16[4,2,16,512]{3,2,1,0:T(8,128)(2,1)S(1)}, bf16[4,2,16,512]{3,2,1,0:T(8,128)(2,1)S(1)}, u32[]{:S(2)}, u32[]{:S(2)}) collective-permute-start(bf16[4,2,16,512]{3,2,1,0:T(8,128)(2,1)S(1)} %get-tuple-element.32), channel_id=1, source_target_pairs={{0,1},{1,0},{2,3},{3,2},{4,5},{5,4},{6,7},{7,6},{8,9},{9,8},{10,11... | collective-permute-start | bytes 393224 | tf_op jit(solution)/shard_map/ppermute | solution.py:33
  37.6 4.3 %collective-permute-start.8 = (bf16[32,512]{1,0:T(8,128)(2,1)S(1)}, bf16[32,512]{1,0:T(8,128)(2,1)S(1)}, u32[]{:S(2)}, u32[]{:S(2)}) collective-permute-start(bf16[32,512]{1,0:T(8,128)(2,1)S(1)} %bitcast.120), channel_id=1, source_target_pairs={{0,7},{1,6},{2,5},{3,4},{4,3},{5,2},{6,1},{7,0},{8,15},{9,14},{10,... | collective-permute-start | bytes 98312 | tf_op jit(solution)/shard_map/ppermute | solution.py:33
  37.7 4.8 %collective-permute-start.6 = (bf16[32,512]{1,0:T(8,128)(2,1)S(1)}, bf16[32,512]{1,0:T(8,128)(2,1)S(1)}, u32[]{:S(2)}, u32[]{:S(2)}) collective-permute-start(bf16[32,512]{1,0:T(8,128)(2,1)S(1)} %bitcast.119), channel_id=1, source_target_pairs={{0,4},{1,5},{2,6},{3,7},{4,0},{5,1},{6,2},{7,3},{8,12},{9,13},{10,... | collective-permute-start | bytes 98312 | tf_op jit(solution)/shard_map/ppermute | solution.py:33
  40.1 3.7 %collective-permute-start.7 = (bf16[32,512]{1,0:T(8,128)(2,1)S(1)}, bf16[32,512]{1,0:T(8,128)(2,1)S(1)}, u32[]{:S(2)}, u32[]{:S(2)}) collective-permute-start(bf16[32,512]{1,0:T(8,128)(2,1)S(1)} %bitcast.118), channel_id=1, source_target_pairs={{0,3},{1,2},{2,1},{3,0},{4,7},{5,6},{6,5},{7,4},{8,11},{9,10},{10,... | collective-permute-start | bytes 98312 | tf_op jit(solution)/shard_map/ppermute | solution.py:33
  43.9 5.0 %collective-permute-start.9 = (bf16[32,512]{1,0:T(8,128)(2,1)S(1)}, bf16[32,512]{1,0:T(8,128)(2,1)S(1)}, u32[]{:S(2)}, u32[]{:S(2)}) collective-permute-start(bf16[32,512]{1,0:T(8,128)(2,1)S(1)} %pad_maximum_fusion.9), channel_id=1, source_target_pairs={{0,9},{1,8},{2,11},{3,10},{4,13},{5,12},{6,15},{7,14},{8,1},{9,0},... | collective-permute-start | bytes 98312 | tf_op jit(solution)/shard_map/ppermute | solution.py:33
  50.3 25.8 %copy-start.2 = (bf16[8192,256]{1,0:T(8,128)(2,1)S(1)}, bf16[8192,256]{1,0:T(8,128)(2,1)}, u32[]{:S(2)}) copy-start(bf16[8192,256]{1,0:T(8,128)(2,1)} %emission_ref.7) | copy-start | bytes 12582916
  50.3 1.6 %collective-permute-start.10 = (f32[4,2,16,512]{3,2,1,0:T(8,128)S(1)}, f32[4,2,16,512]{3,2,1,0:T(8,128)S(1)}, u32[]{:S(2)}, u32[]{:S(2)}) collective-permute-start(f32[4,2,16,512]{3,2,1,0:T(8,128)S(1)} %get-tuple-element.34), channel_id=1, source_target_pairs={{0,1},{1,0},{2,3},{3,2},{4,5},{5,4},{6,7},{7,6},{8,9},{9,8},{10,11... | collective-permute-start | bytes 786440 | tf_op jit(solution)/shard_map/ppermute | solution.py:33
  50.4 27.0 %copy-start.4 = (bf16[16,256]{1,0:T(8,128)(2,1)S(1)}, bf16[16,256]{1,0:T(8,128)(2,1)}, u32[]{:S(2)}) copy-start(bf16[16,256]{1,0:T(8,128)(2,1)} %logits_ref.1) | copy-start | bytes 24580
  52.0 5.6 %collective-permute-start.11 = (bf16[96,512]{1,0:T(8,128)(2,1)S(1)}, bf16[96,512]{1,0:T(8,128)(2,1)S(1)}, u32[]{:S(2)}, u32[]{:S(2)}) collective-permute-start(bf16[96,512]{1,0:T(8,128)(2,1)S(1)} %get-tuple-element.61), channel_id=1, source_target_pairs={{0,4},{1,5},{2,6},{3,7},{4,0},{5,1},{6,2},{7,3},{8,12},{9,13},{10,... | collective-permute-start | bytes 294920 | tf_op jit(solution)/shard_map/ppermute | solution.py:33
  52.1 5.5 %collective-permute-start.12 = (bf16[96,512]{1,0:T(8,128)(2,1)S(1)}, bf16[96,512]{1,0:T(8,128)(2,1)S(1)}, u32[]{:S(2)}, u32[]{:S(2)}) collective-permute-start(bf16[96,512]{1,0:T(8,128)(2,1)S(1)} %get-tuple-element.62), channel_id=1, source_target_pairs={{0,3},{1,2},{2,1},{3,0},{4,7},{5,6},{6,5},{7,4},{8,11},{9,10},{10,... | collective-permute-start | bytes 294920 | tf_op jit(solution)/shard_map/ppermute | solution.py:33
  53.1 6.0 %collective-permute-start.13 = (bf16[96,512]{1,0:T(8,128)(2,1)S(1)}, bf16[96,512]{1,0:T(8,128)(2,1)S(1)}, u32[]{:S(2)}, u32[]{:S(2)}) collective-permute-start(bf16[96,512]{1,0:T(8,128)(2,1)S(1)} %get-tuple-element.63), channel_id=1, source_target_pairs={{0,7},{1,6},{2,5},{3,4},{4,3},{5,2},{6,1},{7,0},{8,15},{9,14},{10,... | collective-permute-start | bytes 294920 | tf_op jit(solution)/shard_map/ppermute | solution.py:33
  59.2 4.3 %collective-permute-start.14 = (bf16[32,512]{1,0:T(8,128)(2,1)S(1)}, bf16[32,512]{1,0:T(8,128)(2,1)S(1)}, u32[]{:S(2)}, u32[]{:S(2)}) collective-permute-start(bf16[32,512]{1,0:T(8,128)(2,1)S(1)} %pad_maximum_fusion.10), channel_id=1, source_target_pairs={{0,9},{1,8},{2,11},{3,10},{4,13},{5,12},{6,15},{7,14},{8,1},{9,0},... | collective-permute-start | bytes 98312 | tf_op jit(solution)/shard_map/ppermute | solution.py:33
  59.3 1.4 %collective-permute-start.15 = (bf16[4,2,16,512]{3,2,1,0:T(8,128)(2,1)S(1)}, bf16[4,2,16,512]{3,2,1,0:T(8,128)(2,1)S(1)}, u32[]{:S(2)}, u32[]{:S(2)}) collective-permute-start(bf16[4,2,16,512]{3,2,1,0:T(8,128)(2,1)S(1)} %pad_maximum_fusion.7.near_ref), channel_id=1, source_target_pairs={{0,1},{1,0},{2,3},{3,2},{4,5},{5,4},{6,7},{7,6},{8,9},{9,8},{10,11... | collective-permute-start | bytes 393224 | tf_op jit(solution)/shard_map/ppermute | solution.py:33
  63.5 4.3 %collective-permute-start.16 = (f32[16,512]{1,0:T(8,128)S(1)}, f32[16,512]{1,0:T(8,128)S(1)}, u32[]{:S(2)}, u32[]{:S(2)}) collective-permute-start(f32[16,512]{1,0:T(8,128)S(1)} %last_messages.1), channel_id=1, source_target_pairs={{0,9},{1,8},{2,11},{3,10},{4,13},{5,12},{6,15},{7,14},{8,1},{9,0},... | collective-permute-start | bytes 98312 | tf_op jit(solution)/shard_map/ppermute | solution.py:33
  67.8 3.9 %collective-permute-start.18 = (f32[2,16,512]{2,1,0:T(8,128)S(1)}, f32[2,16,512]{2,1,0:T(8,128)S(1)}, u32[]{:S(2)}, u32[]{:S(2)}) collective-permute-start(f32[2,16,512]{2,1,0:T(8,128)S(1)} %get-tuple-element.52), channel_id=1, source_target_pairs={{0,3},{1,2},{2,1},{3,0},{4,7},{5,6},{6,5},{7,4},{8,11},{9,10},{10,... | collective-permute-start | bytes 196616 | tf_op jit(solution)/shard_map/ppermute | solution.py:33
  68.9 4.6 %collective-permute-start.17 = (f32[2,16,512]{2,1,0:T(8,128)S(1)}, f32[2,16,512]{2,1,0:T(8,128)S(1)}, u32[]{:S(2)}, u32[]{:S(2)}) collective-permute-start(f32[2,16,512]{2,1,0:T(8,128)S(1)} %get-tuple-element.52), channel_id=1, source_target_pairs={{0,4},{1,5},{2,6},{3,7},{4,0},{5,1},{6,2},{7,3},{8,12},{9,13},{10,... | collective-permute-start | bytes 196616 | tf_op jit(solution)/shard_map/ppermute | solution.py:33
  70.8 5.0 %collective-permute-start.19 = (f32[2,16,512]{2,1,0:T(8,128)S(1)}, f32[2,16,512]{2,1,0:T(8,128)S(1)}, u32[]{:S(2)}, u32[]{:S(2)}) collective-permute-start(f32[2,16,512]{2,1,0:T(8,128)S(1)} %get-tuple-element.52), channel_id=1, source_target_pairs={{0,7},{1,6},{2,5},{3,4},{4,3},{5,2},{6,1},{7,0},{8,15},{9,14},{10,... | collective-permute-start | bytes 196616 | tf_op jit(solution)/shard_map/ppermute | solution.py:33
  75.9 1.6 %collective-permute-start.20 = (f32[4,2,16,512]{3,2,1,0:T(8,128)S(1)}, f32[4,2,16,512]{3,2,1,0:T(8,128)S(1)}, u32[]{:S(2)}, u32[]{:S(2)}) collective-permute-start(f32[4,2,16,512]{3,2,1,0:T(8,128)S(1)} %pad_maximum_fusion.parts_ref), channel_id=1, source_target_pairs={{0,1},{1,0},{2,3},{3,2},{4,5},{5,4},{6,7},{7,6},{8,9},{9,8},{10,11... | collective-permute-start | bytes 786440 | tf_op jit(solution)/shard_map/ppermute | solution.py:33
  79.3 10.0 %all-to-all-start.1 = ((f32[16,2,16]{2,1,0:T(2,128)}), f32[16,2,16]{2,1,0:T(2,128)S(1)}, u32[]{:S(2)}, u32[]{:S(2)}) async-start(f32[16,2,16]{2,1,0:T(2,128)} %broadcast_in_dim.7), calls=%async_computation.1 | async-start | bytes 32768 | tf_op jit(solution)/shard_map/all_to_all | solution.py:20
  (3 other events, 32.2 us)
where the time goes:
time: 90.4 us; the launch traced here: 90.2 us
  waiting for transfers between devices  39.1 us (43%)
  starting transfers between devices  17.7 us (20%)
  blocking collectives  13.8 us (15%)
  Pallas kernels  13.6 us (15%)
  local copies, waits for them, and re-layouts  3.86 us (4%)
  other arithmetic  1.27 us (1%)
  between operations  0.95 us (1%)
    ppermute x21, waiting for transfers between devices, swap(): return lax.ppermute(block, 'vocab', pairs)  33.3 us
    ppermute x21, starting transfers between devices, swap(): return lax.ppermute(block, 'vocab', pairs)  14.2 us
    all_to_all x1, blocking collectives, exchange(): lax.all_to_all(blocks, 'vocab', split_axis=0, concat_axis=0, tiled=True)  13.8 us
    all_to_all x1, waiting for transfers between devices, exchange(): lax.all_to_all(blocks, 'vocab', split_axis=0, concat_axis=0, tiled=True)  5.84 us
    pallas_call x3, Pallas kernels, step(): pl.pallas_call(functools.partial(send_kernel, count, len(parts)), out_sha...  4.34 us
    pallas_call x3, Pallas kernels, step(): pl.pallas_call(functools.partial(keep_kernel, count), out_shape=pltpu.VME...  3.88 us
    all_to_all x1, starting transfers between devices, exchange(): lax.all_to_all(blocks, 'vocab', split_axis=0, concat_axis=0, tiled=True)  3.49 us
    unnamed x11, local copies, waits for them, and re-layouts  2.97 us
  transfers between devices with their start and end apart: 22, of which 20 were waited for; matrix products, arithmetic and copies ran while one was open for 1% of the time, Pallas kernels for 6%

commit v1 on v0

--- a/solution.py
+++ b/solution.py
@@ -75,10 +75,11 @@
     return [partner_of((0, 0, 0) + bits, count) for bits in all_bits(count - 3)]
 
 
-def half_places(count, first):
+def half_places(count, first, squares=range(4)):
+    near = square_partners(count)
     return [
-        ((q, h), first ^ near ^ far)
-        for q, near in enumerate(square_partners(count))
+        ((q, h), first ^ near[q] ^ far)
+        for q in squares
         for h, far in enumerate(far_partners(count))
     ]
 
@@ -102,15 +103,15 @@
     return rows.reshape(shape)
 
 
-def reduce_blocks(kept, received, wide, devices, count, near_extra=(), far_extra=()):
-    total = kept + received.astype(jnp.float32)
-    near, extras = total[0], list(near_extra)
-    for q, offset in enumerate(square_partners(count)):
-        if q:
-            packed = swap(pack(total[q], wide, near_extra), offset, devices)
-            near += unpack(packed, total.shape[1:], wide)
-            for extra in near_extra:
-                extras.append(packed[-extra.shape[0] :])
+def reduce_blocks(leaving, staying, wide, devices, count, near_extra=(), far_extra=()):
+    extras, arrived = list(near_extra), []
+    for q, offset in enumerate(square_partners(count)[1:]):
+        packed = swap(pack(leaving[q], wide, near_extra), offset, devices)
+        arrived.append(unpack(packed, leaving.shape[1:], wide))
+        first = packed
+        for extra in near_extra:
+            extras.append(packed[-extra.shape[0] :])
+    near = functools.reduce(jnp.add, arrived, staying(first))
     blocks = [near[0]]
     for h, offset in enumerate(far_partners(count)):
         if h:
@@ -326,24 +327,22 @@
     )(*blocks, after)
 
 
-def half_products(halves, transition_ref, out_ref, count, first):
+def half_products(halves, transition_ref, out_ref, extra, count, first, squares):
     states = halves.shape[0] // 2
     rows = transition_ref.shape[0] >> count
-    for place, partner in half_places(count, first):
+    for (q, h), partner in half_places(count, first, squares):
         product = dot_rows(halves, transition_ref[partner_rows(partner, rows)])
         product = product[:states] + product[states:]
+        place = (q - squares[0], h)
         out_ref[place + (pl.ds(0, states),)] = product.astype(out_ref.dtype)
-
-
-def add_rows(out_ref, states, extra):
-    for ref in extra:
-        rows = pl.ds(states, ref.shape[2])
-        for place in ((y, k) for y in range(ref.shape[0]) for k in range(ref.shape[1])):
-            out_ref[place + (rows,)] = ref[place].astype(out_ref.dtype)
-
-
-def send_kernel(count, number, transition_ref, route_ref, sums_ref, *refs):
-    parts, extra, (halves_ref, out_ref) = refs[:number], refs[number:-2], refs[-2:]
+        for ref in extra:
+            rows_after = pl.ds(states, ref.shape[2])
+            out_ref[place + (rows_after,)] = ref[q, h].astype(out_ref.dtype)
+
+
+def send_kernel(count, number, further, squares, transition_ref, route_ref, sums_ref, *refs):
+    parts, extra = refs[:number], refs[number : number + further]
+    halves_ref, out_ref = refs[number + further :]
     states = halves_ref.shape[0] // 2
     messages = parts[0][:states].astype(jnp.float32)
     for part in parts[1:]:
@@ -358,25 +357,36 @@
         emitted += selected[b * states : (b + 1) * states] * sums_ref[b]
     halves = jnp.concatenate(split_wide(emitted), axis=0)
     halves_ref[...] = halves
-    half_products(halves, transition_ref, out_ref, count, 1)
-    add_rows(out_ref, states, extra)
-
-
-def keep_kernel(count, transition_ref, halves_ref, *refs):
-    extra, out_ref = refs[:-1], refs[-1]
-    half_products(halves_ref[...], transition_ref, out_ref, count, 0)
-    add_rows(out_ref, halves_ref.shape[0] // 2, extra)
-
-
-def step(transition, route, sums, parts, dtype, devices, count, kept_rows=(), sent_rows=()):
+    half_products(halves, transition_ref, out_ref, extra, count, 1, squares)
+
+
+def more_kernel(count, first, further, squares, transition_ref, halves_ref, *refs):
+    extra, out_ref = refs[:further], refs[-1]
+    half_products(halves_ref[...], transition_ref, out_ref, extra, count, first, squares)
+
+
+def more_products(transition, halves, extra, after, dtype, count, first, squares):
+    states, rows = halves.shape[0] // 2, halves.shape[1]
+    total = states + sum(block.shape[2] for block in extra)
+    shape = (len(squares), 1 << (count - 3), total, rows)
+    return pl.pallas_call(
+        functools.partial(more_kernel, count, first, len(extra), squares),
+        out_shape=pltpu.VMEM(shape, dtype),
+        in_specs=[VMEM] * (2 + len(extra)) + [ANY] * len(after),
+        out_specs=VMEM,
+        compiler_params=PARAMS,
+        name="step_sent_half" if first else "step_kept_half",
+    )(transition, halves, *extra, *after)
+
+
+def step(transition, route, sums, parts, dtype, devices, count, kept_rows, sent_rows):
     states, rows = route.shape[0] // devices, parts[0].shape[1]
     total = states + sum(block.shape[2] for block in kept_rows)
-    shape = (4, devices // 8, total, rows)
     halves, sent = pl.pallas_call(
-        functools.partial(send_kernel, count, len(parts)),
+        functools.partial(send_kernel, count, len(parts), len(sent_rows), range(4)),
         out_shape=[
             pltpu.VMEM((2 * states, rows), jnp.bfloat16),
-            pltpu.VMEM(shape, dtype),
+            pltpu.VMEM((4, devices // 8, total, rows), dtype),
         ],
         in_specs=[VMEM] * (3 + len(parts) + len(sent_rows)),
         out_specs=[VMEM] * 2,
@@ -384,15 +394,13 @@
         name="step_sent_half",
     )(transition, route, sums, *parts, *sent_rows)
     received = swap(sent, 1, devices)
-    kept = pl.pallas_call(
-        functools.partial(keep_kernel, count),
-        out_shape=pltpu.VMEM(shape, jnp.float32),
-        in_specs=[VMEM] * (2 + len(kept_rows)),
-        out_specs=VMEM,
-        compiler_params=PARAMS,
-        name="step_kept_half",
-    )(transition, halves, *kept_rows)
-    return kept, received
+    kept = more_products(transition, halves, kept_rows, (), jnp.float32, count, 0, range(1, 4))
+
+    def staying(after):
+        kept = more_products(transition, halves, kept_rows, (after,), jnp.float32, count, 0, range(1))
+        return kept[0] + received[0].astype(jnp.float32)
+
+    return kept + received[1:].astype(jnp.float32), staying
 
 
 def weigh_half(emission_ref, forward_ref, chooser, parts_ref, count, first):
@@ -500,7 +508,7 @@
         for window_step in range(STEPS):
             wide = window_step == STEPS - 1
             dtype = jnp.float32 if wide else jnp.bfloat16
-            kept, received = step(
+            leaving, staying = step(
                 transition, route, sums, parts, dtype, devices, count, kept_rows, sent_rows
             )
             kept_rows, sent_rows, near_extra, far_extra = (), (), (), ()
@@ -510,7 +518,7 @@
             if window_step == 2:
                 near_extra = (forward,)
             parts, extras = reduce_blocks(
-                kept, received, wide, devices, count, near_extra, far_extra
+                leaving, staying, wide, devices, count, near_extra, far_extra
             )
             if window_step == 1:
                 others = [part[-devices:] for part in parts[1:]]

time: 90.4 us -> 90.8 us (level)
    pallas_call x6 -> x9, Pallas kernels: 8.22 us -> 8.54 us  [the longest x3 4.33 us: step(): pl.pallas_call(functools.partial(send_kernel, count, len(parts), len(sent...]
where the time goes in v1:
time: 90.8 us; the launch traced here: 90.6 us
  waiting for transfers between devices  38.9 us (43%)
  starting transfers between devices  17.9 us (20%)
  Pallas kernels  13.9 us (15%)
  blocking collectives  13.8 us (15%)
  local copies, waits for them, and re-layouts  3.87 us (4%)
  other arithmetic  1.21 us (1%)
  between operations  0.91 us (1%)
    ppermute x21, waiting for transfers between devices, swap(): return lax.ppermute(block, 'vocab', pairs)  33.1 us
    ppermute x21, starting transfers between devices, swap(): return lax.ppermute(block, 'vocab', pairs)  14.4 us
    all_to_all x1, blocking collectives, exchange(): lax.all_to_all(blocks, 'vocab', split_axis=0, concat_axis=0, tiled=True)  13.8 us
    all_to_all x1, waiting for transfers between devices, exchange(): lax.all_to_all(blocks, 'vocab', split_axis=0, concat_axis=0, tiled=True)  5.84 us
    pallas_call x3, Pallas kernels, step(): pl.pallas_call(functools.partial(send_kernel, count, len(parts), len(sent...  4.33 us
    pallas_call x6, Pallas kernels, more_products(): pl.pallas_call(functools.partial(more_kernel, count, first, len(extra), s...  4.21 us
    all_to_all x1, starting transfers between devices, exchange(): lax.all_to_all(blocks, 'vocab', split_axis=0, concat_axis=0, tiled=True)  3.49 us
    unnamed x11, local copies, waits for them, and re-layouts  2.97 us
  transfers between devices with their start and end apart: 22, of which 20 were waited for; matrix products, arithmetic and copies ran while one was open for 1% of the time, Pallas kernels for 6%

profile of v1, /device:TPU:0, one launch (start us, length us, event | category | flops | bytes accessed | tf_op | source)
XLA Modules:
  0.0 90.6 jit_solution(9022686504223971841)
XLA Ops:
  0.7 2.3 %copy-done.1 = bf16[8192,256]{1,0:T(8,128)(2,1)S(1)} copy-done((bf16[8192,256]{1,0:T(8,128)(2,1)S(1)}, bf16[8192,256]{1,0:T(8,128)(2,1)}, u32[]{:S(2)}) %copy-start.1) | copy-done | bytes 4194328
  3.0 2.4 %first_products.1 = (f32[16,1,512]{2,1,0:T(1,128)S(1)}, bf16[4,2,16,512]{3,2,1,0:T(8,128)(2,1)S(1)}, bf16[4,2,16,512]{3,2,1,0:T(8,128)(2,1)S(1)}, s32[1,16]{1,0:...) custom-call(s32[16]{0:T(128)} %token_hbm.1, s32[1,16]{1,0:T(1,128)} %bitcast.111, ...), custom_call_target="tpu_custom_call" | custom-call | tf_op jit(solution)/shard_map/first_products/pallas_call | solution.py:231
  5.8 13.8 %all_to_all.10.sums_ref = f32[16,1,512]{2,1,0:T(1,128)S(1)} all-to-all(f32[16,1,512]{2,1,0:T(1,128)S(1)} %get-tuple-element.25), channel_id=1, replica_groups=mesh['parts'=2,'vocab'=16] {'vocab'}, dimensions={0} | all-to-all | bytes 65536 | tf_op jit(solution)/shard_map/all_to_all | solution.py:20
  19.6 1.4 %step_sent_half.3 = (bf16[32,512]{1,0:T(8,128)(2,1)S(1)}, bf16[4,2,32,512]{3,2,1,0:T(8,128)(2,1)S(1)}) custom-call(bf16[8192,512]{1,0:T(8,128)(2,1)S(1)} %copy-done, bf16[256,48]{1,0:T(8,128)(2,1)S(1)} %get-tuple-element.24.route_ref, f32[16,1,512]{2,1,0:T(1,128)S(1)} %all_to_all.10.sums_ref, f32[16,512]{1,0:T(8,128)S(1)} %get-tuple-element.26.refs_0_, ...), custom_call_target="tpu_custom_call" | custom-call | tf_op jit(solution)/shard_map/step_sent_half/pallas_call | solution.py:385
  22.9 1.4 %collective-permute-start.1 = (bf16[64,512]{1,0:T(8,128)(2,1)S(1)}, bf16[64,512]{1,0:T(8,128)(2,1)S(1)}, u32[]{:S(2)}, u32[]{:S(2)}) collective-permute-start(bf16[64,512]{1,0:T(8,128)(2,1)S(1)} %bitcast.97), channel_id=1, source_target_pairs={{0,7},{1,6},{2,5},{3,4},{4,3},{5,2},{6,1},{7,0},{8,15},{9,14},{10,... | collective-permute-start | bytes 196616 | tf_op jit(solution)/shard_map/ppermute | solution.py:33
  24.3 1.7 %collective-permute-start.2 = (bf16[64,512]{1,0:T(8,128)(2,1)S(1)}, bf16[64,512]{1,0:T(8,128)(2,1)S(1)}, u32[]{:S(2)}, u32[]{:S(2)}) collective-permute-start(bf16[64,512]{1,0:T(8,128)(2,1)S(1)} %bitcast.95), channel_id=1, source_target_pairs={{0,4},{1,5},{2,6},{3,7},{4,0},{5,1},{6,2},{7,3},{8,12},{9,13},{10,... | collective-permute-start | bytes 196616 | tf_op jit(solution)/shard_map/ppermute | solution.py:33
  26.0 1.8 %collective-permute-done.1.refs_1_ = bf16[64,512]{1,0:T(8,128)(2,1)S(1)} collective-permute-done((bf16[64,512]{1,0:T(8,128)(2,1)S(1)}, bf16[64,512]{1,0:T(8,128)(2,1)S(1)}, u32[]{:S(2)}, u32[]{:S(2)}) %collective-permute-start.1) | collective-permute-done | bytes 65568 | tf_op jit(solution)/shard_map/ppermute | solution.py:33
  28.2 1.6 %collective-permute-done.2 = bf16[64,512]{1,0:T(8,128)(2,1)S(1)} collective-permute-done((bf16[64,512]{1,0:T(8,128)(2,1)S(1)}, bf16[64,512]{1,0:T(8,128)(2,1)S(1)}, u32[]{:S(2)}, u32[]{:S(2)}) %collective-permute-start.2) | collective-permute-done | bytes 65568 | tf_op jit(solution)/shard_map/ppermute | solution.py:33
  30.0 4.7 %collective-permute-done.4.refs_1_ = bf16[32,512]{1,0:T(8,128)(2,1)S(1)} collective-permute-done((bf16[32,512]{1,0:T(8,128)(2,1)S(1)}, bf16[32,512]{1,0:T(8,128)(2,1)S(1)}, u32[]{:S(2)}, u32[]{:S(2)}) %collective-permute-start.4) | collective-permute-done | bytes 32800 | tf_op jit(solution)/shard_map/ppermute | solution.py:33
  34.7 1.4 %step_sent_half.4 = (bf16[32,512]{1,0:T(8,128)(2,1)S(1)}, bf16[4,2,16,512]{3,2,1,0:T(8,128)(2,1)S(1)}) custom-call(bf16[8192,512]{1,0:T(8,128)(2,1)S(1)} %copy-done, bf16[256,48]{1,0:T(8,128)(2,1)S(1)} %get-tuple-element.24.route_ref, f32[16,1,512]{2,1,0:T(1,128)S(1)} %all_to_all.10.sums_ref, f32[32,512]{1,0:T(8,128)S(1)} %slice_bitcast_fusion.refs_0_, ...), custom_call_target="tpu_custom_call" | custom-call | tf_op jit(solution)/shard_map/step_sent_half/pallas_call | solution.py:385
  38.8 2.0 %collective-permute-start.7 = (bf16[32,512]{1,0:T(8,128)(2,1)S(1)}, bf16[32,512]{1,0:T(8,128)(2,1)S(1)}, u32[]{:S(2)}, u32[]{:S(2)}) collective-permute-start(bf16[32,512]{1,0:T(8,128)(2,1)S(1)} %bitcast.104), channel_id=1, source_target_pairs={{0,4},{1,5},{2,6},{3,7},{4,0},{5,1},{6,2},{7,3},{8,12},{9,13},{10,... | collective-permute-start | bytes 98312 | tf_op jit(solution)/shard_map/ppermute | solution.py:33
  41.0 1.4 %collective-permute-done.6.refs_0_ = bf16[32,512]{1,0:T(8,128)(2,1)S(1)} collective-permute-done((bf16[32,512]{1,0:T(8,128)(2,1)S(1)}, bf16[32,512]{1,0:T(8,128)(2,1)S(1)}, u32[]{:S(2)}, u32[]{:S(2)}) %collective-permute-start.6) | collective-permute-done | bytes 32800 | tf_op jit(solution)/shard_map/ppermute | solution.py:33
  43.4 4.7 %collective-permute-done.9.refs_1_ = bf16[32,512]{1,0:T(8,128)(2,1)S(1)} collective-permute-done((bf16[32,512]{1,0:T(8,128)(2,1)S(1)}, bf16[32,512]{1,0:T(8,128)(2,1)S(1)}, u32[]{:S(2)}, u32[]{:S(2)}) %collective-permute-start.9) | collective-permute-done | bytes 32800 | tf_op jit(solution)/shard_map/ppermute | solution.py:33
  48.1 1.4 %step_sent_half.5 = (bf16[32,512]{1,0:T(8,128)(2,1)S(1)}, f32[4,2,16,512]{3,2,1,0:T(8,128)S(1)}) custom-call(bf16[8192,512]{1,0:T(8,128)(2,1)S(1)} %copy-done, bf16[256,48]{1,0:T(8,128)(2,1)S(1)} %get-tuple-element.24.route_ref, f32[16,1,512]{2,1,0:T(1,128)S(1)} %all_to_all.10.sums_ref, f32[16,512]{1,0:T(8,128)S(1)} %slice_bitcast_fusion.3.refs_0_, ...), custom_call_target="tpu_custom_call" | custom-call | tf_op jit(solution)/shard_map/step_sent_half/pallas_call | solution.py:385
  52.5 2.0 %collective-permute-start.11 = (bf16[96,512]{1,0:T(8,128)(2,1)S(1)}, bf16[96,512]{1,0:T(8,128)(2,1)S(1)}, u32[]{:S(2)}, u32[]{:S(2)}) collective-permute-start(bf16[96,512]{1,0:T(8,128)(2,1)S(1)} %get-tuple-element.59), channel_id=1, source_target_pairs={{0,7},{1,6},{2,5},{3,4},{4,3},{5,2},{6,1},{7,0},{8,15},{9,14},{10,... | collective-permute-start | bytes 294920 | tf_op jit(solution)/shard_map/ppermute | solution.py:33
  54.5 2.0 %collective-permute-done.12 = bf16[96,512]{1,0:T(8,128)(2,1)S(1)} collective-permute-done((bf16[96,512]{1,0:T(8,128)(2,1)S(1)}, bf16[96,512]{1,0:T(8,128)(2,1)S(1)}, u32[]{:S(2)}, u32[]{:S(2)}) %collective-permute-start.12) | collective-permute-done | bytes 98336 | tf_op jit(solution)/shard_map/ppermute | solution.py:33
  56.5 1.8 %collective-permute-done.11.refs_0_ = bf16[96,512]{1,0:T(8,128)(2,1)S(1)} collective-permute-done((bf16[96,512]{1,0:T(8,128)(2,1)S(1)}, bf16[96,512]{1,0:T(8,128)(2,1)S(1)}, u32[]{:S(2)}, u32[]{:S(2)}) %collective-permute-start.11) | collective-permute-done | bytes 98336 | tf_op jit(solution)/shard_map/ppermute | solution.py:33
  61.4 3.2 %collective-permute-done.14.refs_1_ = bf16[32,512]{1,0:T(8,128)(2,1)S(1)} collective-permute-done((bf16[32,512]{1,0:T(8,128)(2,1)S(1)}, bf16[32,512]{1,0:T(8,128)(2,1)S(1)}, u32[]{:S(2)}, u32[]{:S(2)}) %collective-permute-start.14) | collective-permute-done | bytes 32800 | tf_op jit(solution)/shard_map/ppermute | solution.py:33
  64.7 4.9 %collective-permute-done.16 = f32[16,512]{1,0:T(8,128)S(1)} collective-permute-done((f32[16,512]{1,0:T(8,128)S(1)}, f32[16,512]{1,0:T(8,128)S(1)}, u32[]{:S(2)}, u32[]{:S(2)}) %collective-permute-start.16) | collective-permute-done | bytes 32800 | tf_op jit(solution)/shard_map/ppermute | solution.py:33
  70.0 2.7 %collective-permute-start.19 = (f32[2,16,512]{2,1,0:T(8,128)S(1)}, f32[2,16,512]{2,1,0:T(8,128)S(1)}, u32[]{:S(2)}, u32[]{:S(2)}) collective-permute-start(f32[2,16,512]{2,1,0:T(8,128)S(1)} %get-tuple-element.48), channel_id=1, source_target_pairs={{0,7},{1,6},{2,5},{3,4},{4,3},{5,2},{6,1},{7,0},{8,15},{9,14},{10,... | collective-permute-start | bytes 196616 | tf_op jit(solution)/shard_map/ppermute | solution.py:33
  72.6 1.1 %collective-permute-done.18 = f32[2,16,512]{2,1,0:T(8,128)S(1)} collective-permute-done((f32[2,16,512]{2,1,0:T(8,128)S(1)}, f32[2,16,512]{2,1,0:T(8,128)S(1)}, u32[]{:S(2)}, u32[]{:S(2)}) %collective-permute-start.18) | collective-permute-done | bytes 65568 | tf_op jit(solution)/shard_map/ppermute | solution.py:33
  74.8 1.4 %collective-permute-done.19 = f32[2,16,512]{2,1,0:T(8,128)S(1)} collective-permute-done((f32[2,16,512]{2,1,0:T(8,128)S(1)}, f32[2,16,512]{2,1,0:T(8,128)S(1)}, u32[]{:S(2)}, u32[]{:S(2)}) %collective-permute-start.19) | collective-permute-done | bytes 65568 | tf_op jit(solution)/shard_map/ppermute | solution.py:33
  79.6 3.5 %all-to-all-start.1 = ((f32[16,2,16]{2,1,0:T(2,128)}), f32[16,2,16]{2,1,0:T(2,128)S(1)}, u32[]{:S(2)}, u32[]{:S(2)}) async-start(f32[16,2,16]{2,1,0:T(2,128)} %broadcast_in_dim.7), calls=%async_computation.1 | async-start | bytes 32768 | tf_op jit(solution)/shard_map/all_to_all | solution.py:20
  83.7 5.8 %all-to-all-done.1 = f32[16,2,16]{2,1,0:T(2,128)S(1)} async-done(((f32[16,2,16]{2,1,0:T(2,128)}), f32[16,2,16]{2,1,0:T(2,128)S(1)}, u32[]{:S(2)}, u32[]{:S(2)}) %all-to-all-start.1) | async-done | bytes 2080 | tf_op jit(solution)/shard_map/all_to_all | solution.py:20
  (88 shorter events, 19.1 us)
Async XLA Ops:
  21.1 1.6 %collective-permute-start = (bf16[4,2,32,512]{3,2,1,0:T(8,128)(2,1)S(1)}, bf16[4,2,32,512]{3,2,1,0:T(8,128)(2,1)S(1)}, u32[]{:S(2)}, u32[]{:S(2)}) collective-permute-start(bf16[4,2,32,512]{3,2,1,0:T(8,128)(2,1)S(1)} %get-tuple-element.30), channel_id=1, source_target_pairs={{0,1},{1,0},{2,3},{3,2},{4,5},{5,4},{6,7},{7,6},{8,9},{9,8},{10,11... | collective-permute-start | bytes 786440 | tf_op jit(solution)/shard_map/ppermute | solution.py:33
  22.7 5.5 %collective-permute-start.3 = (bf16[64,512]{1,0:T(8,128)(2,1)S(1)}, bf16[64,512]{1,0:T(8,128)(2,1)S(1)}, u32[]{:S(2)}, u32[]{:S(2)}) collective-permute-start(bf16[64,512]{1,0:T(8,128)(2,1)S(1)} %bitcast.96), channel_id=1, source_target_pairs={{0,3},{1,2},{2,1},{3,0},{4,7},{5,6},{6,5},{7,4},{8,11},{9,10},{10,... | collective-permute-start | bytes 196616 | tf_op jit(solution)/shard_map/ppermute | solution.py:33
  22.9 4.9 %collective-permute-start.1 = (bf16[64,512]{1,0:T(8,128)(2,1)S(1)}, bf16[64,512]{1,0:T(8,128)(2,1)S(1)}, u32[]{:S(2)}, u32[]{:S(2)}) collective-permute-start(bf16[64,512]{1,0:T(8,128)(2,1)S(1)} %bitcast.97), channel_id=1, source_target_pairs={{0,7},{1,6},{2,5},{3,4},{4,3},{5,2},{6,1},{7,0},{8,15},{9,14},{10,... | collective-permute-start | bytes 196616 | tf_op jit(solution)/shard_map/ppermute | solution.py:33
  24.3 5.5 %collective-permute-start.2 = (bf16[64,512]{1,0:T(8,128)(2,1)S(1)}, bf16[64,512]{1,0:T(8,128)(2,1)S(1)}, u32[]{:S(2)}, u32[]{:S(2)}) collective-permute-start(bf16[64,512]{1,0:T(8,128)(2,1)S(1)} %bitcast.95), channel_id=1, source_target_pairs={{0,4},{1,5},{2,6},{3,7},{4,0},{5,1},{6,2},{7,3},{8,12},{9,13},{10,... | collective-permute-start | bytes 196616 | tf_op jit(solution)/shard_map/ppermute | solution.py:33
  29.9 4.8 %collective-permute-start.4 = (bf16[32,512]{1,0:T(8,128)(2,1)S(1)}, bf16[32,512]{1,0:T(8,128)(2,1)S(1)}, u32[]{:S(2)}, u32[]{:S(2)}) collective-permute-start(bf16[32,512]{1,0:T(8,128)(2,1)S(1)} %fusion.8), channel_id=1, source_target_pairs={{0,9},{1,8},{2,11},{3,10},{4,13},{5,12},{6,15},{7,14},{8,1},{9,0},... | collective-permute-start | bytes 98312 | tf_op jit(solution)/shard_map/ppermute | solution.py:33
  36.1 1.4 %collective-permute-start.5 = (bf16[4,2,16,512]{3,2,1,0:T(8,128)(2,1)S(1)}, bf16[4,2,16,512]{3,2,1,0:T(8,128)(2,1)S(1)}, u32[]{:S(2)}, u32[]{:S(2)}) collective-permute-start(bf16[4,2,16,512]{3,2,1,0:T(8,128)(2,1)S(1)} %get-tuple-element.32), channel_id=1, source_target_pairs={{0,1},{1,0},{2,3},{3,2},{4,5},{5,4},{6,7},{7,6},{8,9},{9,8},{10,11... | collective-permute-start | bytes 393224 | tf_op jit(solution)/shard_map/ppermute | solution.py:33
  37.5 5.2 %collective-permute-start.8 = (bf16[32,512]{1,0:T(8,128)(2,1)S(1)}, bf16[32,512]{1,0:T(8,128)(2,1)S(1)}, u32[]{:S(2)}, u32[]{:S(2)}) collective-permute-start(bf16[32,512]{1,0:T(8,128)(2,1)S(1)} %bitcast.105), channel_id=1, source_target_pairs={{0,3},{1,2},{2,1},{3,0},{4,7},{5,6},{6,5},{7,4},{8,11},{9,10},{10,... | collective-permute-start | bytes 98312 | tf_op jit(solution)/shard_map/ppermute | solution.py:33
  38.1 4.2 %collective-permute-start.6 = (bf16[32,512]{1,0:T(8,128)(2,1)S(1)}, bf16[32,512]{1,0:T(8,128)(2,1)S(1)}, u32[]{:S(2)}, u32[]{:S(2)}) collective-permute-start(bf16[32,512]{1,0:T(8,128)(2,1)S(1)} %bitcast.106), channel_id=1, source_target_pairs={{0,7},{1,6},{2,5},{3,4},{4,3},{5,2},{6,1},{7,0},{8,15},{9,14},{10,... | collective-permute-start | bytes 98312 | tf_op jit(solution)/shard_map/ppermute | solution.py:33
  38.8 4.4 %collective-permute-start.7 = (bf16[32,512]{1,0:T(8,128)(2,1)S(1)}, bf16[32,512]{1,0:T(8,128)(2,1)S(1)}, u32[]{:S(2)}, u32[]{:S(2)}) collective-permute-start(bf16[32,512]{1,0:T(8,128)(2,1)S(1)} %bitcast.104), channel_id=1, source_target_pairs={{0,4},{1,5},{2,6},{3,7},{4,0},{5,1},{6,2},{7,3},{8,12},{9,13},{10,... | collective-permute-start | bytes 98312 | tf_op jit(solution)/shard_map/ppermute | solution.py:33
  43.3 4.8 %collective-permute-start.9 = (bf16[32,512]{1,0:T(8,128)(2,1)S(1)}, bf16[32,512]{1,0:T(8,128)(2,1)S(1)}, u32[]{:S(2)}, u32[]{:S(2)}) collective-permute-start(bf16[32,512]{1,0:T(8,128)(2,1)S(1)} %pad_maximum_fusion.9), channel_id=1, source_target_pairs={{0,9},{1,8},{2,11},{3,10},{4,13},{5,12},{6,15},{7,14},{8,1},{9,0},... | collective-permute-start | bytes 98312 | tf_op jit(solution)/shard_map/ppermute | solution.py:33
  49.5 1.6 %collective-permute-start.10 = (f32[4,2,16,512]{3,2,1,0:T(8,128)S(1)}, f32[4,2,16,512]{3,2,1,0:T(8,128)S(1)}, u32[]{:S(2)}, u32[]{:S(2)}) collective-permute-start(f32[4,2,16,512]{3,2,1,0:T(8,128)S(1)} %get-tuple-element.34), channel_id=1, source_target_pairs={{0,1},{1,0},{2,3},{3,2},{4,5},{5,4},{6,7},{7,6},{8,9},{9,8},{10,11... | collective-permute-start | bytes 786440 | tf_op jit(solution)/shard_map/ppermute | solution.py:33
  50.9 25.7 %copy-start.2 = (bf16[8192,256]{1,0:T(8,128)(2,1)S(1)}, bf16[8192,256]{1,0:T(8,128)(2,1)}, u32[]{:S(2)}) copy-start(bf16[8192,256]{1,0:T(8,128)(2,1)} %emission_ref.7) | copy-start | bytes 12582916
  51.2 26.6 %copy-start.4 = (bf16[16,256]{1,0:T(8,128)(2,1)S(1)}, bf16[16,256]{1,0:T(8,128)(2,1)}, u32[]{:S(2)}) copy-start(bf16[16,256]{1,0:T(8,128)(2,1)} %logits_ref.1) | copy-start | bytes 24580
  51.2 5.3 %collective-permute-start.12 = (bf16[96,512]{1,0:T(8,128)(2,1)S(1)}, bf16[96,512]{1,0:T(8,128)(2,1)S(1)}, u32[]{:S(2)}, u32[]{:S(2)}) collective-permute-start(bf16[96,512]{1,0:T(8,128)(2,1)S(1)} %get-tuple-element.57), channel_id=1, source_target_pairs={{0,4},{1,5},{2,6},{3,7},{4,0},{5,1},{6,2},{7,3},{8,12},{9,13},{10,... | collective-permute-start | bytes 294920 | tf_op jit(solution)/shard_map/ppermute | solution.py:33
  52.3 7.2 %collective-permute-start.13 = (bf16[96,512]{1,0:T(8,128)(2,1)S(1)}, bf16[96,512]{1,0:T(8,128)(2,1)S(1)}, u32[]{:S(2)}, u32[]{:S(2)}) collective-permute-start(bf16[96,512]{1,0:T(8,128)(2,1)S(1)} %get-tuple-element.58), channel_id=1, source_target_pairs={{0,3},{1,2},{2,1},{3,0},{4,7},{5,6},{6,5},{7,4},{8,11},{9,10},{10,... | collective-permute-start | bytes 294920 | tf_op jit(solution)/shard_map/ppermute | solution.py:33
  52.5 5.8 %collective-permute-start.11 = (bf16[96,512]{1,0:T(8,128)(2,1)S(1)}, bf16[96,512]{1,0:T(8,128)(2,1)S(1)}, u32[]{:S(2)}, u32[]{:S(2)}) collective-permute-start(bf16[96,512]{1,0:T(8,128)(2,1)S(1)} %get-tuple-element.59), channel_id=1, source_target_pairs={{0,7},{1,6},{2,5},{3,4},{4,3},{5,2},{6,1},{7,0},{8,15},{9,14},{10,... | collective-permute-start | bytes 294920 | tf_op jit(solution)/shard_map/ppermute | solution.py:33
  59.5 5.1 %collective-permute-start.14 = (bf16[32,512]{1,0:T(8,128)(2,1)S(1)}, bf16[32,512]{1,0:T(8,128)(2,1)S(1)}, u32[]{:S(2)}, u32[]{:S(2)}) collective-permute-start(bf16[32,512]{1,0:T(8,128)(2,1)S(1)} %pad_maximum_fusion.10), channel_id=1, source_target_pairs={{0,9},{1,8},{2,11},{3,10},{4,13},{5,12},{6,15},{7,14},{8,1},{9,0},... | collective-permute-start | bytes 98312 | tf_op jit(solution)/shard_map/ppermute | solution.py:33
  59.7 1.4 %collective-permute-start.15 = (bf16[4,2,16,512]{3,2,1,0:T(8,128)(2,1)S(1)}, bf16[4,2,16,512]{3,2,1,0:T(8,128)(2,1)S(1)}, u32[]{:S(2)}, u32[]{:S(2)}) collective-permute-start(bf16[4,2,16,512]{3,2,1,0:T(8,128)(2,1)S(1)} %pad_maximum_fusion.7.near_ref), channel_id=1, source_target_pairs={{0,1},{1,0},{2,3},{3,2},{4,5},{5,4},{6,7},{7,6},{8,9},{9,8},{10,11... | collective-permute-start | bytes 393224 | tf_op jit(solution)/shard_map/ppermute | solution.py:33
  64.6 5.0 %collective-permute-start.16 = (f32[16,512]{1,0:T(8,128)S(1)}, f32[16,512]{1,0:T(8,128)S(1)}, u32[]{:S(2)}, u32[]{:S(2)}) collective-permute-start(f32[16,512]{1,0:T(8,128)S(1)} %last_messages.1), channel_id=1, source_target_pairs={{0,9},{1,8},{2,11},{3,10},{4,13},{5,12},{6,15},{7,14},{8,1},{9,0},... | collective-permute-start | bytes 98312 | tf_op jit(solution)/shard_map/ppermute | solution.py:33
  69.6 4.2 %collective-permute-start.18 = (f32[2,16,512]{2,1,0:T(8,128)S(1)}, f32[2,16,512]{2,1,0:T(8,128)S(1)}, u32[]{:S(2)}, u32[]{:S(2)}) collective-permute-start(f32[2,16,512]{2,1,0:T(8,128)S(1)} %get-tuple-element.48), channel_id=1, source_target_pairs={{0,3},{1,2},{2,1},{3,0},{4,7},{5,6},{6,5},{7,4},{8,11},{9,10},{10,... | collective-permute-start | bytes 196616 | tf_op jit(solution)/shard_map/ppermute | solution.py:33
  69.9 4.9 %collective-permute-start.17 = (f32[2,16,512]{2,1,0:T(8,128)S(1)}, f32[2,16,512]{2,1,0:T(8,128)S(1)}, u32[]{:S(2)}, u32[]{:S(2)}) collective-permute-start(f32[2,16,512]{2,1,0:T(8,128)S(1)} %get-tuple-element.48), channel_id=1, source_target_pairs={{0,4},{1,5},{2,6},{3,7},{4,0},{5,1},{6,2},{7,3},{8,12},{9,13},{10,... | collective-permute-start | bytes 196616 | tf_op jit(solution)/shard_map/ppermute | solution.py:33
  70.0 6.3 %collective-permute-start.19 = (f32[2,16,512]{2,1,0:T(8,128)S(1)}, f32[2,16,512]{2,1,0:T(8,128)S(1)}, u32[]{:S(2)}, u32[]{:S(2)}) collective-permute-start(f32[2,16,512]{2,1,0:T(8,128)S(1)} %get-tuple-element.48), channel_id=1, source_target_pairs={{0,7},{1,6},{2,5},{3,4},{4,3},{5,2},{6,1},{7,0},{8,15},{9,14},{10,... | collective-permute-start | bytes 196616 | tf_op jit(solution)/shard_map/ppermute | solution.py:33
  76.2 1.6 %collective-permute-start.20 = (f32[4,2,16,512]{3,2,1,0:T(8,128)S(1)}, f32[4,2,16,512]{3,2,1,0:T(8,128)S(1)}, u32[]{:S(2)}, u32[]{:S(2)}) collective-permute-start(f32[4,2,16,512]{3,2,1,0:T(8,128)S(1)} %pad_maximum_fusion.parts_ref), channel_id=1, source_target_pairs={{0,1},{1,0},{2,3},{3,2},{4,5},{5,4},{6,7},{7,6},{8,9},{9,8},{10,11... | collective-permute-start | bytes 786440 | tf_op jit(solution)/shard_map/ppermute | solution.py:33
  79.6 10.0 %all-to-all-start.1 = ((f32[16,2,16]{2,1,0:T(2,128)}), f32[16,2,16]{2,1,0:T(2,128)S(1)}, u32[]{:S(2)}, u32[]{:S(2)}) async-start(f32[16,2,16]{2,1,0:T(2,128)} %broadcast_in_dim.7), calls=%async_computation.1 | async-start | bytes 32768 | tf_op jit(solution)/shard_map/all_to_all | solution.py:20
  (3 other events, 32.2 us)

commit v2 on v0

--- a/solution.py
+++ b/solution.py
@@ -181,9 +181,9 @@
 
 
 def products_kernel(
-    count, token_hbm, state_hbm, allow_hbm, table_hbm, start_hbm, emission_ref,
-    sums_ref, kept_ref, sent_ref, state_ref, allow_ref, table_ref, messages_ref,
-    token_ref, columns_ref, sems,
+    count, token_hbm, state_hbm, allow_hbm, table_hbm, start_hbm, emission_hbm,
+    sums_ref, kept_ref, sent_ref, state_ref, allow_ref, table_ref, messages_ref, emission_ref,
+    token_ref, columns_ref, sems, chunk_sems,
 ):
     device = lax.axis_index("vocab")
     devices = 1 << count
@@ -196,7 +196,13 @@
     copies = [
         pltpu.make_async_copy(source, to, sems.at[k]) for k, (source, to) in enumerate(pairs)
     ]
-    for copy in copies:
+    chunks = []
+    for k in range(devices):
+        span = pl.ds(k * rows, rows)
+        chunks.append(
+            pltpu.make_async_copy(emission_hbm.at[span], emission_ref.at[span], chunk_sems.at[k])
+        )
+    for copy in copies + chunks:
         copy.start()
     shape = (devices * devices // 2, devices * devices)
     to, source = (lax.broadcasted_iota(jnp.int32, shape, axis) for axis in (0, 1))
@@ -212,6 +218,7 @@
     onehot = (tokens == lax.broadcasted_iota(jnp.int32, shape, 1)).astype(jnp.bfloat16)
     left = jnp.concatenate([onehot, jnp.ones((16, BLK), jnp.bfloat16)], axis=0)
     for k in range(devices):
+        chunks[k].wait()
         product = dot_rows(left, emission_ref[pl.ds(k * rows, rows)])
         columns_ref[pl.ds(k * devices, devices)] = product[:devices].astype(jnp.bfloat16)
         sums_ref[k] = product[devices : devices + 1]
@@ -231,17 +238,19 @@
         functools.partial(products_kernel, count),
         out_shape=[jax.ShapeDtypeStruct((devices, 1, rows), jnp.float32), half, half]
         + [pltpu.VMEM(array.shape, array.dtype) for array in small]
-        + [pltpu.VMEM((beta_start.shape[1], rows), jnp.float32)],
-        in_specs=[ANY] * len(operands) + [VMEM],
-        out_specs=[VMEM] * 7,
+        + [pltpu.VMEM((beta_start.shape[1], rows), jnp.float32)]
+        + [pltpu.VMEM(emission.shape, emission.dtype)],
+        in_specs=[ANY] * (len(operands) + 1),
+        out_specs=[VMEM] * 8,
         scratch_shapes=[
             pltpu.SMEM(last_token.shape, jnp.int32),
             pltpu.VMEM((devices * devices, rows), jnp.bfloat16),
             pltpu.SemaphoreType.DMA((len(operands),)),
+            pltpu.SemaphoreType.DMA((devices,)),
         ],
         compiler_params=PARAMS,
         name="first_products",
-    )(*(in_hbm(operand) for operand in operands), emission)
+    )(*(in_hbm(operand) for operand in operands + (emission,)))
 
 
 def in_hbm(array):
@@ -423,8 +432,10 @@
     raised = jnp.where(allowed, jnp.exp(logits - top) * weights, 0.0)
     raised_ref[...] = raised
     total = jnp.sum(raised, axis=1, keepdims=True)
-    lane = lax.broadcasted_iota(jnp.int32, pair_ref.shape, 1)
-    pair_ref[...] = jnp.where(lane == 0, top, total)
+    lane = lax.broadcasted_iota(jnp.int32, (raised.shape[0], 128), 1)
+    rows = jnp.where(lane == 0, top, total).T[:2]
+    for k in range(pair_ref.shape[0]):
+        pair_ref[k] = rows
 
 
 def weigh(emission, forward, chooser, logits, near, far, count):
@@ -440,7 +451,7 @@
         functools.partial(far_kernel, count),
         out_shape=[
             pltpu.VMEM(logits.shape, jnp.float32),
-            pltpu.VMEM((logits.shape[0], 128), jnp.float32),
+            pltpu.VMEM((1 << count, 2, logits.shape[0]), jnp.float32),
         ],
         in_specs=[VMEM] * 6,
         out_specs=[VMEM] * 2,
@@ -450,12 +461,12 @@
 
 
 def normalise(raised, pair, devices):
-    pairs = spread(pair[:, :2].T, devices)
-    own_top = pair[:, :1]
+    pairs = exchange(pair)
+    own_top = pair[0, 0]
     tops, totals = pairs[:, 0], pairs[:, 1]
     top = jnp.max(tops, axis=0)
     total = jnp.sum(totals * jnp.exp(tops - top), axis=0)
-    return BLK * devices * (raised * jnp.exp(own_top - top[:, None])) / total[:, None]
+    return BLK * devices * (raised * jnp.exp(own_top - top)[:, None]) / total[:, None]
 
 
 def forward_messages(emission, last_token, prior_msg, devices, device):
@@ -491,10 +502,10 @@
     prompts = prompt_state.shape[0]
     count = devices.bit_length() - 1
     if devices == 1 << count and count > 2 and own_rows % 128 == 0 and prompts == devices:
-        sums, columns, columns_out, state, allow, table, messages = first_products(
+        sums, columns, columns_out, state, allow, table, messages, held = first_products(
             last_token, prompt_state, allow_list, trans_table, beta_start, emission, count
         )
-        route, chooser, sums = tables(state, allow, table, emission, sums, count)
+        route, chooser, sums = tables(state, allow, table, held, sums, count)
         sums = exchange(sums)
         parts, kept_rows, sent_rows = [messages], (columns,), (columns_out,)
         for window_step in range(STEPS):

time: 90.4 us -> 90.8 us (level)
  local copies, waits for them, and re-layouts: 3.86 us -> 0.73 us
  Pallas kernels: 13.6 us -> 16.4 us
    unnamed x11 -> x9, local copies, waits for them, and re-layouts: 2.97 us -> 0.64 us
    pallas_call x1, Pallas kernels: 2.38 us -> 4.57 us  [first_products(): pl.pallas_call(functools.partial(products_kernel, count), out_shape=[jax....]
where the time goes in v2:
time: 90.8 us; the launch traced here: 90.6 us
  waiting for transfers between devices  39.1 us (43%)
  starting transfers between devices  17.7 us (19%)
  Pallas kernels  16.4 us (18%)
  blocking collectives  13.8 us (15%)
  other arithmetic  1.85 us (2%)
  between operations  0.94 us (1%)
    ppermute x21, waiting for transfers between devices, swap(): return lax.ppermute(block, 'vocab', pairs)  33.3 us
    ppermute x21, starting transfers between devices, swap(): return lax.ppermute(block, 'vocab', pairs)  14.2 us
    all_to_all x1, blocking collectives, exchange(): lax.all_to_all(blocks, 'vocab', split_axis=0, concat_axis=0, tiled=True)  13.8 us
    all_to_all x1, waiting for transfers between devices, exchange(): lax.all_to_all(blocks, 'vocab', split_axis=0, concat_axis=0, tiled=True)  5.84 us
    pallas_call x1, Pallas kernels, first_products(): pl.pallas_call(functools.partial(products_kernel, count), out_shape=[jax....  4.57 us
    pallas_call x3, Pallas kernels, step(): pl.pallas_call(functools.partial(send_kernel, count, len(parts)), out_sha...  4.34 us
    pallas_call x3, Pallas kernels, step(): pl.pallas_call(functools.partial(keep_kernel, count), out_shape=pltpu.VME...  3.88 us
    all_to_all x1, starting transfers between devices, exchange(): lax.all_to_all(blocks, 'vocab', split_axis=0, concat_axis=0, tiled=True)  3.49 us
  transfers between devices with their start and end apart: 22, of which 20 were waited for; matrix products, arithmetic and copies ran while one was open for 1% of the time, Pallas kernels for 6%

profile of v2, /device:TPU:0, one launch (start us, length us, event | category | flops | bytes accessed | tf_op | source)
XLA Modules:
  0.0 90.6 jit_solution(471585134701085746)
XLA Ops:
  0.6 4.6 %first_products.1 = (f32[16,1,512]{2,1,0:T(1,128)S(1)}, bf16[4,2,16,512]{3,2,1,0:T(8,128)(2,1)S(1)}, bf16[4,2,16,512]{3,2,1,0:T(8,128)(2,1)S(1)}, s32[1,16]{1,0:...) custom-call(s32[16]{0:T(128)} %token_hbm.1, ...), custom_call_target="tpu_custom_call" | custom-call | tf_op jit(solution)/shard_map/first_products/pallas_call | solution.py:237
  5.7 13.8 %all_to_all.10.sums_ref = f32[16,1,512]{2,1,0:T(1,128)S(1)} all-to-all(f32[16,1,512]{2,1,0:T(1,128)S(1)} %get-tuple-element.27), channel_id=1, replica_groups=mesh['parts'=2,'vocab'=16] {'vocab'}, dimensions={0} | all-to-all | bytes 65536 | tf_op jit(solution)/shard_map/all_to_all | solution.py:20
  19.5 1.5 %step_sent_half.3 = (bf16[32,512]{1,0:T(8,128)(2,1)S(1)}, bf16[4,2,32,512]{3,2,1,0:T(8,128)(2,1)S(1)}) custom-call(bf16[8192,512]{1,0:T(8,128)(2,1)S(1)} %copy-done, bf16[256,48]{1,0:T(8,128)(2,1)S(1)} %get-tuple-element.26.route_ref, f32[16,1,512]{2,1,0:T(1,128)S(1)} %all_to_all.10.sums_ref, f32[16,512]{1,0:T(8,128)S(1)} %get-tuple-element.28.refs_0_, ...), custom_call_target="tpu_custom_call" | custom-call | tf_op jit(solution)/shard_map/step_sent_half/pallas_call | solution.py:384
  20.9 1.3 %step_kept_half.3 = f32[4,2,32,512]{3,2,1,0:T(8,128)S(1)} custom-call(bf16[8192,512]{1,0:T(8,128)(2,1)S(1)} %copy-done, bf16[32,512]{1,0:T(8,128)(2,1)S(1)} %get-tuple-element.30.halves_ref, bf16[4,2,16,512]{3,2,1,0:T(8,128)(2,1)S(1)} %get-tuple-element.31.refs_0_), custom_call_target="tpu_custom_call" | custom-call | tf_op jit(solution)/shard_map/step_kept_half/pallas_call | solution.py:396
  22.9 1.4 %collective-permute-start.1 = (bf16[64,512]{1,0:T(8,128)(2,1)S(1)}, bf16[64,512]{1,0:T(8,128)(2,1)S(1)}, u32[]{:S(2)}, u32[]{:S(2)}) collective-permute-start(bf16[64,512]{1,0:T(8,128)(2,1)S(1)} %bitcast.110), channel_id=1, source_target_pairs={{0,4},{1,5},{2,6},{3,7},{4,0},{5,1},{6,2},{7,3},{8,12},{9,13},{10,... | collective-permute-start | bytes 196616 | tf_op jit(solution)/shard_map/ppermute | solution.py:33
  25.6 2.0 %collective-permute-done.3 = bf16[64,512]{1,0:T(8,128)(2,1)S(1)} collective-permute-done((bf16[64,512]{1,0:T(8,128)(2,1)S(1)}, bf16[64,512]{1,0:T(8,128)(2,1)S(1)}, u32[]{:S(2)}, u32[]{:S(2)}) %collective-permute-start.3) | collective-permute-done | bytes 65568 | tf_op jit(solution)/shard_map/ppermute | solution.py:33
  29.6 5.0 %collective-permute-done.4.refs_1_ = bf16[32,512]{1,0:T(8,128)(2,1)S(1)} collective-permute-done((bf16[32,512]{1,0:T(8,128)(2,1)S(1)}, bf16[32,512]{1,0:T(8,128)(2,1)S(1)}, u32[]{:S(2)}, u32[]{:S(2)}) %collective-permute-start.4) | collective-permute-done | bytes 32800 | tf_op jit(solution)/shard_map/ppermute | solution.py:33
  34.5 1.4 %step_sent_half.4 = (bf16[32,512]{1,0:T(8,128)(2,1)S(1)}, bf16[4,2,16,512]{3,2,1,0:T(8,128)(2,1)S(1)}) custom-call(bf16[8192,512]{1,0:T(8,128)(2,1)S(1)} %copy-done, bf16[256,48]{1,0:T(8,128)(2,1)S(1)} %get-tuple-element.26.route_ref, f32[16,1,512]{2,1,0:T(1,128)S(1)} %all_to_all.10.sums_ref, f32[32,512]{1,0:T(8,128)S(1)} %slice_bitcast_fusion.3.refs_0_, ...), custom_call_target="tpu_custom_call" | custom-call | tf_op jit(solution)/shard_map/step_sent_half/pallas_call | solution.py:384
  37.6 2.4 %collective-permute-start.6 = (bf16[32,512]{1,0:T(8,128)(2,1)S(1)}, bf16[32,512]{1,0:T(8,128)(2,1)S(1)}, u32[]{:S(2)}, u32[]{:S(2)}) collective-permute-start(bf16[32,512]{1,0:T(8,128)(2,1)S(1)} %bitcast.120), channel_id=1, source_target_pairs={{0,4},{1,5},{2,6},{3,7},{4,0},{5,1},{6,2},{7,3},{8,12},{9,13},{10,... | collective-permute-start | bytes 98312 | tf_op jit(solution)/shard_map/ppermute | solution.py:33
  42.3 1.3 %collective-permute-done.7 = bf16[32,512]{1,0:T(8,128)(2,1)S(1)} collective-permute-done((bf16[32,512]{1,0:T(8,128)(2,1)S(1)}, bf16[32,512]{1,0:T(8,128)(2,1)S(1)}, u32[]{:S(2)}, u32[]{:S(2)}) %collective-permute-start.7) | collective-permute-done | bytes 32800 | tf_op jit(solution)/shard_map/ppermute | solution.py:33
  43.8 4.9 %collective-permute-done.9.refs_1_ = bf16[32,512]{1,0:T(8,128)(2,1)S(1)} collective-permute-done((bf16[32,512]{1,0:T(8,128)(2,1)S(1)}, bf16[32,512]{1,0:T(8,128)(2,1)S(1)}, u32[]{:S(2)}, u32[]{:S(2)}) %collective-permute-start.9) | collective-permute-done | bytes 32800 | tf_op jit(solution)/shard_map/ppermute | solution.py:33
  48.7 1.4 %step_sent_half.5 = (bf16[32,512]{1,0:T(8,128)(2,1)S(1)}, f32[4,2,16,512]{3,2,1,0:T(8,128)S(1)}) custom-call(bf16[8192,512]{1,0:T(8,128)(2,1)S(1)} %copy-done, bf16[256,48]{1,0:T(8,128)(2,1)S(1)} %get-tuple-element.26.route_ref, f32[16,1,512]{2,1,0:T(1,128)S(1)} %all_to_all.10.sums_ref, f32[16,512]{1,0:T(8,128)S(1)} %slice_bitcast_fusion.6.refs_0_, ...), custom_call_target="tpu_custom_call" | custom-call | tf_op jit(solution)/shard_map/step_sent_half/pallas_call | solution.py:384
  50.3 1.3 %step_kept_half.5 = f32[4,2,16,512]{3,2,1,0:T(8,128)S(1)} custom-call(bf16[8192,512]{1,0:T(8,128)(2,1)S(1)} %copy-done, bf16[32,512]{1,0:T(8,128)(2,1)S(1)} %get-tuple-element.35.halves_ref), custom_call_target="tpu_custom_call" | custom-call | tf_op jit(solution)/shard_map/step_kept_half/pallas_call | solution.py:396
  53.0 2.2 %collective-permute-start.13 = (bf16[96,512]{1,0:T(8,128)(2,1)S(1)}, bf16[96,512]{1,0:T(8,128)(2,1)S(1)}, u32[]{:S(2)}, u32[]{:S(2)}) collective-permute-start(bf16[96,512]{1,0:T(8,128)(2,1)S(1)} %get-tuple-element.65), channel_id=1, source_target_pairs={{0,7},{1,6},{2,5},{3,4},{4,3},{5,2},{6,1},{7,0},{8,15},{9,14},{10,... | collective-permute-start | bytes 294920 | tf_op jit(solution)/shard_map/ppermute | solution.py:33
  55.2 2.3 %collective-permute-done.11 = bf16[96,512]{1,0:T(8,128)(2,1)S(1)} collective-permute-done((bf16[96,512]{1,0:T(8,128)(2,1)S(1)}, bf16[96,512]{1,0:T(8,128)(2,1)S(1)}, u32[]{:S(2)}, u32[]{:S(2)}) %collective-permute-start.11) | collective-permute-done | bytes 98336 | tf_op jit(solution)/shard_map/ppermute | solution.py:33
  57.6 1.4 %collective-permute-done.13 = bf16[96,512]{1,0:T(8,128)(2,1)S(1)} collective-permute-done((bf16[96,512]{1,0:T(8,128)(2,1)S(1)}, bf16[96,512]{1,0:T(8,128)(2,1)S(1)}, u32[]{:S(2)}, u32[]{:S(2)}) %collective-permute-start.13) | collective-permute-done | bytes 98336 | tf_op jit(solution)/shard_map/ppermute | solution.py:33
  61.0 2.4 %collective-permute-done.14.refs_1_ = bf16[32,512]{1,0:T(8,128)(2,1)S(1)} collective-permute-done((bf16[32,512]{1,0:T(8,128)(2,1)S(1)}, bf16[32,512]{1,0:T(8,128)(2,1)S(1)}, u32[]{:S(2)}, u32[]{:S(2)}) %collective-permute-start.14) | collective-permute-done | bytes 32800 | tf_op jit(solution)/shard_map/ppermute | solution.py:33
  63.7 4.0 %collective-permute-done.16 = f32[16,512]{1,0:T(8,128)S(1)} collective-permute-done((f32[16,512]{1,0:T(8,128)S(1)}, f32[16,512]{1,0:T(8,128)S(1)}, u32[]{:S(2)}, u32[]{:S(2)}) %collective-permute-start.16) | collective-permute-done | bytes 32800 | tf_op jit(solution)/shard_map/ppermute | solution.py:33
  68.8 2.0 %collective-permute-start.17 = (f32[2,16,512]{2,1,0:T(8,128)S(1)}, f32[2,16,512]{2,1,0:T(8,128)S(1)}, u32[]{:S(2)}, u32[]{:S(2)}) collective-permute-start(f32[2,16,512]{2,1,0:T(8,128)S(1)} %get-tuple-element.54), channel_id=1, source_target_pairs={{0,4},{1,5},{2,6},{3,7},{4,0},{5,1},{6,2},{7,3},{8,12},{9,13},{10,... | collective-permute-start | bytes 196616 | tf_op jit(solution)/shard_map/ppermute | solution.py:33
  71.6 1.8 %collective-permute-done.17 = f32[2,16,512]{2,1,0:T(8,128)S(1)} collective-permute-done((f32[2,16,512]{2,1,0:T(8,128)S(1)}, f32[2,16,512]{2,1,0:T(8,128)S(1)}, u32[]{:S(2)}, u32[]{:S(2)}) %collective-permute-start.17) | collective-permute-done | bytes 65568 | tf_op jit(solution)/shard_map/ppermute | solution.py:33
  73.3 2.4 %collective-permute-done.19 = f32[2,16,512]{2,1,0:T(8,128)S(1)} collective-permute-done((f32[2,16,512]{2,1,0:T(8,128)S(1)}, f32[2,16,512]{2,1,0:T(8,128)S(1)}, u32[]{:S(2)}, u32[]{:S(2)}) %collective-permute-start.19) | collective-permute-done | bytes 65568 | tf_op jit(solution)/shard_map/ppermute | solution.py:33
  77.4 1.8 %weigh_far.1 = (f32[16,256]{1,0:T(8,128)S(1)}, f32[16,2,16]{2,1,0:T(2,128)}) custom-call(bf16[8192,256]{1,0:T(8,128)(2,1)S(1)} %copy-done.1, bf16[256,512]{1,0:T(8,128)(2,1)S(1)} %order_forward.1.refs_2_.forward_ref, bf16[16,48]{1,0:T(8,128)(2,1)S(1)} %get-tuple-element.37.chooser_ref, bf16[16,256]{1,0:T(8,128)(2,1)S(1)} %copy-done.3, ...), custom_call_target="tpu_custom_call" | custom-call | tf_op jit(solution)/shard_map/weigh_far/pallas_call | solution.py:450
  79.1 3.5 %all-to-all-start.1 = ((f32[16,2,16]{2,1,0:T(2,128)}), f32[16,2,16]{2,1,0:T(2,128)S(1)}, u32[]{:S(2)}, u32[]{:S(2)}) async-start(f32[16,2,16]{2,1,0:T(2,128)} %get-tuple-element.39), calls=%async_computation.1 | async-start | bytes 32768 | tf_op jit(solution)/shard_map/all_to_all | solution.py:20
  83.3 5.8 %all-to-all-done.1 = f32[16,2,16]{2,1,0:T(2,128)S(1)} async-done(((f32[16,2,16]{2,1,0:T(2,128)}), f32[16,2,16]{2,1,0:T(2,128)S(1)}, u32[]{:S(2)}, u32[]{:S(2)}) %all-to-all-start.1) | async-done | bytes 2080 | tf_op jit(solution)/shard_map/all_to_all | solution.py:20
  (79 shorter events, 17.7 us)
Async XLA Ops:
  20.9 1.6 %collective-permute-start = (bf16[4,2,32,512]{3,2,1,0:T(8,128)(2,1)S(1)}, bf16[4,2,32,512]{3,2,1,0:T(8,128)(2,1)S(1)}, u32[]{:S(2)}, u32[]{:S(2)}) collective-permute-start(bf16[4,2,32,512]{3,2,1,0:T(8,128)(2,1)S(1)} %get-tuple-element.32), channel_id=1, source_target_pairs={{0,1},{1,0},{2,3},{3,2},{4,5},{5,4},{6,7},{7,6},{8,9},{9,8},{10,11... | collective-permute-start | bytes 786440 | tf_op jit(solution)/shard_map/ppermute | solution.py:33
  22.6 5.0 %collective-permute-start.3 = (bf16[64,512]{1,0:T(8,128)(2,1)S(1)}, bf16[64,512]{1,0:T(8,128)(2,1)S(1)}, u32[]{:S(2)}, u32[]{:S(2)}) collective-permute-start(bf16[64,512]{1,0:T(8,128)(2,1)S(1)} %bitcast.111), channel_id=1, source_target_pairs={{0,7},{1,6},{2,5},{3,4},{4,3},{5,2},{6,1},{7,0},{8,15},{9,14},{10,... | collective-permute-start | bytes 196616 | tf_op jit(solution)/shard_map/ppermute | solution.py:33
  22.9 5.3 %collective-permute-start.1 = (bf16[64,512]{1,0:T(8,128)(2,1)S(1)}, bf16[64,512]{1,0:T(8,128)(2,1)S(1)}, u32[]{:S(2)}, u32[]{:S(2)}) collective-permute-start(bf16[64,512]{1,0:T(8,128)(2,1)S(1)} %bitcast.110), channel_id=1, source_target_pairs={{0,4},{1,5},{2,6},{3,7},{4,0},{5,1},{6,2},{7,3},{8,12},{9,13},{10,... | collective-permute-start | bytes 196616 | tf_op jit(solution)/shard_map/ppermute | solution.py:33
  24.4 5.0 %collective-permute-start.2 = (bf16[64,512]{1,0:T(8,128)(2,1)S(1)}, bf16[64,512]{1,0:T(8,128)(2,1)S(1)}, u32[]{:S(2)}, u32[]{:S(2)}) collective-permute-start(bf16[64,512]{1,0:T(8,128)(2,1)S(1)} %bitcast.109), channel_id=1, source_target_pairs={{0,3},{1,2},{2,1},{3,0},{4,7},{5,6},{6,5},{7,4},{8,11},{9,10},{10,... | collective-permute-start | bytes 196616 | tf_op jit(solution)/shard_map/ppermute | solution.py:33
  29.4 5.1 %collective-permute-start.4 = (bf16[32,512]{1,0:T(8,128)(2,1)S(1)}, bf16[32,512]{1,0:T(8,128)(2,1)S(1)}, u32[]{:S(2)}, u32[]{:S(2)}) collective-permute-start(bf16[32,512]{1,0:T(8,128)(2,1)S(1)} %fusion.13), channel_id=1, source_target_pairs={{0,9},{1,8},{2,11},{3,10},{4,13},{5,12},{6,15},{7,14},{8,1},{9,0},... | collective-permute-start | bytes 98312 | tf_op jit(solution)/shard_map/ppermute | solution.py:33
  36.0 1.4 %collective-permute-start.5 = (bf16[4,2,16,512]{3,2,1,0:T(8,128)(2,1)S(1)}, bf16[4,2,16,512]{3,2,1,0:T(8,128)(2,1)S(1)}, u32[]{:S(2)}, u32[]{:S(2)}) collective-permute-start(bf16[4,2,16,512]{3,2,1,0:T(8,128)(2,1)S(1)} %get-tuple-element.34), channel_id=1, source_target_pairs={{0,1},{1,0},{2,3},{3,2},{4,5},{5,4},{6,7},{7,6},{8,9},{9,8},{10,11... | collective-permute-start | bytes 393224 | tf_op jit(solution)/shard_map/ppermute | solution.py:33
  37.5 4.3 %collective-permute-start.8 = (bf16[32,512]{1,0:T(8,128)(2,1)S(1)}, bf16[32,512]{1,0:T(8,128)(2,1)S(1)}, u32[]{:S(2)}, u32[]{:S(2)}) collective-permute-start(bf16[32,512]{1,0:T(8,128)(2,1)S(1)} %bitcast.121), channel_id=1, source_target_pairs={{0,7},{1,6},{2,5},{3,4},{4,3},{5,2},{6,1},{7,0},{8,15},{9,14},{10,... | collective-permute-start | bytes 98312 | tf_op jit(solution)/shard_map/ppermute | solution.py:33
  37.6 4.8 %collective-permute-start.6 = (bf16[32,512]{1,0:T(8,128)(2,1)S(1)}, bf16[32,512]{1,0:T(8,128)(2,1)S(1)}, u32[]{:S(2)}, u32[]{:S(2)}) collective-permute-start(bf16[32,512]{1,0:T(8,128)(2,1)S(1)} %bitcast.120), channel_id=1, source_target_pairs={{0,4},{1,5},{2,6},{3,7},{4,0},{5,1},{6,2},{7,3},{8,12},{9,13},{10,... | collective-permute-start | bytes 98312 | tf_op jit(solution)/shard_map/ppermute | solution.py:33
  40.0 3.7 %collective-permute-start.7 = (bf16[32,512]{1,0:T(8,128)(2,1)S(1)}, bf16[32,512]{1,0:T(8,128)(2,1)S(1)}, u32[]{:S(2)}, u32[]{:S(2)}) collective-permute-start(bf16[32,512]{1,0:T(8,128)(2,1)S(1)} %bitcast.119), channel_id=1, source_target_pairs={{0,3},{1,2},{2,1},{3,0},{4,7},{5,6},{6,5},{7,4},{8,11},{9,10},{10,... | collective-permute-start | bytes 98312 | tf_op jit(solution)/shard_map/ppermute | solution.py:33
  43.7 5.0 %collective-permute-start.9 = (bf16[32,512]{1,0:T(8,128)(2,1)S(1)}, bf16[32,512]{1,0:T(8,128)(2,1)S(1)}, u32[]{:S(2)}, u32[]{:S(2)}) collective-permute-start(bf16[32,512]{1,0:T(8,128)(2,1)S(1)} %pad_maximum_fusion.9), channel_id=1, source_target_pairs={{0,9},{1,8},{2,11},{3,10},{4,13},{5,12},{6,15},{7,14},{8,1},{9,0},... | collective-permute-start | bytes 98312 | tf_op jit(solution)/shard_map/ppermute | solution.py:33
  50.2 1.6 %collective-permute-start.10 = (f32[4,2,16,512]{3,2,1,0:T(8,128)S(1)}, f32[4,2,16,512]{3,2,1,0:T(8,128)S(1)}, u32[]{:S(2)}, u32[]{:S(2)}) collective-permute-start(f32[4,2,16,512]{3,2,1,0:T(8,128)S(1)} %get-tuple-element.36), channel_id=1, source_target_pairs={{0,1},{1,0},{2,3},{3,2},{4,5},{5,4},{6,7},{7,6},{8,9},{9,8},{10,11... | collective-permute-start | bytes 786440 | tf_op jit(solution)/shard_map/ppermute | solution.py:33
  51.6 24.4 %copy-start.1 = (bf16[8192,256]{1,0:T(8,128)(2,1)S(1)}, bf16[8192,256]{1,0:T(8,128)(2,1)}, u32[]{:S(2)}) copy-start(bf16[8192,256]{1,0:T(8,128)(2,1)} %emission_ref.3) | copy-start | bytes 12582916
  51.9 25.5 %copy-start.3 = (bf16[16,256]{1,0:T(8,128)(2,1)S(1)}, bf16[16,256]{1,0:T(8,128)(2,1)}, u32[]{:S(2)}) copy-start(bf16[16,256]{1,0:T(8,128)(2,1)} %logits_ref.1) | copy-start | bytes 24580
  51.9 5.6 %collective-permute-start.11 = (bf16[96,512]{1,0:T(8,128)(2,1)S(1)}, bf16[96,512]{1,0:T(8,128)(2,1)S(1)}, u32[]{:S(2)}, u32[]{:S(2)}) collective-permute-start(bf16[96,512]{1,0:T(8,128)(2,1)S(1)} %get-tuple-element.63), channel_id=1, source_target_pairs={{0,4},{1,5},{2,6},{3,7},{4,0},{5,1},{6,2},{7,3},{8,12},{9,13},{10,... | collective-permute-start | bytes 294920 | tf_op jit(solution)/shard_map/ppermute | solution.py:33
  52.0 5.6 %collective-permute-start.12 = (bf16[96,512]{1,0:T(8,128)(2,1)S(1)}, bf16[96,512]{1,0:T(8,128)(2,1)S(1)}, u32[]{:S(2)}, u32[]{:S(2)}) collective-permute-start(bf16[96,512]{1,0:T(8,128)(2,1)S(1)} %get-tuple-element.64), channel_id=1, source_target_pairs={{0,3},{1,2},{2,1},{3,0},{4,7},{5,6},{6,5},{7,4},{8,11},{9,10},{10,... | collective-permute-start | bytes 294920 | tf_op jit(solution)/shard_map/ppermute | solution.py:33
  53.0 6.0 %collective-permute-start.13 = (bf16[96,512]{1,0:T(8,128)(2,1)S(1)}, bf16[96,512]{1,0:T(8,128)(2,1)S(1)}, u32[]{:S(2)}, u32[]{:S(2)}) collective-permute-start(bf16[96,512]{1,0:T(8,128)(2,1)S(1)} %get-tuple-element.65), channel_id=1, source_target_pairs={{0,7},{1,6},{2,5},{3,4},{4,3},{5,2},{6,1},{7,0},{8,15},{9,14},{10,... | collective-permute-start | bytes 294920 | tf_op jit(solution)/shard_map/ppermute | solution.py:33
  59.1 4.3 %collective-permute-start.14 = (bf16[32,512]{1,0:T(8,128)(2,1)S(1)}, bf16[32,512]{1,0:T(8,128)(2,1)S(1)}, u32[]{:S(2)}, u32[]{:S(2)}) collective-permute-start(bf16[32,512]{1,0:T(8,128)(2,1)S(1)} %pad_maximum_fusion.10), channel_id=1, source_target_pairs={{0,9},{1,8},{2,11},{3,10},{4,13},{5,12},{6,15},{7,14},{8,1},{9,0},... | collective-permute-start | bytes 98312 | tf_op jit(solution)/shard_map/ppermute | solution.py:33
  59.2 1.4 %collective-permute-start.15 = (bf16[4,2,16,512]{3,2,1,0:T(8,128)(2,1)S(1)}, bf16[4,2,16,512]{3,2,1,0:T(8,128)(2,1)S(1)}, u32[]{:S(2)}, u32[]{:S(2)}) collective-permute-start(bf16[4,2,16,512]{3,2,1,0:T(8,128)(2,1)S(1)} %pad_maximum_fusion.7.near_ref), channel_id=1, source_target_pairs={{0,1},{1,0},{2,3},{3,2},{4,5},{5,4},{6,7},{7,6},{8,9},{9,8},{10,11... | collective-permute-start | bytes 393224 | tf_op jit(solution)/shard_map/ppermute | solution.py:33
  63.4 4.3 %collective-permute-start.16 = (f32[16,512]{1,0:T(8,128)S(1)}, f32[16,512]{1,0:T(8,128)S(1)}, u32[]{:S(2)}, u32[]{:S(2)}) collective-permute-start(f32[16,512]{1,0:T(8,128)S(1)} %last_messages.1), channel_id=1, source_target_pairs={{0,9},{1,8},{2,11},{3,10},{4,13},{5,12},{6,15},{7,14},{8,1},{9,0},... | collective-permute-start | bytes 98312 | tf_op jit(solution)/shard_map/ppermute | solution.py:33
  67.7 3.9 %collective-permute-start.18 = (f32[2,16,512]{2,1,0:T(8,128)S(1)}, f32[2,16,512]{2,1,0:T(8,128)S(1)}, u32[]{:S(2)}, u32[]{:S(2)}) collective-permute-start(f32[2,16,512]{2,1,0:T(8,128)S(1)} %get-tuple-element.54), channel_id=1, source_target_pairs={{0,3},{1,2},{2,1},{3,0},{4,7},{5,6},{6,5},{7,4},{8,11},{9,10},{10,... | collective-permute-start | bytes 196616 | tf_op jit(solution)/shard_map/ppermute | solution.py:33
  68.8 4.6 %collective-permute-start.17 = (f32[2,16,512]{2,1,0:T(8,128)S(1)}, f32[2,16,512]{2,1,0:T(8,128)S(1)}, u32[]{:S(2)}, u32[]{:S(2)}) collective-permute-start(f32[2,16,512]{2,1,0:T(8,128)S(1)} %get-tuple-element.54), channel_id=1, source_target_pairs={{0,4},{1,5},{2,6},{3,7},{4,0},{5,1},{6,2},{7,3},{8,12},{9,13},{10,... | collective-permute-start | bytes 196616 | tf_op jit(solution)/shard_map/ppermute | solution.py:33
  70.7 5.0 %collective-permute-start.19 = (f32[2,16,512]{2,1,0:T(8,128)S(1)}, f32[2,16,512]{2,1,0:T(8,128)S(1)}, u32[]{:S(2)}, u32[]{:S(2)}) collective-permute-start(f32[2,16,512]{2,1,0:T(8,128)S(1)} %get-tuple-element.54), channel_id=1, source_target_pairs={{0,7},{1,6},{2,5},{3,4},{4,3},{5,2},{6,1},{7,0},{8,15},{9,14},{10,... | collective-permute-start | bytes 196616 | tf_op jit(solution)/shard_map/ppermute | solution.py:33
  75.8 1.6 %collective-permute-start.20 = (f32[4,2,16,512]{3,2,1,0:T(8,128)S(1)}, f32[4,2,16,512]{3,2,1,0:T(8,128)S(1)}, u32[]{:S(2)}, u32[]{:S(2)}) collective-permute-start(f32[4,2,16,512]{3,2,1,0:T(8,128)S(1)} %pad_maximum_fusion.parts_ref), channel_id=1, source_target_pairs={{0,1},{1,0},{2,3},{3,2},{4,5},{5,4},{6,7},{7,6},{8,9},{9,8},{10,11... | collective-permute-start | bytes 786440 | tf_op jit(solution)/shard_map/ppermute | solution.py:33
  79.1 10.0 %all-to-all-start.1 = ((f32[16,2,16]{2,1,0:T(2,128)}), f32[16,2,16]{2,1,0:T(2,128)S(1)}, u32[]{:S(2)}, u32[]{:S(2)}) async-start(f32[16,2,16]{2,1,0:T(2,128)} %get-tuple-element.39), calls=%async_computation.1 | async-start | bytes 32768 | tf_op jit(solution)/shard_map/all_to_all | solution.py:20
  (2 other events, 23.2 us)

commit v3 on v0

--- a/solution.py
+++ b/solution.py
@@ -102,24 +102,27 @@
     return rows.reshape(shape)
 
 
-def reduce_blocks(kept, received, wide, devices, count, near_extra=(), far_extra=()):
+def reduce_square(kept, received, wide, devices, count, extra=()):
     total = kept + received.astype(jnp.float32)
-    near, extras = total[0], list(near_extra)
+    near, extras = total[0], list(extra)
     for q, offset in enumerate(square_partners(count)):
         if q:
-            packed = swap(pack(total[q], wide, near_extra), offset, devices)
+            packed = swap(pack(total[q], wide, extra), offset, devices)
             near += unpack(packed, total.shape[1:], wide)
-            for extra in near_extra:
-                extras.append(packed[-extra.shape[0] :])
+            for rows in extra:
+                extras.append(packed[-rows.shape[0] :])
+    return near, extras
+
+
+def reduce_far(near, devices, count, extra=()):
     blocks = [near[0]]
     for h, offset in enumerate(far_partners(count)):
         if h:
-            blocks.append(swap(pack(near[h], wide, far_extra), offset, devices))
-    return blocks, extras
-
-
-def gather_blocks(own, devices, count):
-    far = jnp.stack([own] + [swap(own, offset, devices) for offset in far_partners(count)[1:]])
+            blocks.append(swap(pack(near[h], False, extra), offset, devices))
+    return blocks
+
+
+def gather_square(far, devices, count):
     near = jnp.stack([far] + [swap(far, offset, devices) for offset in square_partners(count)[1:]])
     return near, swap(near, 1, devices)
 
@@ -305,25 +308,29 @@
     )(near, far)
 
 
-def last_kernel(*refs):
+def last_kernel(near_ref, *refs):
     blocks, out_ref = refs[:-2], refs[-1]
-    states = out_ref.shape[0]
-    messages = blocks[0][...]
-    for block in blocks[1:]:
-        for part in range(2):
-            messages += block[pl.ds(part * states, states)].astype(jnp.float32)
-    out_ref[...] = messages
-
-
-def last_sum(blocks, after):
+    count, states, _ = out_ref.shape
+    for h in range(count):
+        messages = near_ref[h]
+        for g, block in enumerate(blocks, 1):
+            for part in range(2):
+                start = (part * count + (h ^ g)) * states
+                messages += block[pl.ds(start, states)].astype(jnp.float32)
+        out_ref[h] = messages
+
+
+def last_sum(near, after, devices, count):
+    packed = pack(near, True, ())
+    blocks = [swap(packed, offset, devices) for offset in far_partners(count)[1:]]
     return pl.pallas_call(
         last_kernel,
-        out_shape=pltpu.VMEM(blocks[0].shape, jnp.float32),
-        in_specs=[VMEM] * len(blocks) + [ANY],
+        out_shape=pltpu.VMEM(near.shape, jnp.float32),
+        in_specs=[VMEM] * (1 + len(blocks)) + [ANY],
         out_specs=VMEM,
         compiler_params=PARAMS,
         name="last_messages",
-    )(*blocks, after)
+    )(near, *blocks, after)
 
 
 def half_products(halves, transition_ref, out_ref, count, first):
@@ -503,22 +510,23 @@
             kept, received = step(
                 transition, route, sums, parts, dtype, devices, count, kept_rows, sent_rows
             )
-            kept_rows, sent_rows, near_extra, far_extra = (), (), (), ()
+            kept_rows, sent_rows, extra = (), (), ()
             if window_step == 1:
                 forward = forward_messages_here(prior_msg, parts, devices)
-                far_extra = (forward,)
             if window_step == 2:
-                near_extra = (forward,)
-            parts, extras = reduce_blocks(
-                kept, received, wide, devices, count, near_extra, far_extra
-            )
+                extra = (forward,)
+            near, extras = reduce_square(kept, received, wide, devices, count, extra)
+            if window_step == 0:
+                parts = reduce_far(near, devices, count)
             if window_step == 1:
+                parts = reduce_far(near, devices, count, (forward,))
                 others = [part[-devices:] for part in parts[1:]]
                 forward = jnp.concatenate([forward] + others, axis=0)
-        near = jnp.stack(extras).reshape(4, devices // 8, devices, own_rows)
-        forward = order_forward(near, swap(near, 1, devices), count)
-        messages = last_sum(parts, forward)
-        near, far = gather_blocks(messages, devices, count)
+        forward = jnp.stack(extras).reshape(4, devices // 8, devices, own_rows)
+        forward = order_forward(forward, swap(forward, 1, devices), count)
+        messages = last_sum(near, forward, devices, count)
+        near, far = gather_square(messages, devices, count)
+        messages = messages[0]
         raised, pair = weigh(emission, forward, chooser, lm_logits, near, far, count)
         return messages.T, normalise(raised, pair, devices)
     state_ids = jnp.arange(states, dtype=jnp.int32)

time: 90.4 us -> 86.4 us (0.956)
  waiting for transfers between devices: 39.1 us -> 35.3 us
    ppermute x21 -> x20, waiting for transfers between devices: 33.3 us -> 29.5 us  [swap(): return lax.ppermute(block, 'vocab', pairs)]
    unnamed x11 -> x10, local copies, waits for them, and re-layouts: 2.97 us -> 2.35 us
    ppermute x21 -> x20, starting transfers between devices: 14.2 us -> 13.9 us  [swap(): return lax.ppermute(block, 'vocab', pairs)]
  transfers between devices with their start and end apart: 22 -> 21, of which waited for: 20 -> 19; matrix products, arithmetic and copies ran while one was open for 1% -> 1% of each run, Pallas kernels for 6% -> 6%
where the time goes in v3:
time: 86.4 us; the launch traced here: 86.2 us
  waiting for transfers between devices  35.3 us (41%)
  starting transfers between devices  17.4 us (20%)
  blocking collectives  13.8 us (16%)
  Pallas kernels  13.6 us (16%)
  local copies, waits for them, and re-layouts  3.87 us (4%)
  other arithmetic  1.26 us (1%)
  between operations  0.93 us (1%)
    ppermute x20, waiting for transfers between devices, swap(): return lax.ppermute(block, 'vocab', pairs)  29.5 us
    ppermute x20, starting transfers between devices, swap(): return lax.ppermute(block, 'vocab', pairs)  13.9 us
    all_to_all x1, blocking collectives, exchange(): lax.all_to_all(blocks, 'vocab', split_axis=0, concat_axis=0, tiled=True)  13.8 us
    all_to_all x1, waiting for transfers between devices, exchange(): lax.all_to_all(blocks, 'vocab', split_axis=0, concat_axis=0, tiled=True)  5.86 us
    pallas_call x3, Pallas kernels, step(): pl.pallas_call(functools.partial(send_kernel, count, len(parts)), out_sha...  4.34 us
    pallas_call x3, Pallas kernels, step(): pl.pallas_call(functools.partial(keep_kernel, count), out_shape=pltpu.VME...  3.88 us
    all_to_all x1, starting transfers between devices, exchange(): lax.all_to_all(blocks, 'vocab', split_axis=0, concat_axis=0, tiled=True)  3.5 us
    pallas_call x1, Pallas kernels, first_products(): pl.pallas_call(functools.partial(products_kernel, count), out_shape=[jax....  2.38 us
  transfers between devices with their start and end apart: 21, of which 19 were waited for; matrix products, arithmetic and copies ran while one was open for 1% of the time, Pallas kernels for 6%

profile of v3, /device:TPU:0, one launch (start us, length us, event | category | flops | bytes accessed | tf_op | source)
XLA Modules:
  0.0 86.2 jit_solution(2569052296307498178)
XLA Ops:
  0.7 2.3 %copy-done.1 = bf16[8192,256]{1,0:T(8,128)(2,1)S(1)} copy-done((bf16[8192,256]{1,0:T(8,128)(2,1)S(1)}, bf16[8192,256]{1,0:T(8,128)(2,1)}, u32[]{:S(2)}) %copy-start.1) | copy-done | bytes 4194328
  3.0 2.4 %first_products.1 = (f32[16,1,512]{2,1,0:T(1,128)S(1)}, bf16[4,2,16,512]{3,2,1,0:T(8,128)(2,1)S(1)}, bf16[4,2,16,512]{3,2,1,0:T(8,128)(2,1)S(1)}, s32[1,16]{1,0:...) custom-call(s32[16]{0:T(128)} %token_hbm.1, s32[1,16]{1,0:T(1,128)} %bitcast.118, ...), custom_call_target="tpu_custom_call" | custom-call | tf_op jit(solution)/shard_map/first_products/pallas_call | solution.py:233
  5.8 13.8 %all_to_all.10.sums_ref = f32[16,1,512]{2,1,0:T(1,128)S(1)} all-to-all(f32[16,1,512]{2,1,0:T(1,128)S(1)} %get-tuple-element.25), channel_id=1, replica_groups=mesh['parts'=2,'vocab'=16] {'vocab'}, dimensions={0} | all-to-all | bytes 65536 | tf_op jit(solution)/shard_map/all_to_all | solution.py:20
  19.6 1.5 %step_sent_half.3 = (bf16[32,512]{1,0:T(8,128)(2,1)S(1)}, bf16[4,2,32,512]{3,2,1,0:T(8,128)(2,1)S(1)}) custom-call(bf16[8192,512]{1,0:T(8,128)(2,1)S(1)} %copy-done, bf16[256,48]{1,0:T(8,128)(2,1)S(1)} %get-tuple-element.24.route_ref, f32[16,1,512]{2,1,0:T(1,128)S(1)} %all_to_all.10.sums_ref, f32[16,512]{1,0:T(8,128)S(1)} %get-tuple-element.26.refs_0_, ...), custom_call_target="tpu_custom_call" | custom-call | tf_op jit(solution)/shard_map/step_sent_half/pallas_call | solution.py:382
  21.1 1.3 %step_kept_half.3 = f32[4,2,32,512]{3,2,1,0:T(8,128)S(1)} custom-call(bf16[8192,512]{1,0:T(8,128)(2,1)S(1)} %copy-done, bf16[32,512]{1,0:T(8,128)(2,1)S(1)} %get-tuple-element.28.halves_ref, bf16[4,2,16,512]{3,2,1,0:T(8,128)(2,1)S(1)} %get-tuple-element.29.refs_0_), custom_call_target="tpu_custom_call" | custom-call | tf_op jit(solution)/shard_map/step_kept_half/pallas_call | solution.py:394
  23.1 1.4 %collective-permute-start.1 = (bf16[64,512]{1,0:T(8,128)(2,1)S(1)}, bf16[64,512]{1,0:T(8,128)(2,1)S(1)}, u32[]{:S(2)}, u32[]{:S(2)}) collective-permute-start(bf16[64,512]{1,0:T(8,128)(2,1)S(1)} %bitcast.104), channel_id=1, source_target_pairs={{0,4},{1,5},{2,6},{3,7},{4,0},{5,1},{6,2},{7,3},{8,12},{9,13},{10,... | collective-permute-start | bytes 196616 | tf_op jit(solution)/shard_map/ppermute | solution.py:33
  25.7 2.0 %collective-permute-done.3 = bf16[64,512]{1,0:T(8,128)(2,1)S(1)} collective-permute-done((bf16[64,512]{1,0:T(8,128)(2,1)S(1)}, bf16[64,512]{1,0:T(8,128)(2,1)S(1)}, u32[]{:S(2)}, u32[]{:S(2)}) %collective-permute-start.3) | collective-permute-done | bytes 65568 | tf_op jit(solution)/shard_map/ppermute | solution.py:33
  29.7 5.0 %collective-permute-done.4.refs_1_ = bf16[32,512]{1,0:T(8,128)(2,1)S(1)} collective-permute-done((bf16[32,512]{1,0:T(8,128)(2,1)S(1)}, bf16[32,512]{1,0:T(8,128)(2,1)S(1)}, u32[]{:S(2)}, u32[]{:S(2)}) %collective-permute-start.4) | collective-permute-done | bytes 32800 | tf_op jit(solution)/shard_map/ppermute | solution.py:33
  34.7 1.4 %step_sent_half.4 = (bf16[32,512]{1,0:T(8,128)(2,1)S(1)}, bf16[4,2,16,512]{3,2,1,0:T(8,128)(2,1)S(1)}) custom-call(bf16[8192,512]{1,0:T(8,128)(2,1)S(1)} %copy-done, bf16[256,48]{1,0:T(8,128)(2,1)S(1)} %get-tuple-element.24.route_ref, f32[16,1,512]{2,1,0:T(1,128)S(1)} %all_to_all.10.sums_ref, f32[32,512]{1,0:T(8,128)S(1)} %slice_bitcast_fusion.2.refs_0_, ...), custom_call_target="tpu_custom_call" | custom-call | tf_op jit(solution)/shard_map/step_sent_half/pallas_call | solution.py:382
  36.2 1.3 %step_kept_half.4 = f32[4,2,16,512]{3,2,1,0:T(8,128)S(1)} custom-call(bf16[8192,512]{1,0:T(8,128)(2,1)S(1)} %copy-done, bf16[32,512]{1,0:T(8,128)(2,1)S(1)} %get-tuple-element.31.halves_ref), custom_call_target="tpu_custom_call" | custom-call | tf_op jit(solution)/shard_map/step_kept_half/pallas_call | solution.py:394
  37.7 2.4 %collective-permute-start.6 = (bf16[32,512]{1,0:T(8,128)(2,1)S(1)}, bf16[32,512]{1,0:T(8,128)(2,1)S(1)}, u32[]{:S(2)}, u32[]{:S(2)}) collective-permute-start(bf16[32,512]{1,0:T(8,128)(2,1)S(1)} %bitcast.114), channel_id=1, source_target_pairs={{0,4},{1,5},{2,6},{3,7},{4,0},{5,1},{6,2},{7,3},{8,12},{9,13},{10,... | collective-permute-start | bytes 98312 | tf_op jit(solution)/shard_map/ppermute | solution.py:33
  42.5 1.3 %collective-permute-done.7 = bf16[32,512]{1,0:T(8,128)(2,1)S(1)} collective-permute-done((bf16[32,512]{1,0:T(8,128)(2,1)S(1)}, bf16[32,512]{1,0:T(8,128)(2,1)S(1)}, u32[]{:S(2)}, u32[]{:S(2)}) %collective-permute-start.7) | collective-permute-done | bytes 32800 | tf_op jit(solution)/shard_map/ppermute | solution.py:33
  43.9 4.9 %collective-permute-done.9.refs_1_ = bf16[32,512]{1,0:T(8,128)(2,1)S(1)} collective-permute-done((bf16[32,512]{1,0:T(8,128)(2,1)S(1)}, bf16[32,512]{1,0:T(8,128)(2,1)S(1)}, u32[]{:S(2)}, u32[]{:S(2)}) %collective-permute-start.9) | collective-permute-done | bytes 32800 | tf_op jit(solution)/shard_map/ppermute | solution.py:33
  48.9 1.4 %step_sent_half.5 = (bf16[32,512]{1,0:T(8,128)(2,1)S(1)}, f32[4,2,16,512]{3,2,1,0:T(8,128)S(1)}) custom-call(bf16[8192,512]{1,0:T(8,128)(2,1)S(1)} %copy-done, bf16[256,48]{1,0:T(8,128)(2,1)S(1)} %get-tuple-element.24.route_ref, f32[16,1,512]{2,1,0:T(1,128)S(1)} %all_to_all.10.sums_ref, f32[16,512]{1,0:T(8,128)S(1)} %slice_bitcast_fusion.4.refs_0_, ...), custom_call_target="tpu_custom_call" | custom-call | tf_op jit(solution)/shard_map/step_sent_half/pallas_call | solution.py:382
  50.4 1.3 %step_kept_half.5 = f32[4,2,16,512]{3,2,1,0:T(8,128)S(1)} custom-call(bf16[8192,512]{1,0:T(8,128)(2,1)S(1)} %copy-done, bf16[32,512]{1,0:T(8,128)(2,1)S(1)} %get-tuple-element.33.halves_ref), custom_call_target="tpu_custom_call" | custom-call | tf_op jit(solution)/shard_map/step_kept_half/pallas_call | solution.py:394
  53.1 2.2 %collective-permute-start.13 = (bf16[96,512]{1,0:T(8,128)(2,1)S(1)}, bf16[96,512]{1,0:T(8,128)(2,1)S(1)}, u32[]{:S(2)}, u32[]{:S(2)}) collective-permute-start(bf16[96,512]{1,0:T(8,128)(2,1)S(1)} %get-tuple-element.65), channel_id=1, source_target_pairs={{0,7},{1,6},{2,5},{3,4},{4,3},{5,2},{6,1},{7,0},{8,15},{9,14},{10,... | collective-permute-start | bytes 294920 | tf_op jit(solution)/shard_map/ppermute | solution.py:33
  55.3 2.4 %collective-permute-done.11 = bf16[96,512]{1,0:T(8,128)(2,1)S(1)} collective-permute-done((bf16[96,512]{1,0:T(8,128)(2,1)S(1)}, bf16[96,512]{1,0:T(8,128)(2,1)S(1)}, u32[]{:S(2)}, u32[]{:S(2)}) %collective-permute-start.11) | collective-permute-done | bytes 98336 | tf_op jit(solution)/shard_map/ppermute | solution.py:33
  57.7 1.4 %collective-permute-done.13 = bf16[96,512]{1,0:T(8,128)(2,1)S(1)} collective-permute-done((bf16[96,512]{1,0:T(8,128)(2,1)S(1)}, bf16[96,512]{1,0:T(8,128)(2,1)S(1)}, u32[]{:S(2)}, u32[]{:S(2)}) %collective-permute-start.13) | collective-permute-done | bytes 98336 | tf_op jit(solution)/shard_map/ppermute | solution.py:33
  61.1 2.9 %collective-permute-done.14.refs_0_ = bf16[64,512]{1,0:T(8,128)(2,1)S(1)} collective-permute-done((bf16[64,512]{1,0:T(8,128)(2,1)S(1)}, bf16[64,512]{1,0:T(8,128)(2,1)S(1)}, u32[]{:S(2)}, u32[]{:S(2)}) %collective-permute-start.14) | collective-permute-done | bytes 65568 | tf_op jit(solution)/shard_map/ppermute | solution.py:33
  64.0 2.6 %collective-permute-start.18 = (f32[2,16,512]{2,1,0:T(8,128)S(1)}, f32[2,16,512]{2,1,0:T(8,128)S(1)}, u32[]{:S(2)}, u32[]{:S(2)}) collective-permute-start(f32[2,16,512]{2,1,0:T(8,128)S(1)} %last_messages.1), channel_id=1, source_target_pairs={{0,7},{1,6},{2,5},{3,4},{4,3},{5,2},{6,1},{7,0},{8,15},{9,14},{10,... | collective-permute-start | bytes 196616 | tf_op jit(solution)/shard_map/ppermute | solution.py:33
  67.5 1.6 %collective-permute-done.18 = f32[2,16,512]{2,1,0:T(8,128)S(1)} collective-permute-done((f32[2,16,512]{2,1,0:T(8,128)S(1)}, f32[2,16,512]{2,1,0:T(8,128)S(1)}, u32[]{:S(2)}, u32[]{:S(2)}) %collective-permute-start.18) | collective-permute-done | bytes 65568 | tf_op jit(solution)/shard_map/ppermute | solution.py:33
  69.1 1.4 %collective-permute-done.17 = f32[2,16,512]{2,1,0:T(8,128)S(1)} collective-permute-done((f32[2,16,512]{2,1,0:T(8,128)S(1)}, f32[2,16,512]{2,1,0:T(8,128)S(1)}, u32[]{:S(2)}, u32[]{:S(2)}) %collective-permute-start.17) | collective-permute-done | bytes 65568 | tf_op jit(solution)/shard_map/ppermute | solution.py:33
  75.2 3.5 %all-to-all-start.1 = ((f32[16,2,16]{2,1,0:T(2,128)}), f32[16,2,16]{2,1,0:T(2,128)S(1)}, u32[]{:S(2)}, u32[]{:S(2)}) async-start(f32[16,2,16]{2,1,0:T(2,128)} %broadcast_in_dim.7), calls=%async_computation.1 | async-start | bytes 32768 | tf_op jit(solution)/shard_map/all_to_all | solution.py:20
  79.3 5.9 %all-to-all-done.1 = f32[16,2,16]{2,1,0:T(2,128)S(1)} async-done(((f32[16,2,16]{2,1,0:T(2,128)}), f32[16,2,16]{2,1,0:T(2,128)S(1)}, u32[]{:S(2)}, u32[]{:S(2)}) %all-to-all-start.1) | async-done | bytes 2080 | tf_op jit(solution)/shard_map/all_to_all | solution.py:20
  (79 shorter events, 17.6 us)
Async XLA Ops:
  0.6 19.0 %copy-start = (bf16[8192,512]{1,0:T(8,128)(2,1)S(1)}, bf16[8192,512]{1,0:T(8,128)(2,1)}, u32[]{:S(2)}) copy-start(bf16[8192,512]{1,0:T(8,128)(2,1)} %transition_ref.11) | copy-start | bytes 25165828
  21.1 1.6 %collective-permute-start = (bf16[4,2,32,512]{3,2,1,0:T(8,128)(2,1)S(1)}, bf16[4,2,32,512]{3,2,1,0:T(8,128)(2,1)S(1)}, u32[]{:S(2)}, u32[]{:S(2)}) collective-permute-start(bf16[4,2,32,512]{3,2,1,0:T(8,128)(2,1)S(1)} %get-tuple-element.30), channel_id=1, source_target_pairs={{0,1},{1,0},{2,3},{3,2},{4,5},{5,4},{6,7},{7,6},{8,9},{9,8},{10,11... | collective-permute-start | bytes 786440 | tf_op jit(solution)/shard_map/ppermute | solution.py:33
  22.8 5.0 %collective-permute-start.3 = (bf16[64,512]{1,0:T(8,128)(2,1)S(1)}, bf16[64,512]{1,0:T(8,128)(2,1)S(1)}, u32[]{:S(2)}, u32[]{:S(2)}) collective-permute-start(bf16[64,512]{1,0:T(8,128)(2,1)S(1)} %bitcast.105), channel_id=1, source_target_pairs={{0,7},{1,6},{2,5},{3,4},{4,3},{5,2},{6,1},{7,0},{8,15},{9,14},{10,... | collective-permute-start | bytes 196616 | tf_op jit(solution)/shard_map/ppermute | solution.py:33
  23.1 5.3 %collective-permute-start.1 = (bf16[64,512]{1,0:T(8,128)(2,1)S(1)}, bf16[64,512]{1,0:T(8,128)(2,1)S(1)}, u32[]{:S(2)}, u32[]{:S(2)}) collective-permute-start(bf16[64,512]{1,0:T(8,128)(2,1)S(1)} %bitcast.104), channel_id=1, source_target_pairs={{0,4},{1,5},{2,6},{3,7},{4,0},{5,1},{6,2},{7,3},{8,12},{9,13},{10,... | collective-permute-start | bytes 196616 | tf_op jit(solution)/shard_map/ppermute | solution.py:33
  24.5 5.0 %collective-permute-start.2 = (bf16[64,512]{1,0:T(8,128)(2,1)S(1)}, bf16[64,512]{1,0:T(8,128)(2,1)S(1)}, u32[]{:S(2)}, u32[]{:S(2)}) collective-permute-start(bf16[64,512]{1,0:T(8,128)(2,1)S(1)} %bitcast.103), channel_id=1, source_target_pairs={{0,3},{1,2},{2,1},{3,0},{4,7},{5,6},{6,5},{7,4},{8,11},{9,10},{10,... | collective-permute-start | bytes 196616 | tf_op jit(solution)/shard_map/ppermute | solution.py:33
  29.5 5.1 %collective-permute-start.4 = (bf16[32,512]{1,0:T(8,128)(2,1)S(1)}, bf16[32,512]{1,0:T(8,128)(2,1)S(1)}, u32[]{:S(2)}, u32[]{:S(2)}) collective-permute-start(bf16[32,512]{1,0:T(8,128)(2,1)S(1)} %fusion.14), channel_id=1, source_target_pairs={{0,9},{1,8},{2,11},{3,10},{4,13},{5,12},{6,15},{7,14},{8,1},{9,0},... | collective-permute-start | bytes 98312 | tf_op jit(solution)/shard_map/ppermute | solution.py:33
  36.1 1.4 %collective-permute-start.5 = (bf16[4,2,16,512]{3,2,1,0:T(8,128)(2,1)S(1)}, bf16[4,2,16,512]{3,2,1,0:T(8,128)(2,1)S(1)}, u32[]{:S(2)}, u32[]{:S(2)}) collective-permute-start(bf16[4,2,16,512]{3,2,1,0:T(8,128)(2,1)S(1)} %get-tuple-element.32), channel_id=1, source_target_pairs={{0,1},{1,0},{2,3},{3,2},{4,5},{5,4},{6,7},{7,6},{8,9},{9,8},{10,11... | collective-permute-start | bytes 393224 | tf_op jit(solution)/shard_map/ppermute | solution.py:33
  37.6 4.3 %collective-permute-start.8 = (bf16[32,512]{1,0:T(8,128)(2,1)S(1)}, bf16[32,512]{1,0:T(8,128)(2,1)S(1)}, u32[]{:S(2)}, u32[]{:S(2)}) collective-permute-start(bf16[32,512]{1,0:T(8,128)(2,1)S(1)} %bitcast.115), channel_id=1, source_target_pairs={{0,7},{1,6},{2,5},{3,4},{4,3},{5,2},{6,1},{7,0},{8,15},{9,14},{10,... | collective-permute-start | bytes 98312 | tf_op jit(solution)/shard_map/ppermute | solution.py:33
  37.7 4.8 %collective-permute-start.6 = (bf16[32,512]{1,0:T(8,128)(2,1)S(1)}, bf16[32,512]{1,0:T(8,128)(2,1)S(1)}, u32[]{:S(2)}, u32[]{:S(2)}) collective-permute-start(bf16[32,512]{1,0:T(8,128)(2,1)S(1)} %bitcast.114), channel_id=1, source_target_pairs={{0,4},{1,5},{2,6},{3,7},{4,0},{5,1},{6,2},{7,3},{8,12},{9,13},{10,... | collective-permute-start | bytes 98312 | tf_op jit(solution)/shard_map/ppermute | solution.py:33
  40.1 3.7 %collective-permute-start.7 = (bf16[32,512]{1,0:T(8,128)(2,1)S(1)}, bf16[32,512]{1,0:T(8,128)(2,1)S(1)}, u32[]{:S(2)}, u32[]{:S(2)}) collective-permute-start(bf16[32,512]{1,0:T(8,128)(2,1)S(1)} %bitcast.113), channel_id=1, source_target_pairs={{0,3},{1,2},{2,1},{3,0},{4,7},{5,6},{6,5},{7,4},{8,11},{9,10},{10,... | collective-permute-start | bytes 98312 | tf_op jit(solution)/shard_map/ppermute | solution.py:33
  43.9 5.0 %collective-permute-start.9 = (bf16[32,512]{1,0:T(8,128)(2,1)S(1)}, bf16[32,512]{1,0:T(8,128)(2,1)S(1)}, u32[]{:S(2)}, u32[]{:S(2)}) collective-permute-start(bf16[32,512]{1,0:T(8,128)(2,1)S(1)} %pad_maximum_fusion.9), channel_id=1, source_target_pairs={{0,9},{1,8},{2,11},{3,10},{4,13},{5,12},{6,15},{7,14},{8,1},{9,0},... | collective-permute-start | bytes 98312 | tf_op jit(solution)/shard_map/ppermute | solution.py:33
  50.3 21.6 %copy-start.2 = (bf16[8192,256]{1,0:T(8,128)(2,1)S(1)}, bf16[8192,256]{1,0:T(8,128)(2,1)}, u32[]{:S(2)}) copy-start(bf16[8192,256]{1,0:T(8,128)(2,1)} %emission_ref.7) | copy-start | bytes 12582916
  50.3 1.6 %collective-permute-start.10 = (f32[4,2,16,512]{3,2,1,0:T(8,128)S(1)}, f32[4,2,16,512]{3,2,1,0:T(8,128)S(1)}, u32[]{:S(2)}, u32[]{:S(2)}) collective-permute-start(f32[4,2,16,512]{3,2,1,0:T(8,128)S(1)} %get-tuple-element.34), channel_id=1, source_target_pairs={{0,1},{1,0},{2,3},{3,2},{4,5},{5,4},{6,7},{7,6},{8,9},{9,8},{10,11... | collective-permute-start | bytes 786440 | tf_op jit(solution)/shard_map/ppermute | solution.py:33
  50.4 23.0 %copy-start.4 = (bf16[16,256]{1,0:T(8,128)(2,1)S(1)}, bf16[16,256]{1,0:T(8,128)(2,1)}, u32[]{:S(2)}) copy-start(bf16[16,256]{1,0:T(8,128)(2,1)} %logits_ref.1) | copy-start | bytes 24580
  52.0 5.6 %collective-permute-start.11 = (bf16[96,512]{1,0:T(8,128)(2,1)S(1)}, bf16[96,512]{1,0:T(8,128)(2,1)S(1)}, u32[]{:S(2)}, u32[]{:S(2)}) collective-permute-start(bf16[96,512]{1,0:T(8,128)(2,1)S(1)} %get-tuple-element.63), channel_id=1, source_target_pairs={{0,4},{1,5},{2,6},{3,7},{4,0},{5,1},{6,2},{7,3},{8,12},{9,13},{10,... | collective-permute-start | bytes 294920 | tf_op jit(solution)/shard_map/ppermute | solution.py:33
  52.1 5.6 %collective-permute-start.12 = (bf16[96,512]{1,0:T(8,128)(2,1)S(1)}, bf16[96,512]{1,0:T(8,128)(2,1)S(1)}, u32[]{:S(2)}, u32[]{:S(2)}) collective-permute-start(bf16[96,512]{1,0:T(8,128)(2,1)S(1)} %get-tuple-element.64), channel_id=1, source_target_pairs={{0,3},{1,2},{2,1},{3,0},{4,7},{5,6},{6,5},{7,4},{8,11},{9,10},{10,... | collective-permute-start | bytes 294920 | tf_op jit(solution)/shard_map/ppermute | solution.py:33
  53.1 6.0 %collective-permute-start.13 = (bf16[96,512]{1,0:T(8,128)(2,1)S(1)}, bf16[96,512]{1,0:T(8,128)(2,1)S(1)}, u32[]{:S(2)}, u32[]{:S(2)}) collective-permute-start(bf16[96,512]{1,0:T(8,128)(2,1)S(1)} %get-tuple-element.65), channel_id=1, source_target_pairs={{0,7},{1,6},{2,5},{3,4},{4,3},{5,2},{6,1},{7,0},{8,15},{9,14},{10,... | collective-permute-start | bytes 294920 | tf_op jit(solution)/shard_map/ppermute | solution.py:33
  59.2 4.8 %collective-permute-start.14 = (bf16[64,512]{1,0:T(8,128)(2,1)S(1)}, bf16[64,512]{1,0:T(8,128)(2,1)S(1)}, u32[]{:S(2)}, u32[]{:S(2)}) collective-permute-start(bf16[64,512]{1,0:T(8,128)(2,1)S(1)} %pad_maximum_fusion.8), channel_id=1, source_target_pairs={{0,9},{1,8},{2,11},{3,10},{4,13},{5,12},{6,15},{7,14},{8,1},{9,0},... | collective-permute-start | bytes 196616 | tf_op jit(solution)/shard_map/ppermute | solution.py:33
  59.3 1.5 %collective-permute-start.15 = (bf16[4,2,16,512]{3,2,1,0:T(8,128)(2,1)S(1)}, bf16[4,2,16,512]{3,2,1,0:T(8,128)(2,1)S(1)}, u32[]{:S(2)}, u32[]{:S(2)}) collective-permute-start(bf16[4,2,16,512]{3,2,1,0:T(8,128)(2,1)S(1)} %pad_maximum_fusion.7.near_ref), channel_id=1, source_target_pairs={{0,1},{1,0},{2,3},{3,2},{4,5},{5,4},{6,7},{7,6},{8,9},{9,8},{10,11... | collective-permute-start | bytes 393224 | tf_op jit(solution)/shard_map/ppermute | solution.py:33
  64.0 5.1 %collective-permute-start.18 = (f32[2,16,512]{2,1,0:T(8,128)S(1)}, f32[2,16,512]{2,1,0:T(8,128)S(1)}, u32[]{:S(2)}, u32[]{:S(2)}) collective-permute-start(f32[2,16,512]{2,1,0:T(8,128)S(1)} %last_messages.1), channel_id=1, source_target_pairs={{0,7},{1,6},{2,5},{3,4},{4,3},{5,2},{6,1},{7,0},{8,15},{9,14},{10,... | collective-permute-start | bytes 196616 | tf_op jit(solution)/shard_map/ppermute | solution.py:33
  66.6 3.9 %collective-permute-start.17 = (f32[2,16,512]{2,1,0:T(8,128)S(1)}, f32[2,16,512]{2,1,0:T(8,128)S(1)}, u32[]{:S(2)}, u32[]{:S(2)}) collective-permute-start(f32[2,16,512]{2,1,0:T(8,128)S(1)} %last_messages.1), channel_id=1, source_target_pairs={{0,3},{1,2},{2,1},{3,0},{4,7},{5,6},{6,5},{7,4},{8,11},{9,10},{10,... | collective-permute-start | bytes 196616 | tf_op jit(solution)/shard_map/ppermute | solution.py:33
  67.5 4.3 %collective-permute-start.16 = (f32[2,16,512]{2,1,0:T(8,128)S(1)}, f32[2,16,512]{2,1,0:T(8,128)S(1)}, u32[]{:S(2)}, u32[]{:S(2)}) collective-permute-start(f32[2,16,512]{2,1,0:T(8,128)S(1)} %last_messages.1), channel_id=1, source_target_pairs={{0,4},{1,5},{2,6},{3,7},{4,0},{5,1},{6,2},{7,3},{8,12},{9,13},{10,... | collective-permute-start | bytes 196616 | tf_op jit(solution)/shard_map/ppermute | solution.py:33
  71.8 1.6 %collective-permute-start.19 = (f32[4,2,16,512]{3,2,1,0:T(8,128)S(1)}, f32[4,2,16,512]{3,2,1,0:T(8,128)S(1)}, u32[]{:S(2)}, u32[]{:S(2)}) collective-permute-start(f32[4,2,16,512]{3,2,1,0:T(8,128)S(1)} %pad_maximum_fusion.parts_ref), channel_id=1, source_target_pairs={{0,1},{1,0},{2,3},{3,2},{4,5},{5,4},{6,7},{7,6},{8,9},{9,8},{10,11... | collective-permute-start | bytes 786440 | tf_op jit(solution)/shard_map/ppermute | solution.py:33
  75.2 10.0 %all-to-all-start.1 = ((f32[16,2,16]{2,1,0:T(2,128)}), f32[16,2,16]{2,1,0:T(2,128)S(1)}, u32[]{:S(2)}, u32[]{:S(2)}) async-start(f32[16,2,16]{2,1,0:T(2,128)} %broadcast_in_dim.7), calls=%async_computation.1 | async-start | bytes 32768 | tf_op jit(solution)/shard_map/all_to_all | solution.py:20
  (2 other events, 13.3 us)

commit v4 on v3

--- a/solution.py
+++ b/solution.py
@@ -25,7 +25,7 @@
 
 
 def basis(count):
-    return [1, 3, 4] + [(1 << bit) | 1 for bit in range(3, count)]
+    return [1] + [(1 << bit) | 1 for bit in range(1, count)]
 
 
 def swap(block, offset, devices):

time: 86.4 us -> 86 us (level)
  transfers between devices with their start and end apart: 21 -> 21, of which waited for: 19 -> 18; matrix products, arithmetic and copies ran while one was open for 1% -> 1% of each run, Pallas kernels for 6% -> 6%
where the time goes in v4:
time: 86 us; the launch traced here: 85.8 us
  waiting for transfers between devices  34.9 us (41%)
  starting transfers between devices  17.5 us (20%)
  blocking collectives  13.8 us (16%)
  Pallas kernels  13.6 us (16%)
  local copies, waits for them, and re-layouts  3.87 us (4%)
  other arithmetic  1.26 us (1%)
  between operations  0.92 us (1%)
    ppermute x20, waiting for transfers between devices, swap(): return lax.ppermute(block, 'vocab', pairs)  29 us
    ppermute x20, starting transfers between devices, swap(): return lax.ppermute(block, 'vocab', pairs)  14 us
    all_to_all x1, blocking collectives, exchange(): lax.all_to_all(blocks, 'vocab', split_axis=0, concat_axis=0, tiled=True)  13.8 us
    all_to_all x1, waiting for transfers between devices, exchange(): lax.all_to_all(blocks, 'vocab', split_axis=0, concat_axis=0, tiled=True)  5.84 us
    pallas_call x3, Pallas kernels, step(): pl.pallas_call(functools.partial(send_kernel, count, len(parts)), out_sha...  4.34 us
    pallas_call x3, Pallas kernels, step(): pl.pallas_call(functools.partial(keep_kernel, count), out_shape=pltpu.VME...  3.88 us
    all_to_all x1, starting transfers between devices, exchange(): lax.all_to_all(blocks, 'vocab', split_axis=0, concat_axis=0, tiled=True)  3.49 us
    pallas_call x1, Pallas kernels, first_products(): pl.pallas_call(functools.partial(products_kernel, count), out_shape=[jax....  2.38 us
  transfers between devices with their start and end apart: 21, of which 18 were waited for; matrix products, arithmetic and copies ran while one was open for 1% of the time, Pallas kernels for 6%

profile of v4, /device:TPU:0, one launch (start us, length us, event | category | flops | bytes accessed | tf_op | source)
XLA Modules:
  0.0 85.8 jit_solution(6534569353309862056)
XLA Ops:
  0.7 2.3 %copy-done.1 = bf16[8192,256]{1,0:T(8,128)(2,1)S(1)} copy-done((bf16[8192,256]{1,0:T(8,128)(2,1)S(1)}, bf16[8192,256]{1,0:T(8,128)(2,1)}, u32[]{:S(2)}) %copy-start.1) | copy-done | bytes 4194328
  3.0 2.4 %first_products.1 = (f32[16,1,512]{2,1,0:T(1,128)S(1)}, bf16[4,2,16,512]{3,2,1,0:T(8,128)(2,1)S(1)}, bf16[4,2,16,512]{3,2,1,0:T(8,128)(2,1)S(1)}, s32[1,16]{1,0:...) custom-call(s32[16]{0:T(128)} %token_hbm.1, s32[1,16]{1,0:T(1,128)} %bitcast.118, ...), custom_call_target="tpu_custom_call" | custom-call | tf_op jit(solution)/shard_map/first_products/pallas_call | solution.py:233
  5.8 13.8 %all_to_all.10.sums_ref = f32[16,1,512]{2,1,0:T(1,128)S(1)} all-to-all(f32[16,1,512]{2,1,0:T(1,128)S(1)} %get-tuple-element.25), channel_id=1, replica_groups=mesh['parts'=2,'vocab'=16] {'vocab'}, dimensions={0} | all-to-all | bytes 65536 | tf_op jit(solution)/shard_map/all_to_all | solution.py:20
  19.6 1.5 %step_sent_half.3 = (bf16[32,512]{1,0:T(8,128)(2,1)S(1)}, bf16[4,2,32,512]{3,2,1,0:T(8,128)(2,1)S(1)}) custom-call(bf16[8192,512]{1,0:T(8,128)(2,1)S(1)} %copy-done, bf16[256,48]{1,0:T(8,128)(2,1)S(1)} %get-tuple-element.24.route_ref, f32[16,1,512]{2,1,0:T(1,128)S(1)} %all_to_all.10.sums_ref, f32[16,512]{1,0:T(8,128)S(1)} %get-tuple-element.26.refs_0_, ...), custom_call_target="tpu_custom_call" | custom-call | tf_op jit(solution)/shard_map/step_sent_half/pallas_call | solution.py:382
  21.1 1.3 %step_kept_half.3 = f32[4,2,32,512]{3,2,1,0:T(8,128)S(1)} custom-call(bf16[8192,512]{1,0:T(8,128)(2,1)S(1)} %copy-done, bf16[32,512]{1,0:T(8,128)(2,1)S(1)} %get-tuple-element.28.halves_ref, bf16[4,2,16,512]{3,2,1,0:T(8,128)(2,1)S(1)} %get-tuple-element.29.refs_0_), custom_call_target="tpu_custom_call" | custom-call | tf_op jit(solution)/shard_map/step_kept_half/pallas_call | solution.py:394
  24.2 1.8 %collective-permute-start.2 = (bf16[64,512]{1,0:T(8,128)(2,1)S(1)}, bf16[64,512]{1,0:T(8,128)(2,1)S(1)}, u32[]{:S(2)}, u32[]{:S(2)}) collective-permute-start(bf16[64,512]{1,0:T(8,128)(2,1)S(1)} %bitcast.103), channel_id=1, source_target_pairs={{0,3},{1,2},{2,1},{3,0},{4,7},{5,6},{6,5},{7,4},{8,11},{9,10},{10,... | collective-permute-start | bytes 196616 | tf_op jit(solution)/shard_map/ppermute | solution.py:33
  26.0 2.6 %collective-permute-done.3 = bf16[64,512]{1,0:T(8,128)(2,1)S(1)} collective-permute-done((bf16[64,512]{1,0:T(8,128)(2,1)S(1)}, bf16[64,512]{1,0:T(8,128)(2,1)S(1)}, u32[]{:S(2)}, u32[]{:S(2)}) %collective-permute-start.3) | collective-permute-done | bytes 65568 | tf_op jit(solution)/shard_map/ppermute | solution.py:33
  29.4 5.0 %collective-permute-done.4.refs_1_ = bf16[32,512]{1,0:T(8,128)(2,1)S(1)} collective-permute-done((bf16[32,512]{1,0:T(8,128)(2,1)S(1)}, bf16[32,512]{1,0:T(8,128)(2,1)S(1)}, u32[]{:S(2)}, u32[]{:S(2)}) %collective-permute-start.4) | collective-permute-done | bytes 32800 | tf_op jit(solution)/shard_map/ppermute | solution.py:33
  34.4 1.5 %step_sent_half.4 = (bf16[32,512]{1,0:T(8,128)(2,1)S(1)}, bf16[4,2,16,512]{3,2,1,0:T(8,128)(2,1)S(1)}) custom-call(bf16[8192,512]{1,0:T(8,128)(2,1)S(1)} %copy-done, bf16[256,48]{1,0:T(8,128)(2,1)S(1)} %get-tuple-element.24.route_ref, f32[16,1,512]{2,1,0:T(1,128)S(1)} %all_to_all.10.sums_ref, f32[32,512]{1,0:T(8,128)S(1)} %slice_bitcast_fusion.2.refs_0_, ...), custom_call_target="tpu_custom_call" | custom-call | tf_op jit(solution)/shard_map/step_sent_half/pallas_call | solution.py:382
  37.5 1.6 %collective-permute-start.6 = (bf16[32,512]{1,0:T(8,128)(2,1)S(1)}, bf16[32,512]{1,0:T(8,128)(2,1)S(1)}, u32[]{:S(2)}, u32[]{:S(2)}) collective-permute-start(bf16[32,512]{1,0:T(8,128)(2,1)S(1)} %bitcast.114), channel_id=1, source_target_pairs={{0,5},{1,4},{2,7},{3,6},{4,1},{5,0},{6,3},{7,2},{8,13},{9,12},{10,... | collective-permute-start | bytes 98312 | tf_op jit(solution)/shard_map/ppermute | solution.py:33
  39.0 1.6 %collective-permute-start.7 = (bf16[32,512]{1,0:T(8,128)(2,1)S(1)}, bf16[32,512]{1,0:T(8,128)(2,1)S(1)}, u32[]{:S(2)}, u32[]{:S(2)}) collective-permute-start(bf16[32,512]{1,0:T(8,128)(2,1)S(1)} %bitcast.113), channel_id=1, source_target_pairs={{0,3},{1,2},{2,1},{3,0},{4,7},{5,6},{6,5},{7,4},{8,11},{9,10},{10,... | collective-permute-start | bytes 98312 | tf_op jit(solution)/shard_map/ppermute | solution.py:33
  40.8 1.7 %collective-permute-done.8 = bf16[32,512]{1,0:T(8,128)(2,1)S(1)} collective-permute-done((bf16[32,512]{1,0:T(8,128)(2,1)S(1)}, bf16[32,512]{1,0:T(8,128)(2,1)S(1)}, u32[]{:S(2)}, u32[]{:S(2)}) %collective-permute-start.8) | collective-permute-done | bytes 32800 | tf_op jit(solution)/shard_map/ppermute | solution.py:33
  42.8 5.0 %collective-permute-done.9.refs_1_ = bf16[32,512]{1,0:T(8,128)(2,1)S(1)} collective-permute-done((bf16[32,512]{1,0:T(8,128)(2,1)S(1)}, bf16[32,512]{1,0:T(8,128)(2,1)S(1)}, u32[]{:S(2)}, u32[]{:S(2)}) %collective-permute-start.9) | collective-permute-done | bytes 32800 | tf_op jit(solution)/shard_map/ppermute | solution.py:33
  47.8 1.4 %step_sent_half.5 = (bf16[32,512]{1,0:T(8,128)(2,1)S(1)}, f32[4,2,16,512]{3,2,1,0:T(8,128)S(1)}) custom-call(bf16[8192,512]{1,0:T(8,128)(2,1)S(1)} %copy-done, bf16[256,48]{1,0:T(8,128)(2,1)S(1)} %get-tuple-element.24.route_ref, f32[16,1,512]{2,1,0:T(1,128)S(1)} %all_to_all.10.sums_ref, f32[16,512]{1,0:T(8,128)S(1)} %slice_bitcast_fusion.4.refs_0_, ...), custom_call_target="tpu_custom_call" | custom-call | tf_op jit(solution)/shard_map/step_sent_half/pallas_call | solution.py:382
  49.4 1.3 %step_kept_half.5 = f32[4,2,16,512]{3,2,1,0:T(8,128)S(1)} custom-call(bf16[8192,512]{1,0:T(8,128)(2,1)S(1)} %copy-done, bf16[32,512]{1,0:T(8,128)(2,1)S(1)} %get-tuple-element.33.halves_ref), custom_call_target="tpu_custom_call" | custom-call | tf_op jit(solution)/shard_map/step_kept_half/pallas_call | solution.py:394
  52.1 2.0 %collective-permute-start.13 = (bf16[96,512]{1,0:T(8,128)(2,1)S(1)}, bf16[96,512]{1,0:T(8,128)(2,1)S(1)}, u32[]{:S(2)}, u32[]{:S(2)}) collective-permute-start(bf16[96,512]{1,0:T(8,128)(2,1)S(1)} %get-tuple-element.65), channel_id=1, source_target_pairs={{0,6},{1,7},{2,4},{3,5},{4,2},{5,3},{6,0},{7,1},{8,14},{9,15},{10,... | collective-permute-start | bytes 294920 | tf_op jit(solution)/shard_map/ppermute | solution.py:33
  54.2 1.5 %collective-permute-done.11 = bf16[96,512]{1,0:T(8,128)(2,1)S(1)} collective-permute-done((bf16[96,512]{1,0:T(8,128)(2,1)S(1)}, bf16[96,512]{1,0:T(8,128)(2,1)S(1)}, u32[]{:S(2)}, u32[]{:S(2)}) %collective-permute-start.11) | collective-permute-done | bytes 98336 | tf_op jit(solution)/shard_map/ppermute | solution.py:33
  55.8 3.1 %collective-permute-done.13 = bf16[96,512]{1,0:T(8,128)(2,1)S(1)} collective-permute-done((bf16[96,512]{1,0:T(8,128)(2,1)S(1)}, bf16[96,512]{1,0:T(8,128)(2,1)S(1)}, u32[]{:S(2)}, u32[]{:S(2)}) %collective-permute-start.13) | collective-permute-done | bytes 98336 | tf_op jit(solution)/shard_map/ppermute | solution.py:33
  59.1 1.3 %collective-permute-done.15.far_ref = bf16[4,2,16,512]{3,2,1,0:T(8,128)(2,1)S(1)} collective-permute-done((bf16[4,2,16,512]{3,2,1,0:T(8,128)(2,1)S(1)}, bf16[4,2,16,512]{3,2,1,0:T(8,128)(2,1)S(1)}, u32[]{:S(2)}, u32[]{:S(2)}) %collective-permute-start.15) | collective-permute-done | bytes 131104 | tf_op jit(solution)/shard_map/ppermute | solution.py:33
  60.8 4.8 %collective-permute-done.14.refs_0_ = bf16[64,512]{1,0:T(8,128)(2,1)S(1)} collective-permute-done((bf16[64,512]{1,0:T(8,128)(2,1)S(1)}, bf16[64,512]{1,0:T(8,128)(2,1)S(1)}, u32[]{:S(2)}, u32[]{:S(2)}) %collective-permute-start.14) | collective-permute-done | bytes 65568 | tf_op jit(solution)/shard_map/ppermute | solution.py:33
  66.2 2.7 %collective-permute-start.16 = (f32[2,16,512]{2,1,0:T(8,128)S(1)}, f32[2,16,512]{2,1,0:T(8,128)S(1)}, u32[]{:S(2)}, u32[]{:S(2)}) collective-permute-start(f32[2,16,512]{2,1,0:T(8,128)S(1)} %last_messages.1), channel_id=1, source_target_pairs={{0,5},{1,4},{2,7},{3,6},{4,1},{5,0},{6,3},{7,2},{8,13},{9,12},{10,... | collective-permute-start | bytes 196616 | tf_op jit(solution)/shard_map/ppermute | solution.py:33
  68.8 2.4 %collective-permute-done.18 = f32[2,16,512]{2,1,0:T(8,128)S(1)} collective-permute-done((f32[2,16,512]{2,1,0:T(8,128)S(1)}, f32[2,16,512]{2,1,0:T(8,128)S(1)}, u32[]{:S(2)}, u32[]{:S(2)}) %collective-permute-start.18) | collective-permute-done | bytes 65568 | tf_op jit(solution)/shard_map/ppermute | solution.py:33
  74.8 3.5 %all-to-all-start.1 = ((f32[16,2,16]{2,1,0:T(2,128)}), f32[16,2,16]{2,1,0:T(2,128)S(1)}, u32[]{:S(2)}, u32[]{:S(2)}) async-start(f32[16,2,16]{2,1,0:T(2,128)} %broadcast_in_dim.7), calls=%async_computation.1 | async-start | bytes 32768 | tf_op jit(solution)/shard_map/all_to_all | solution.py:20
  79.0 5.8 %all-to-all-done.1 = f32[16,2,16]{2,1,0:T(2,128)S(1)} async-done(((f32[16,2,16]{2,1,0:T(2,128)}), f32[16,2,16]{2,1,0:T(2,128)S(1)}, u32[]{:S(2)}, u32[]{:S(2)}) %all-to-all-start.1) | async-done | bytes 2080 | tf_op jit(solution)/shard_map/all_to_all | solution.py:20
  (79 shorter events, 13.1 us)
Async XLA Ops:
  0.6 19.0 %copy-start = (bf16[8192,512]{1,0:T(8,128)(2,1)S(1)}, bf16[8192,512]{1,0:T(8,128)(2,1)}, u32[]{:S(2)}) copy-start(bf16[8192,512]{1,0:T(8,128)(2,1)} %transition_ref.11) | copy-start | bytes 25165828
  21.1 1.6 %collective-permute-start = (bf16[4,2,32,512]{3,2,1,0:T(8,128)(2,1)S(1)}, bf16[4,2,32,512]{3,2,1,0:T(8,128)(2,1)S(1)}, u32[]{:S(2)}, u32[]{:S(2)}) collective-permute-start(bf16[4,2,32,512]{3,2,1,0:T(8,128)(2,1)S(1)} %get-tuple-element.30), channel_id=1, source_target_pairs={{0,1},{1,0},{2,3},{3,2},{4,5},{5,4},{6,7},{7,6},{8,9},{9,8},{10,11... | collective-permute-start | bytes 786440 | tf_op jit(solution)/shard_map/ppermute | solution.py:33
  22.8 5.9 %collective-permute-start.3 = (bf16[64,512]{1,0:T(8,128)(2,1)S(1)}, bf16[64,512]{1,0:T(8,128)(2,1)S(1)}, u32[]{:S(2)}, u32[]{:S(2)}) collective-permute-start(bf16[64,512]{1,0:T(8,128)(2,1)S(1)} %bitcast.105), channel_id=1, source_target_pairs={{0,6},{1,7},{2,4},{3,5},{4,2},{5,3},{6,0},{7,1},{8,14},{9,15},{10,... | collective-permute-start | bytes 196616 | tf_op jit(solution)/shard_map/ppermute | solution.py:33
  23.2 5.4 %collective-permute-start.1 = (bf16[64,512]{1,0:T(8,128)(2,1)S(1)}, bf16[64,512]{1,0:T(8,128)(2,1)S(1)}, u32[]{:S(2)}, u32[]{:S(2)}) collective-permute-start(bf16[64,512]{1,0:T(8,128)(2,1)S(1)} %bitcast.104), channel_id=1, source_target_pairs={{0,5},{1,4},{2,7},{3,6},{4,1},{5,0},{6,3},{7,2},{8,13},{9,12},{10,... | collective-permute-start | bytes 196616 | tf_op jit(solution)/shard_map/ppermute | solution.py:33
  24.2 4.9 %collective-permute-start.2 = (bf16[64,512]{1,0:T(8,128)(2,1)S(1)}, bf16[64,512]{1,0:T(8,128)(2,1)S(1)}, u32[]{:S(2)}, u32[]{:S(2)}) collective-permute-start(bf16[64,512]{1,0:T(8,128)(2,1)S(1)} %bitcast.103), channel_id=1, source_target_pairs={{0,3},{1,2},{2,1},{3,0},{4,7},{5,6},{6,5},{7,4},{8,11},{9,10},{10,... | collective-permute-start | bytes 196616 | tf_op jit(solution)/shard_map/ppermute | solution.py:33
  29.2 5.2 %collective-permute-start.4 = (bf16[32,512]{1,0:T(8,128)(2,1)S(1)}, bf16[32,512]{1,0:T(8,128)(2,1)S(1)}, u32[]{:S(2)}, u32[]{:S(2)}) collective-permute-start(bf16[32,512]{1,0:T(8,128)(2,1)S(1)} %fusion.14), channel_id=1, source_target_pairs={{0,9},{1,8},{2,11},{3,10},{4,13},{5,12},{6,15},{7,14},{8,1},{9,0},... | collective-permute-start | bytes 98312 | tf_op jit(solution)/shard_map/ppermute | solution.py:33
  35.8 1.4 %collective-permute-start.5 = (bf16[4,2,16,512]{3,2,1,0:T(8,128)(2,1)S(1)}, bf16[4,2,16,512]{3,2,1,0:T(8,128)(2,1)S(1)}, u32[]{:S(2)}, u32[]{:S(2)}) collective-permute-start(bf16[4,2,16,512]{3,2,1,0:T(8,128)(2,1)S(1)} %get-tuple-element.32), channel_id=1, source_target_pairs={{0,1},{1,0},{2,3},{3,2},{4,5},{5,4},{6,7},{7,6},{8,9},{9,8},{10,11... | collective-permute-start | bytes 393224 | tf_op jit(solution)/shard_map/ppermute | solution.py:33
  37.3 5.1 %collective-permute-start.8 = (bf16[32,512]{1,0:T(8,128)(2,1)S(1)}, bf16[32,512]{1,0:T(8,128)(2,1)S(1)}, u32[]{:S(2)}, u32[]{:S(2)}) collective-permute-start(bf16[32,512]{1,0:T(8,128)(2,1)S(1)} %bitcast.115), channel_id=1, source_target_pairs={{0,6},{1,7},{2,4},{3,5},{4,2},{5,3},{6,0},{7,1},{8,14},{9,15},{10,... | collective-permute-start | bytes 98312 | tf_op jit(solution)/shard_map/ppermute | solution.py:33
  37.5 5.0 %collective-permute-start.6 = (bf16[32,512]{1,0:T(8,128)(2,1)S(1)}, bf16[32,512]{1,0:T(8,128)(2,1)S(1)}, u32[]{:S(2)}, u32[]{:S(2)}) collective-permute-start(bf16[32,512]{1,0:T(8,128)(2,1)S(1)} %bitcast.114), channel_id=1, source_target_pairs={{0,5},{1,4},{2,7},{3,6},{4,1},{5,0},{6,3},{7,2},{8,13},{9,12},{10,... | collective-permute-start | bytes 98312 | tf_op jit(solution)/shard_map/ppermute | solution.py:33
  39.0 3.6 %collective-permute-start.7 = (bf16[32,512]{1,0:T(8,128)(2,1)S(1)}, bf16[32,512]{1,0:T(8,128)(2,1)S(1)}, u32[]{:S(2)}, u32[]{:S(2)}) collective-permute-start(bf16[32,512]{1,0:T(8,128)(2,1)S(1)} %bitcast.113), channel_id=1, source_target_pairs={{0,3},{1,2},{2,1},{3,0},{4,7},{5,6},{6,5},{7,4},{8,11},{9,10},{10,... | collective-permute-start | bytes 98312 | tf_op jit(solution)/shard_map/ppermute | solution.py:33
  42.7 5.1 %collective-permute-start.9 = (bf16[32,512]{1,0:T(8,128)(2,1)S(1)}, bf16[32,512]{1,0:T(8,128)(2,1)S(1)}, u32[]{:S(2)}, u32[]{:S(2)}) collective-permute-start(bf16[32,512]{1,0:T(8,128)(2,1)S(1)} %pad_maximum_fusion.9), channel_id=1, source_target_pairs={{0,9},{1,8},{2,11},{3,10},{4,13},{5,12},{6,15},{7,14},{8,1},{9,0},... | collective-permute-start | bytes 98312 | tf_op jit(solution)/shard_map/ppermute | solution.py:33
  49.2 22.4 %copy-start.2 = (bf16[8192,256]{1,0:T(8,128)(2,1)S(1)}, bf16[8192,256]{1,0:T(8,128)(2,1)}, u32[]{:S(2)}) copy-start(bf16[8192,256]{1,0:T(8,128)(2,1)} %emission_ref.7) | copy-start | bytes 12582916
  49.2 1.6 %collective-permute-start.10 = (f32[4,2,16,512]{3,2,1,0:T(8,128)S(1)}, f32[4,2,16,512]{3,2,1,0:T(8,128)S(1)}, u32[]{:S(2)}, u32[]{:S(2)}) collective-permute-start(f32[4,2,16,512]{3,2,1,0:T(8,128)S(1)} %get-tuple-element.34), channel_id=1, source_target_pairs={{0,1},{1,0},{2,3},{3,2},{4,5},{5,4},{6,7},{7,6},{8,9},{9,8},{10,11... | collective-permute-start | bytes 786440 | tf_op jit(solution)/shard_map/ppermute | solution.py:33
  49.4 23.7 %copy-start.4 = (bf16[16,256]{1,0:T(8,128)(2,1)S(1)}, bf16[16,256]{1,0:T(8,128)(2,1)}, u32[]{:S(2)}) copy-start(bf16[16,256]{1,0:T(8,128)(2,1)} %logits_ref.1) | copy-start | bytes 24580
  50.9 4.8 %collective-permute-start.11 = (bf16[96,512]{1,0:T(8,128)(2,1)S(1)}, bf16[96,512]{1,0:T(8,128)(2,1)S(1)}, u32[]{:S(2)}, u32[]{:S(2)}) collective-permute-start(bf16[96,512]{1,0:T(8,128)(2,1)S(1)} %get-tuple-element.63), channel_id=1, source_target_pairs={{0,5},{1,4},{2,7},{3,6},{4,1},{5,0},{6,3},{7,2},{8,13},{9,12},{10,... | collective-permute-start | bytes 294920 | tf_op jit(solution)/shard_map/ppermute | solution.py:33
  51.0 4.8 %collective-permute-start.12 = (bf16[96,512]{1,0:T(8,128)(2,1)S(1)}, bf16[96,512]{1,0:T(8,128)(2,1)S(1)}, u32[]{:S(2)}, u32[]{:S(2)}) collective-permute-start(bf16[96,512]{1,0:T(8,128)(2,1)S(1)} %get-tuple-element.64), channel_id=1, source_target_pairs={{0,3},{1,2},{2,1},{3,0},{4,7},{5,6},{6,5},{7,4},{8,11},{9,10},{10,... | collective-permute-start | bytes 294920 | tf_op jit(solution)/shard_map/ppermute | solution.py:33
  52.1 6.7 %collective-permute-start.13 = (bf16[96,512]{1,0:T(8,128)(2,1)S(1)}, bf16[96,512]{1,0:T(8,128)(2,1)S(1)}, u32[]{:S(2)}, u32[]{:S(2)}) collective-permute-start(bf16[96,512]{1,0:T(8,128)(2,1)S(1)} %get-tuple-element.65), channel_id=1, source_target_pairs={{0,6},{1,7},{2,4},{3,5},{4,2},{5,3},{6,0},{7,1},{8,14},{9,15},{10,... | collective-permute-start | bytes 294920 | tf_op jit(solution)/shard_map/ppermute | solution.py:33
  58.9 6.7 %collective-permute-start.14 = (bf16[64,512]{1,0:T(8,128)(2,1)S(1)}, bf16[64,512]{1,0:T(8,128)(2,1)S(1)}, u32[]{:S(2)}, u32[]{:S(2)}) collective-permute-start(bf16[64,512]{1,0:T(8,128)(2,1)S(1)} %pad_maximum_fusion.8), channel_id=1, source_target_pairs={{0,9},{1,8},{2,11},{3,10},{4,13},{5,12},{6,15},{7,14},{8,1},{9,0},... | collective-permute-start | bytes 196616 | tf_op jit(solution)/shard_map/ppermute | solution.py:33
  59.0 1.4 %collective-permute-start.15 = (bf16[4,2,16,512]{3,2,1,0:T(8,128)(2,1)S(1)}, bf16[4,2,16,512]{3,2,1,0:T(8,128)(2,1)S(1)}, u32[]{:S(2)}, u32[]{:S(2)}) collective-permute-start(bf16[4,2,16,512]{3,2,1,0:T(8,128)(2,1)S(1)} %pad_maximum_fusion.7.near_ref), channel_id=1, source_target_pairs={{0,1},{1,0},{2,3},{3,2},{4,5},{5,4},{6,7},{7,6},{8,9},{9,8},{10,11... | collective-permute-start | bytes 393224 | tf_op jit(solution)/shard_map/ppermute | solution.py:33
  65.6 5.7 %collective-permute-start.18 = (f32[2,16,512]{2,1,0:T(8,128)S(1)}, f32[2,16,512]{2,1,0:T(8,128)S(1)}, u32[]{:S(2)}, u32[]{:S(2)}) collective-permute-start(f32[2,16,512]{2,1,0:T(8,128)S(1)} %last_messages.1), channel_id=1, source_target_pairs={{0,6},{1,7},{2,4},{3,5},{4,2},{5,3},{6,0},{7,1},{8,14},{9,15},{10,... | collective-permute-start | bytes 196616 | tf_op jit(solution)/shard_map/ppermute | solution.py:33
  65.7 5.6 %collective-permute-start.17 = (f32[2,16,512]{2,1,0:T(8,128)S(1)}, f32[2,16,512]{2,1,0:T(8,128)S(1)}, u32[]{:S(2)}, u32[]{:S(2)}) collective-permute-start(f32[2,16,512]{2,1,0:T(8,128)S(1)} %last_messages.1), channel_id=1, source_target_pairs={{0,3},{1,2},{2,1},{3,0},{4,7},{5,6},{6,5},{7,4},{8,11},{9,10},{10,... | collective-permute-start | bytes 196616 | tf_op jit(solution)/shard_map/ppermute | solution.py:33
  66.2 5.3 %collective-permute-start.16 = (f32[2,16,512]{2,1,0:T(8,128)S(1)}, f32[2,16,512]{2,1,0:T(8,128)S(1)}, u32[]{:S(2)}, u32[]{:S(2)}) collective-permute-start(f32[2,16,512]{2,1,0:T(8,128)S(1)} %last_messages.1), channel_id=1, source_target_pairs={{0,5},{1,4},{2,7},{3,6},{4,1},{5,0},{6,3},{7,2},{8,13},{9,12},{10,... | collective-permute-start | bytes 196616 | tf_op jit(solution)/shard_map/ppermute | solution.py:33
  71.5 1.6 %collective-permute-start.19 = (f32[4,2,16,512]{3,2,1,0:T(8,128)S(1)}, f32[4,2,16,512]{3,2,1,0:T(8,128)S(1)}, u32[]{:S(2)}, u32[]{:S(2)}) collective-permute-start(f32[4,2,16,512]{3,2,1,0:T(8,128)S(1)} %pad_maximum_fusion.parts_ref), channel_id=1, source_target_pairs={{0,1},{1,0},{2,3},{3,2},{4,5},{5,4},{6,7},{7,6},{8,9},{9,8},{10,11... | collective-permute-start | bytes 786440 | tf_op jit(solution)/shard_map/ppermute | solution.py:33
  74.8 10.0 %all-to-all-start.1 = ((f32[16,2,16]{2,1,0:T(2,128)}), f32[16,2,16]{2,1,0:T(2,128)S(1)}, u32[]{:S(2)}, u32[]{:S(2)}) async-start(f32[16,2,16]{2,1,0:T(2,128)} %broadcast_in_dim.7), calls=%async_computation.1 | async-start | bytes 32768 | tf_op jit(solution)/shard_map/all_to_all | solution.py:20
  (2 other events, 13.6 us)

commit v5 on v4

--- a/solution.py
+++ b/solution.py
@@ -120,11 +120,6 @@
         if h:
             blocks.append(swap(pack(near[h], False, extra), offset, devices))
     return blocks
-
-
-def gather_square(far, devices, count):
-    near = jnp.stack([far] + [swap(far, offset, devices) for offset in square_partners(count)[1:]])
-    return near, swap(near, 1, devices)
 
 
 def column_of(scalars_ref, shape):
@@ -402,12 +397,14 @@
     return kept, received
 
 
-def weigh_half(emission_ref, forward_ref, chooser, parts_ref, count, first):
+def weigh_blocks(emission_ref, forward_ref, chooser, parts_ref, count, first, squares):
     rows = emission_ref.shape[0] >> count
     prompts = chooser.shape[0]
     weights = jnp.zeros((prompts, emission_ref.shape[1]), jnp.float32)
-    for order, (place, partner) in enumerate(half_places(count, first)):
-        pieces = jnp.concatenate(split_three(parts_ref[place]), axis=0)
+    for order, ((q, h), partner) in enumerate(half_places(count, first)):
+        if q not in squares:
+            continue
+        pieces = jnp.concatenate(split_three(parts_ref[squares.index(q), h]), axis=0)
         chosen = jnp.dot(chooser, pieces, preferred_element_type=jnp.float32)
         block = order + (first << (count - 1))
         forward = forward_ref[pl.ds(block * prompts, prompts)].astype(jnp.float32)
@@ -417,15 +414,25 @@
     return weights
 
 
-def near_kernel(count, emission_ref, forward_ref, chooser_ref, parts_ref, out_ref):
-    out_ref[...] = weigh_half(emission_ref, forward_ref, chooser_ref[...], parts_ref, count, 0)
-
-
-def far_kernel(count, emission_ref, forward_ref, chooser_ref, logits_ref, near_ref, parts_ref, raised_ref, pair_ref):
+def weigh_kernel(count, groups, emission_ref, forward_ref, chooser_ref, *refs):
+    parts, out_ref = refs[:-1], refs[-1]
+    chooser = chooser_ref[...]
+    out_ref[...] = functools.reduce(jnp.add, [
+        weigh_blocks(emission_ref, forward_ref, chooser, part_ref, count, first, squares)
+        for part_ref, (first, squares) in zip(parts, groups)
+    ])
+
+
+def last_weigh_kernel(
+    count, first, squares, emission_ref, forward_ref, chooser_ref, logits_ref, before_ref,
+    parts_ref, raised_ref, pair_ref,
+):
     chooser = chooser_ref[...]
     logits = logits_ref[...].astype(jnp.float32)
     top = jnp.max(logits, axis=1, keepdims=True)
-    weights = near_ref[...] + weigh_half(emission_ref, forward_ref, chooser, parts_ref, count, 1)
+    weights = weigh_blocks(
+        emission_ref, forward_ref, chooser, parts_ref, count, first, squares
+    ) + before_ref[...]
     allowed = jnp.sum(chooser.astype(jnp.float32), axis=1, keepdims=True) > 0
     raised = jnp.where(allowed, jnp.exp(logits - top) * weights, 0.0)
     raised_ref[...] = raised
@@ -434,17 +441,27 @@
     pair_ref[...] = jnp.where(lane == 0, top, total)
 
 
-def weigh(emission, forward, chooser, logits, near, far, count):
-    half = pl.pallas_call(
-        functools.partial(near_kernel, count),
-        out_shape=pltpu.VMEM(logits.shape, jnp.float32),
-        in_specs=[VMEM] * 4,
-        out_specs=VMEM,
-        compiler_params=PARAMS,
-        name="weigh_near",
-    )(emission, forward, chooser, near)
+def weigh(emission, forward, chooser, logits, far, devices, count):
+    early, late = (0, 1), (2, 3)
+    offsets = square_partners(count)
+    arrived = [far] + [swap(far, offset, devices) for offset in offsets[1:]]
+    near_early = jnp.stack([arrived[q] for q in early])
+    near_late = jnp.stack([arrived[q] for q in late])
+    far_early, far_late = swap(near_early, 1, devices), swap(near_late, 1, devices)
+
+    def add(parts, groups):
+        return pl.pallas_call(
+            functools.partial(weigh_kernel, count, groups),
+            out_shape=pltpu.VMEM(logits.shape, jnp.float32),
+            in_specs=[VMEM] * (3 + len(parts)),
+            out_specs=VMEM,
+            compiler_params=PARAMS,
+            name="weigh_tokens",
+        )(emission, forward, chooser, *parts)
+
+    weights = add((near_early, far_early, near_late), ((0, early), (1, early), (0, late)))
     return pl.pallas_call(
-        functools.partial(far_kernel, count),
+        functools.partial(last_weigh_kernel, count, 1, late),
         out_shape=[
             pltpu.VMEM(logits.shape, jnp.float32),
             pltpu.VMEM((logits.shape[0], 128), jnp.float32),
@@ -452,8 +469,8 @@
         in_specs=[VMEM] * 6,
         out_specs=[VMEM] * 2,
         compiler_params=PARAMS,
-        name="weigh_far",
-    )(emission, forward, chooser, logits, half, far)
+        name="weigh_last",
+    )(emission, forward, chooser, logits, weights, far_late)
 
 
 def normalise(raised, pair, devices):
@@ -525,10 +542,8 @@
         forward = jnp.stack(extras).reshape(4, devices // 8, devices, own_rows)
         forward = order_forward(forward, swap(forward, 1, devices), count)
         messages = last_sum(near, forward, devices, count)
-        near, far = gather_square(messages, devices, count)
-        messages = messages[0]
-        raised, pair = weigh(emission, forward, chooser, lm_logits, near, far, count)
-        return messages.T, normalise(raised, pair, devices)
+        raised, pair = weigh(emission, forward, chooser, lm_logits, messages, devices, count)
+        return messages[0].T, normalise(raised, pair, devices)
     state_ids = jnp.arange(states, dtype=jnp.int32)
     block_ids = jnp.arange(devices, dtype=jnp.int32)
     allowed = jnp.any(allow_list[:, :, None] == block_ids, axis=1)

time: 86 us -> 87 us (1.012)
  waiting for transfers between devices: 34.9 us -> 36 us
    ppermute x20 -> x21, waiting for transfers between devices: 29 us -> 30.1 us  [swap(): return lax.ppermute(block, 'vocab', pairs)]
    ppermute x20 -> x21, starting transfers between devices: 14 us -> 14 us  [swap(): return lax.ppermute(block, 'vocab', pairs)]
  transfers between devices with their start and end apart: 21 -> 22, of which waited for: 18 -> 17; matrix products, arithmetic and copies ran while one was open for 1% -> 1% of each run, Pallas kernels for 6% -> 7%
where the time goes in v5:
time: 87 us; the launch traced here: 86.8 us
  waiting for transfers between devices  36 us (41%)
  starting transfers between devices  17.4 us (20%)
  blocking collectives  13.8 us (16%)
  Pallas kernels  13.5 us (16%)
  local copies, waits for them, and re-layouts  3.86 us (4%)
  other arithmetic  1.27 us (1%)
  between operations  0.93 us (1%)
    ppermute x21, waiting for transfers between devices, swap(): return lax.ppermute(block, 'vocab', pairs)  30.1 us
    ppermute x21, starting transfers between devices, swap(): return lax.ppermute(block, 'vocab', pairs)  14 us
    all_to_all x1, blocking collectives, exchange(): lax.all_to_all(blocks, 'vocab', split_axis=0, concat_axis=0, tiled=True)  13.8 us
    all_to_all x1, waiting for transfers between devices, exchange(): lax.all_to_all(blocks, 'vocab', split_axis=0, concat_axis=0, tiled=True)  5.84 us
    pallas_call x3, Pallas kernels, step(): pl.pallas_call(functools.partial(send_kernel, count, len(parts)), out_sha...  4.34 us
    pallas_call x3, Pallas kernels, step(): pl.pallas_call(functools.partial(keep_kernel, count), out_shape=pltpu.VME...  3.88 us
    all_to_all x1, starting transfers between devices, exchange(): lax.all_to_all(blocks, 'vocab', split_axis=0, concat_axis=0, tiled=True)  3.49 us
    pallas_call x1, Pallas kernels, first_products(): pl.pallas_call(functools.partial(products_kernel, count), out_shape=[jax....  2.38 us
  transfers between devices with their start and end apart: 22, of which 17 were waited for; matrix products, arithmetic and copies ran while one was open for 1% of the time, Pallas kernels for 7%

profile of v5, /device:TPU:0, one launch (start us, length us, event | category | flops | bytes accessed | tf_op | source)
XLA Modules:
  0.0 86.8 jit_solution(1678466019892853971)
XLA Ops:
  0.7 2.3 %copy-done.1 = bf16[8192,256]{1,0:T(8,128)(2,1)S(1)} copy-done((bf16[8192,256]{1,0:T(8,128)(2,1)S(1)}, bf16[8192,256]{1,0:T(8,128)(2,1)}, u32[]{:S(2)}) %copy-start.1) | copy-done | bytes 4194328
  3.0 2.4 %first_products.1 = (f32[16,1,512]{2,1,0:T(1,128)S(1)}, bf16[4,2,16,512]{3,2,1,0:T(8,128)(2,1)S(1)}, bf16[4,2,16,512]{3,2,1,0:T(8,128)(2,1)S(1)}, s32[1,16]{1,0:...) custom-call(s32[16]{0:T(128)} %token_hbm.1, s32[1,16]{1,0:T(1,128)} %bitcast.118, ...), custom_call_target="tpu_custom_call" | custom-call | tf_op jit(solution)/shard_map/first_products/pallas_call | solution.py:228
  5.8 13.8 %all_to_all.10.sums_ref = f32[16,1,512]{2,1,0:T(1,128)S(1)} all-to-all(f32[16,1,512]{2,1,0:T(1,128)S(1)} %get-tuple-element.25), channel_id=1, replica_groups=mesh['parts'=2,'vocab'=16] {'vocab'}, dimensions={0} | all-to-all | bytes 65536 | tf_op jit(solution)/shard_map/all_to_all | solution.py:20
  19.6 1.5 %step_sent_half.3 = (bf16[32,512]{1,0:T(8,128)(2,1)S(1)}, bf16[4,2,32,512]{3,2,1,0:T(8,128)(2,1)S(1)}) custom-call(bf16[8192,512]{1,0:T(8,128)(2,1)S(1)} %copy-done, bf16[256,48]{1,0:T(8,128)(2,1)S(1)} %get-tuple-element.24.route_ref, f32[16,1,512]{2,1,0:T(1,128)S(1)} %all_to_all.10.sums_ref, f32[16,512]{1,0:T(8,128)S(1)} %get-tuple-element.26.refs_0_, ...), custom_call_target="tpu_custom_call" | custom-call | tf_op jit(solution)/shard_map/step_sent_half/pallas_call | solution.py:377
  21.1 1.3 %step_kept_half.3 = f32[4,2,32,512]{3,2,1,0:T(8,128)S(1)} custom-call(bf16[8192,512]{1,0:T(8,128)(2,1)S(1)} %copy-done, bf16[32,512]{1,0:T(8,128)(2,1)S(1)} %get-tuple-element.28.halves_ref, bf16[4,2,16,512]{3,2,1,0:T(8,128)(2,1)S(1)} %get-tuple-element.29.refs_0_), custom_call_target="tpu_custom_call" | custom-call | tf_op jit(solution)/shard_map/step_kept_half/pallas_call | solution.py:389
  24.2 1.8 %collective-permute-start.2 = (bf16[64,512]{1,0:T(8,128)(2,1)S(1)}, bf16[64,512]{1,0:T(8,128)(2,1)S(1)}, u32[]{:S(2)}, u32[]{:S(2)}) collective-permute-start(bf16[64,512]{1,0:T(8,128)(2,1)S(1)} %bitcast.103), channel_id=1, source_target_pairs={{0,3},{1,2},{2,1},{3,0},{4,7},{5,6},{6,5},{7,4},{8,11},{9,10},{10,... | collective-permute-start | bytes 196616 | tf_op jit(solution)/shard_map/ppermute | solution.py:33
  26.0 2.6 %collective-permute-done.3 = bf16[64,512]{1,0:T(8,128)(2,1)S(1)} collective-permute-done((bf16[64,512]{1,0:T(8,128)(2,1)S(1)}, bf16[64,512]{1,0:T(8,128)(2,1)S(1)}, u32[]{:S(2)}, u32[]{:S(2)}) %collective-permute-start.3) | collective-permute-done | bytes 65568 | tf_op jit(solution)/shard_map/ppermute | solution.py:33
  29.4 5.0 %collective-permute-done.4.refs_1_ = bf16[32,512]{1,0:T(8,128)(2,1)S(1)} collective-permute-done((bf16[32,512]{1,0:T(8,128)(2,1)S(1)}, bf16[32,512]{1,0:T(8,128)(2,1)S(1)}, u32[]{:S(2)}, u32[]{:S(2)}) %collective-permute-start.4) | collective-permute-done | bytes 32800 | tf_op jit(solution)/shard_map/ppermute | solution.py:33
  34.4 1.5 %step_sent_half.4 = (bf16[32,512]{1,0:T(8,128)(2,1)S(1)}, bf16[4,2,16,512]{3,2,1,0:T(8,128)(2,1)S(1)}) custom-call(bf16[8192,512]{1,0:T(8,128)(2,1)S(1)} %copy-done, bf16[256,48]{1,0:T(8,128)(2,1)S(1)} %get-tuple-element.24.route_ref, f32[16,1,512]{2,1,0:T(1,128)S(1)} %all_to_all.10.sums_ref, f32[32,512]{1,0:T(8,128)S(1)} %slice_bitcast_fusion.2.refs_0_, ...), custom_call_target="tpu_custom_call" | custom-call | tf_op jit(solution)/shard_map/step_sent_half/pallas_call | solution.py:377
  37.5 1.5 %collective-permute-start.6 = (bf16[32,512]{1,0:T(8,128)(2,1)S(1)}, bf16[32,512]{1,0:T(8,128)(2,1)S(1)}, u32[]{:S(2)}, u32[]{:S(2)}) collective-permute-start(bf16[32,512]{1,0:T(8,128)(2,1)S(1)} %bitcast.114), channel_id=1, source_target_pairs={{0,5},{1,4},{2,7},{3,6},{4,1},{5,0},{6,3},{7,2},{8,13},{9,12},{10,... | collective-permute-start | bytes 98312 | tf_op jit(solution)/shard_map/ppermute | solution.py:33
  39.0 1.6 %collective-permute-start.7 = (bf16[32,512]{1,0:T(8,128)(2,1)S(1)}, bf16[32,512]{1,0:T(8,128)(2,1)S(1)}, u32[]{:S(2)}, u32[]{:S(2)}) collective-permute-start(bf16[32,512]{1,0:T(8,128)(2,1)S(1)} %bitcast.113), channel_id=1, source_target_pairs={{0,3},{1,2},{2,1},{3,0},{4,7},{5,6},{6,5},{7,4},{8,11},{9,10},{10,... | collective-permute-start | bytes 98312 | tf_op jit(solution)/shard_map/ppermute | solution.py:33
  40.8 1.7 %collective-permute-done.8 = bf16[32,512]{1,0:T(8,128)(2,1)S(1)} collective-permute-done((bf16[32,512]{1,0:T(8,128)(2,1)S(1)}, bf16[32,512]{1,0:T(8,128)(2,1)S(1)}, u32[]{:S(2)}, u32[]{:S(2)}) %collective-permute-start.8) | collective-permute-done | bytes 32800 | tf_op jit(solution)/shard_map/ppermute | solution.py:33
  42.8 4.9 %collective-permute-done.9.refs_1_ = bf16[32,512]{1,0:T(8,128)(2,1)S(1)} collective-permute-done((bf16[32,512]{1,0:T(8,128)(2,1)S(1)}, bf16[32,512]{1,0:T(8,128)(2,1)S(1)}, u32[]{:S(2)}, u32[]{:S(2)}) %collective-permute-start.9) | collective-permute-done | bytes 32800 | tf_op jit(solution)/shard_map/ppermute | solution.py:33
  47.7 1.4 %step_sent_half.5 = (bf16[32,512]{1,0:T(8,128)(2,1)S(1)}, f32[4,2,16,512]{3,2,1,0:T(8,128)S(1)}) custom-call(bf16[8192,512]{1,0:T(8,128)(2,1)S(1)} %copy-done, bf16[256,48]{1,0:T(8,128)(2,1)S(1)} %get-tuple-element.24.route_ref, f32[16,1,512]{2,1,0:T(1,128)S(1)} %all_to_all.10.sums_ref, f32[16,512]{1,0:T(8,128)S(1)} %slice_bitcast_fusion.4.refs_0_, ...), custom_call_target="tpu_custom_call" | custom-call | tf_op jit(solution)/shard_map/step_sent_half/pallas_call | solution.py:377
  52.1 1.9 %collective-permute-start.13 = (bf16[96,512]{1,0:T(8,128)(2,1)S(1)}, bf16[96,512]{1,0:T(8,128)(2,1)S(1)}, u32[]{:S(2)}, u32[]{:S(2)}) collective-permute-start(bf16[96,512]{1,0:T(8,128)(2,1)S(1)} %get-tuple-element.65), channel_id=1, source_target_pairs={{0,6},{1,7},{2,4},{3,5},{4,2},{5,3},{6,0},{7,1},{8,14},{9,15},{10,... | collective-permute-start | bytes 294920 | tf_op jit(solution)/shard_map/ppermute | solution.py:33
  54.1 1.5 %collective-permute-done.11 = bf16[96,512]{1,0:T(8,128)(2,1)S(1)} collective-permute-done((bf16[96,512]{1,0:T(8,128)(2,1)S(1)}, bf16[96,512]{1,0:T(8,128)(2,1)S(1)}, u32[]{:S(2)}, u32[]{:S(2)}) %collective-permute-start.11) | collective-permute-done | bytes 98336 | tf_op jit(solution)/shard_map/ppermute | solution.py:33
  55.7 3.2 %collective-permute-done.13 = bf16[96,512]{1,0:T(8,128)(2,1)S(1)} collective-permute-done((bf16[96,512]{1,0:T(8,128)(2,1)S(1)}, bf16[96,512]{1,0:T(8,128)(2,1)S(1)}, u32[]{:S(2)}, u32[]{:S(2)}) %collective-permute-start.13) | collective-permute-done | bytes 98336 | tf_op jit(solution)/shard_map/ppermute | solution.py:33
  59.1 1.3 %collective-permute-done.15.far_ref = bf16[4,2,16,512]{3,2,1,0:T(8,128)(2,1)S(1)} collective-permute-done((bf16[4,2,16,512]{3,2,1,0:T(8,128)(2,1)S(1)}, bf16[4,2,16,512]{3,2,1,0:T(8,128)(2,1)S(1)}, u32[]{:S(2)}, u32[]{:S(2)}) %collective-permute-start.15) | collective-permute-done | bytes 131104 | tf_op jit(solution)/shard_map/ppermute | solution.py:33
  60.8 4.8 %collective-permute-done.14.refs_0_ = bf16[64,512]{1,0:T(8,128)(2,1)S(1)} collective-permute-done((bf16[64,512]{1,0:T(8,128)(2,1)S(1)}, bf16[64,512]{1,0:T(8,128)(2,1)S(1)}, u32[]{:S(2)}, u32[]{:S(2)}) %collective-permute-start.14) | collective-permute-done | bytes 65568 | tf_op jit(solution)/shard_map/ppermute | solution.py:33
  65.6 1.8 %collective-permute-start.19 = (f32[2,16,512]{2,1,0:T(8,128)S(1)}, f32[2,16,512]{2,1,0:T(8,128)S(1)}, u32[]{:S(2)}, u32[]{:S(2)}) collective-permute-start(f32[2,16,512]{2,1,0:T(8,128)S(1)} %last_messages.1), channel_id=1, source_target_pairs={{0,6},{1,7},{2,4},{3,5},{4,2},{5,3},{6,0},{7,1},{8,14},{9,15},{10,... | collective-permute-start | bytes 196616 | tf_op jit(solution)/shard_map/ppermute | solution.py:33
  70.1 1.6 %collective-permute-done.19 = f32[2,16,512]{2,1,0:T(8,128)S(1)} collective-permute-done((f32[2,16,512]{2,1,0:T(8,128)S(1)}, f32[2,16,512]{2,1,0:T(8,128)S(1)}, u32[]{:S(2)}, u32[]{:S(2)}) %collective-permute-start.19) | collective-permute-done | bytes 65568 | tf_op jit(solution)/shard_map/ppermute | solution.py:33
  73.2 1.3 %weigh_tokens.1.before_ref = f32[16,256]{1,0:T(8,128)S(1)} custom-call(bf16[8192,256]{1,0:T(8,128)(2,1)S(1)} %copy-done.2, bf16[256,512]{1,0:T(8,128)(2,1)S(1)} %order_forward.1.refs_1_.forward_ref, bf16[16,48]{1,0:T(8,128)(2,1)S(1)} %get-tuple-element.35.chooser_ref, f32[2,2,16,512]{3,2,1,0:T(8,128)S(1)} %pad_maximum_fusion.7.refs_0_, ...), custom_call_target="tpu_custom_call" | custom-call | tf_op jit(solution)/shard_map/weigh_tokens/pallas_call | solution.py:453
  75.9 3.5 %all-to-all-start.1 = ((f32[16,2,16]{2,1,0:T(2,128)}), f32[16,2,16]{2,1,0:T(2,128)S(1)}, u32[]{:S(2)}, u32[]{:S(2)}) async-start(f32[16,2,16]{2,1,0:T(2,128)} %broadcast_in_dim.7), calls=%async_computation.1 | async-start | bytes 32768 | tf_op jit(solution)/shard_map/all_to_all | solution.py:20
  80.0 5.8 %all-to-all-done.1 = f32[16,2,16]{2,1,0:T(2,128)S(1)} async-done(((f32[16,2,16]{2,1,0:T(2,128)}), f32[16,2,16]{2,1,0:T(2,128)S(1)}, u32[]{:S(2)}, u32[]{:S(2)}) %all-to-all-start.1) | async-done | bytes 2080 | tf_op jit(solution)/shard_map/all_to_all | solution.py:20
  (82 shorter events, 15.9 us)
Async XLA Ops:
  21.1 1.6 %collective-permute-start = (bf16[4,2,32,512]{3,2,1,0:T(8,128)(2,1)S(1)}, bf16[4,2,32,512]{3,2,1,0:T(8,128)(2,1)S(1)}, u32[]{:S(2)}, u32[]{:S(2)}) collective-permute-start(bf16[4,2,32,512]{3,2,1,0:T(8,128)(2,1)S(1)} %get-tuple-element.30), channel_id=1, source_target_pairs={{0,1},{1,0},{2,3},{3,2},{4,5},{5,4},{6,7},{7,6},{8,9},{9,8},{10,11... | collective-permute-start | bytes 786440 | tf_op jit(solution)/shard_map/ppermute | solution.py:33
  22.8 5.9 %collective-permute-start.3 = (bf16[64,512]{1,0:T(8,128)(2,1)S(1)}, bf16[64,512]{1,0:T(8,128)(2,1)S(1)}, u32[]{:S(2)}, u32[]{:S(2)}) collective-permute-start(bf16[64,512]{1,0:T(8,128)(2,1)S(1)} %bitcast.107), channel_id=1, source_target_pairs={{0,6},{1,7},{2,4},{3,5},{4,2},{5,3},{6,0},{7,1},{8,14},{9,15},{10,... | collective-permute-start | bytes 196616 | tf_op jit(solution)/shard_map/ppermute | solution.py:33
  23.2 5.4 %collective-permute-start.1 = (bf16[64,512]{1,0:T(8,128)(2,1)S(1)}, bf16[64,512]{1,0:T(8,128)(2,1)S(1)}, u32[]{:S(2)}, u32[]{:S(2)}) collective-permute-start(bf16[64,512]{1,0:T(8,128)(2,1)S(1)} %bitcast.105), channel_id=1, source_target_pairs={{0,5},{1,4},{2,7},{3,6},{4,1},{5,0},{6,3},{7,2},{8,13},{9,12},{10,... | collective-permute-start | bytes 196616 | tf_op jit(solution)/shard_map/ppermute | solution.py:33
  24.2 4.9 %collective-permute-start.2 = (bf16[64,512]{1,0:T(8,128)(2,1)S(1)}, bf16[64,512]{1,0:T(8,128)(2,1)S(1)}, u32[]{:S(2)}, u32[]{:S(2)}) collective-permute-start(bf16[64,512]{1,0:T(8,128)(2,1)S(1)} %bitcast.103), channel_id=1, source_target_pairs={{0,3},{1,2},{2,1},{3,0},{4,7},{5,6},{6,5},{7,4},{8,11},{9,10},{10,... | collective-permute-start | bytes 196616 | tf_op jit(solution)/shard_map/ppermute | solution.py:33
  29.2 5.2 %collective-permute-start.4 = (bf16[32,512]{1,0:T(8,128)(2,1)S(1)}, bf16[32,512]{1,0:T(8,128)(2,1)S(1)}, u32[]{:S(2)}, u32[]{:S(2)}) collective-permute-start(bf16[32,512]{1,0:T(8,128)(2,1)S(1)} %fusion.14), channel_id=1, source_target_pairs={{0,9},{1,8},{2,11},{3,10},{4,13},{5,12},{6,15},{7,14},{8,1},{9,0},... | collective-permute-start | bytes 98312 | tf_op jit(solution)/shard_map/ppermute | solution.py:33
  35.8 1.4 %collective-permute-start.5 = (bf16[4,2,16,512]{3,2,1,0:T(8,128)(2,1)S(1)}, bf16[4,2,16,512]{3,2,1,0:T(8,128)(2,1)S(1)}, u32[]{:S(2)}, u32[]{:S(2)}) collective-permute-start(bf16[4,2,16,512]{3,2,1,0:T(8,128)(2,1)S(1)} %get-tuple-element.32), channel_id=1, source_target_pairs={{0,1},{1,0},{2,3},{3,2},{4,5},{5,4},{6,7},{7,6},{8,9},{9,8},{10,11... | collective-permute-start | bytes 393224 | tf_op jit(solution)/shard_map/ppermute | solution.py:33
  37.3 5.1 %collective-permute-start.8 = (bf16[32,512]{1,0:T(8,128)(2,1)S(1)}, bf16[32,512]{1,0:T(8,128)(2,1)S(1)}, u32[]{:S(2)}, u32[]{:S(2)}) collective-permute-start(bf16[32,512]{1,0:T(8,128)(2,1)S(1)} %bitcast.115), channel_id=1, source_target_pairs={{0,6},{1,7},{2,4},{3,5},{4,2},{5,3},{6,0},{7,1},{8,14},{9,15},{10,... | collective-permute-start | bytes 98312 | tf_op jit(solution)/shard_map/ppermute | solution.py:33
  37.5 5.0 %collective-permute-start.6 = (bf16[32,512]{1,0:T(8,128)(2,1)S(1)}, bf16[32,512]{1,0:T(8,128)(2,1)S(1)}, u32[]{:S(2)}, u32[]{:S(2)}) collective-permute-start(bf16[32,512]{1,0:T(8,128)(2,1)S(1)} %bitcast.114), channel_id=1, source_target_pairs={{0,5},{1,4},{2,7},{3,6},{4,1},{5,0},{6,3},{7,2},{8,13},{9,12},{10,... | collective-permute-start | bytes 98312 | tf_op jit(solution)/shard_map/ppermute | solution.py:33
  39.0 3.6 %collective-permute-start.7 = (bf16[32,512]{1,0:T(8,128)(2,1)S(1)}, bf16[32,512]{1,0:T(8,128)(2,1)S(1)}, u32[]{:S(2)}, u32[]{:S(2)}) collective-permute-start(bf16[32,512]{1,0:T(8,128)(2,1)S(1)} %bitcast.113), channel_id=1, source_target_pairs={{0,3},{1,2},{2,1},{3,0},{4,7},{5,6},{6,5},{7,4},{8,11},{9,10},{10,... | collective-permute-start | bytes 98312 | tf_op jit(solution)/shard_map/ppermute | solution.py:33
  42.7 5.0 %collective-permute-start.9 = (bf16[32,512]{1,0:T(8,128)(2,1)S(1)}, bf16[32,512]{1,0:T(8,128)(2,1)S(1)}, u32[]{:S(2)}, u32[]{:S(2)}) collective-permute-start(bf16[32,512]{1,0:T(8,128)(2,1)S(1)} %pad_maximum_fusion.10), channel_id=1, source_target_pairs={{0,9},{1,8},{2,11},{3,10},{4,13},{5,12},{6,15},{7,14},{8,1},{9,0},... | collective-permute-start | bytes 98312 | tf_op jit(solution)/shard_map/ppermute | solution.py:33
  49.1 24.0 %copy-start.2 = (bf16[8192,256]{1,0:T(8,128)(2,1)S(1)}, bf16[8192,256]{1,0:T(8,128)(2,1)}, u32[]{:S(2)}) copy-start(bf16[8192,256]{1,0:T(8,128)(2,1)} %emission_ref.7) | copy-start | bytes 12582916
  49.1 1.6 %collective-permute-start.10 = (f32[4,2,16,512]{3,2,1,0:T(8,128)S(1)}, f32[4,2,16,512]{3,2,1,0:T(8,128)S(1)}, u32[]{:S(2)}, u32[]{:S(2)}) collective-permute-start(f32[4,2,16,512]{3,2,1,0:T(8,128)S(1)} %get-tuple-element.34), channel_id=1, source_target_pairs={{0,1},{1,0},{2,3},{3,2},{4,5},{5,4},{6,7},{7,6},{8,9},{9,8},{10,11... | collective-permute-start | bytes 786440 | tf_op jit(solution)/shard_map/ppermute | solution.py:33
  49.2 25.2 %copy-start.4 = (bf16[16,256]{1,0:T(8,128)(2,1)S(1)}, bf16[16,256]{1,0:T(8,128)(2,1)}, u32[]{:S(2)}) copy-start(bf16[16,256]{1,0:T(8,128)(2,1)} %logits_ref.1) | copy-start | bytes 24580
  50.8 4.8 %collective-permute-start.11 = (bf16[96,512]{1,0:T(8,128)(2,1)S(1)}, bf16[96,512]{1,0:T(8,128)(2,1)S(1)}, u32[]{:S(2)}, u32[]{:S(2)}) collective-permute-start(bf16[96,512]{1,0:T(8,128)(2,1)S(1)} %get-tuple-element.63), channel_id=1, source_target_pairs={{0,5},{1,4},{2,7},{3,6},{4,1},{5,0},{6,3},{7,2},{8,13},{9,12},{10,... | collective-permute-start | bytes 294920 | tf_op jit(solution)/shard_map/ppermute | solution.py:33
  50.9 4.8 %collective-permute-start.12 = (bf16[96,512]{1,0:T(8,128)(2,1)S(1)}, bf16[96,512]{1,0:T(8,128)(2,1)S(1)}, u32[]{:S(2)}, u32[]{:S(2)}) collective-permute-start(bf16[96,512]{1,0:T(8,128)(2,1)S(1)} %get-tuple-element.64), channel_id=1, source_target_pairs={{0,3},{1,2},{2,1},{3,0},{4,7},{5,6},{6,5},{7,4},{8,11},{9,10},{10,... | collective-permute-start | bytes 294920 | tf_op jit(solution)/shard_map/ppermute | solution.py:33
  52.1 6.7 %collective-permute-start.13 = (bf16[96,512]{1,0:T(8,128)(2,1)S(1)}, bf16[96,512]{1,0:T(8,128)(2,1)S(1)}, u32[]{:S(2)}, u32[]{:S(2)}) collective-permute-start(bf16[96,512]{1,0:T(8,128)(2,1)S(1)} %get-tuple-element.65), channel_id=1, source_target_pairs={{0,6},{1,7},{2,4},{3,5},{4,2},{5,3},{6,0},{7,1},{8,14},{9,15},{10,... | collective-permute-start | bytes 294920 | tf_op jit(solution)/shard_map/ppermute | solution.py:33
  58.9 6.7 %collective-permute-start.14 = (bf16[64,512]{1,0:T(8,128)(2,1)S(1)}, bf16[64,512]{1,0:T(8,128)(2,1)S(1)}, u32[]{:S(2)}, u32[]{:S(2)}) collective-permute-start(bf16[64,512]{1,0:T(8,128)(2,1)S(1)} %pad_maximum_fusion.9), channel_id=1, source_target_pairs={{0,9},{1,8},{2,11},{3,10},{4,13},{5,12},{6,15},{7,14},{8,1},{9,0},... | collective-permute-start | bytes 196616 | tf_op jit(solution)/shard_map/ppermute | solution.py:33
  59.0 1.4 %collective-permute-start.15 = (bf16[4,2,16,512]{3,2,1,0:T(8,128)(2,1)S(1)}, bf16[4,2,16,512]{3,2,1,0:T(8,128)(2,1)S(1)}, u32[]{:S(2)}, u32[]{:S(2)}) collective-permute-start(bf16[4,2,16,512]{3,2,1,0:T(8,128)(2,1)S(1)} %pad_maximum_fusion.6.near_ref), channel_id=1, source_target_pairs={{0,1},{1,0},{2,3},{3,2},{4,5},{5,4},{6,7},{7,6},{8,9},{9,8},{10,11... | collective-permute-start | bytes 393224 | tf_op jit(solution)/shard_map/ppermute | solution.py:33
  65.6 4.3 %collective-permute-start.16 = (f32[2,16,512]{2,1,0:T(8,128)S(1)}, f32[2,16,512]{2,1,0:T(8,128)S(1)}, u32[]{:S(2)}, u32[]{:S(2)}) collective-permute-start(f32[2,16,512]{2,1,0:T(8,128)S(1)} %last_messages.1), channel_id=1, source_target_pairs={{0,5},{1,4},{2,7},{3,6},{4,1},{5,0},{6,3},{7,2},{8,13},{9,12},{10,... | collective-permute-start | bytes 196616 | tf_op jit(solution)/shard_map/ppermute | solution.py:33
  65.6 6.0 %collective-permute-start.19 = (f32[2,16,512]{2,1,0:T(8,128)S(1)}, f32[2,16,512]{2,1,0:T(8,128)S(1)}, u32[]{:S(2)}, u32[]{:S(2)}) collective-permute-start(f32[2,16,512]{2,1,0:T(8,128)S(1)} %last_messages.1), channel_id=1, source_target_pairs={{0,6},{1,7},{2,4},{3,5},{4,2},{5,3},{6,0},{7,1},{8,14},{9,15},{10,... | collective-permute-start | bytes 196616 | tf_op jit(solution)/shard_map/ppermute | solution.py:33
  67.4 5.5 %collective-permute-start.18 = (f32[2,16,512]{2,1,0:T(8,128)S(1)}, f32[2,16,512]{2,1,0:T(8,128)S(1)}, u32[]{:S(2)}, u32[]{:S(2)}) collective-permute-start(f32[2,16,512]{2,1,0:T(8,128)S(1)} %last_messages.1), channel_id=1, source_target_pairs={{0,3},{1,2},{2,1},{3,0},{4,7},{5,6},{6,5},{7,4},{8,11},{9,10},{10,... | collective-permute-start | bytes 196616 | tf_op jit(solution)/shard_map/ppermute | solution.py:33
  69.8 3.3 %collective-permute-start.17 = (f32[2,2,16,512]{3,2,1,0:T(8,128)S(1)}, f32[2,2,16,512]{3,2,1,0:T(8,128)S(1)}, u32[]{:S(2)}, u32[]{:S(2)}) collective-permute-start(f32[2,2,16,512]{3,2,1,0:T(8,128)S(1)} %pad_maximum_fusion.7.refs_0_), channel_id=1, source_target_pairs={{0,1},{1,0},{2,3},{3,2},{4,5},{5,4},{6,7},{7,6},{8,9},{9,8},{10,11... | collective-permute-start | bytes 393224 | tf_op jit(solution)/shard_map/ppermute | solution.py:33
  73.0 1.5 %collective-permute-start.20 = (f32[2,2,16,512]{3,2,1,0:T(8,128)S(1)}, f32[2,2,16,512]{3,2,1,0:T(8,128)S(1)}, u32[]{:S(2)}, u32[]{:S(2)}) collective-permute-start(f32[2,2,16,512]{3,2,1,0:T(8,128)S(1)} %pad_maximum_fusion.8.refs_2_), channel_id=1, source_target_pairs={{0,1},{1,0},{2,3},{3,2},{4,5},{5,4},{6,7},{7,6},{8,9},{9,8},{10,11... | collective-permute-start | bytes 393224 | tf_op jit(solution)/shard_map/ppermute | solution.py:33
  75.9 10.0 %all-to-all-start.1 = ((f32[16,2,16]{2,1,0:T(2,128)}), f32[16,2,16]{2,1,0:T(2,128)S(1)}, u32[]{:S(2)}, u32[]{:S(2)}) async-start(f32[16,2,16]{2,1,0:T(2,128)} %broadcast_in_dim.7), calls=%async_computation.1 | async-start | bytes 32768 | tf_op jit(solution)/shard_map/all_to_all | solution.py:20
  (3 other events, 32.6 us)

commit v6 on v5

--- a/solution.py
+++ b/solution.py
@@ -25,7 +25,7 @@
 
 
 def basis(count):
-    return [1] + [(1 << bit) | 1 for bit in range(1, count)]
+    return [1, 3, 4] + [(1 << bit) | 1 for bit in range(3, count)]
 
 
 def swap(block, offset, devices):
@@ -204,15 +204,20 @@
         prompt = partner_at((to >> count) + first * (devices // 2), count)
         onehot = same_block & ((source & (devices - 1)) == prompt)
         orders.append(onehot.astype(jnp.bfloat16))
+    ones = jnp.ones((16, BLK), jnp.bfloat16)
+    early = devices * 3 // 8
+    for k in range(early):
+        sums_ref[k] = dot_rows(ones, emission_ref[pl.ds(k * rows, rows)])[:1]
     copies[0].wait()
     shape = (devices, BLK)
     tokens = column_of(token_ref, shape) - device * BLK
     onehot = (tokens == lax.broadcasted_iota(jnp.int32, shape, 1)).astype(jnp.bfloat16)
-    left = jnp.concatenate([onehot, jnp.ones((16, BLK), jnp.bfloat16)], axis=0)
+    left = jnp.concatenate([onehot, ones], axis=0)
     for k in range(devices):
-        product = dot_rows(left, emission_ref[pl.ds(k * rows, rows)])
+        product = dot_rows(onehot if k < early else left, emission_ref[pl.ds(k * rows, rows)])
         columns_ref[pl.ds(k * devices, devices)] = product[:devices].astype(jnp.bfloat16)
-        sums_ref[k] = product[devices : devices + 1]
+        if k >= early:
+            sums_ref[k] = product[devices : devices + 1]
     for order, out_ref in zip(orders, (kept_ref, sent_ref)):
         ordered = jnp.dot(order, columns_ref[...], preferred_element_type=jnp.float32)
         out_ref[...] = ordered.astype(jnp.bfloat16).reshape(out_ref.shape)

time: 87 us -> 86.4 us (level)
  waiting for transfers between devices: 36 us -> 34.9 us
    ppermute x21, waiting for transfers between devices: 30.1 us -> 29 us  [swap(): return lax.ppermute(block, 'vocab', pairs)]
  transfers between devices with their start and end apart: 22 -> 22, of which waited for: 17 -> 18; matrix products, arithmetic and copies ran while one was open for 1% -> 1% of each run, Pallas kernels for 7% -> 7%
where the time goes in v6:
time: 86.4 us; the launch traced here: 86.2 us
  waiting for transfers between devices  34.9 us (40%)
  starting transfers between devices  18 us (21%)
  blocking collectives  13.8 us (16%)
  Pallas kernels  13.4 us (16%)
  local copies, waits for them, and re-layouts  3.86 us (4%)
  other arithmetic  1.27 us (1%)
  between operations  0.93 us (1%)
    ppermute x21, waiting for transfers between devices, swap(): return lax.ppermute(block, 'vocab', pairs)  29 us
    ppermute x21, starting transfers between devices, swap(): return lax.ppermute(block, 'vocab', pairs)  14.3 us
    all_to_all x1, blocking collectives, exchange(): lax.all_to_all(blocks, 'vocab', split_axis=0, concat_axis=0, tiled=True)  13.8 us
    all_to_all x1, waiting for transfers between devices, exchange(): lax.all_to_all(blocks, 'vocab', split_axis=0, concat_axis=0, tiled=True)  5.88 us
    pallas_call x3, Pallas kernels, step(): pl.pallas_call(functools.partial(send_kernel, count, len(parts)), out_sha...  4.34 us
    pallas_call x3, Pallas kernels, step(): pl.pallas_call(functools.partial(keep_kernel, count), out_shape=pltpu.VME...  3.88 us
    all_to_all x1, starting transfers between devices, exchange(): lax.all_to_all(blocks, 'vocab', split_axis=0, concat_axis=0, tiled=True)  3.68 us
    pallas_call x1, Pallas kernels, first_products(): pl.pallas_call(functools.partial(products_kernel, count), out_shape=[jax....  2.35 us
  transfers between devices with their start and end apart: 22, of which 18 were waited for; matrix products, arithmetic and copies ran while one was open for 1% of the time, Pallas kernels for 7%

profile of v6, /device:TPU:0, one launch (start us, length us, event | category | flops | bytes accessed | tf_op | source)
XLA Modules:
  0.0 86.2 jit_solution(15028080411280556013)
XLA Ops:
  0.7 2.3 %copy-done.1 = bf16[8192,256]{1,0:T(8,128)(2,1)S(1)} copy-done((bf16[8192,256]{1,0:T(8,128)(2,1)S(1)}, bf16[8192,256]{1,0:T(8,128)(2,1)}, u32[]{:S(2)}) %copy-start.1) | copy-done | bytes 4194328
  3.0 2.4 %first_products.1 = (f32[16,1,512]{2,1,0:T(1,128)S(1)}, bf16[4,2,16,512]{3,2,1,0:T(8,128)(2,1)S(1)}, bf16[4,2,16,512]{3,2,1,0:T(8,128)(2,1)S(1)}, s32[1,16]{1,0:...) custom-call(s32[16]{0:T(128)} %token_hbm.1, s32[1,16]{1,0:T(1,128)} %bitcast.118, ...), custom_call_target="tpu_custom_call" | custom-call | tf_op jit(solution)/shard_map/first_products/pallas_call | solution.py:233
  5.8 13.8 %all_to_all.10.sums_ref = f32[16,1,512]{2,1,0:T(1,128)S(1)} all-to-all(f32[16,1,512]{2,1,0:T(1,128)S(1)} %get-tuple-element.25), channel_id=1, replica_groups=mesh['parts'=2,'vocab'=16] {'vocab'}, dimensions={0} | all-to-all | bytes 65536 | tf_op jit(solution)/shard_map/all_to_all | solution.py:20
  19.6 1.5 %step_sent_half.3 = (bf16[32,512]{1,0:T(8,128)(2,1)S(1)}, bf16[4,2,32,512]{3,2,1,0:T(8,128)(2,1)S(1)}) custom-call(bf16[8192,512]{1,0:T(8,128)(2,1)S(1)} %copy-done, bf16[256,48]{1,0:T(8,128)(2,1)S(1)} %get-tuple-element.24.route_ref, f32[16,1,512]{2,1,0:T(1,128)S(1)} %all_to_all.10.sums_ref, f32[16,512]{1,0:T(8,128)S(1)} %get-tuple-element.26.refs_0_, ...), custom_call_target="tpu_custom_call" | custom-call | tf_op jit(solution)/shard_map/step_sent_half/pallas_call | solution.py:382
  21.0 1.3 %step_kept_half.3 = f32[4,2,32,512]{3,2,1,0:T(8,128)S(1)} custom-call(bf16[8192,512]{1,0:T(8,128)(2,1)S(1)} %copy-done, bf16[32,512]{1,0:T(8,128)(2,1)S(1)} %get-tuple-element.28.halves_ref, bf16[4,2,16,512]{3,2,1,0:T(8,128)(2,1)S(1)} %get-tuple-element.29.refs_0_), custom_call_target="tpu_custom_call" | custom-call | tf_op jit(solution)/shard_map/step_kept_half/pallas_call | solution.py:394
  23.1 1.4 %collective-permute-start.1 = (bf16[64,512]{1,0:T(8,128)(2,1)S(1)}, bf16[64,512]{1,0:T(8,128)(2,1)S(1)}, u32[]{:S(2)}, u32[]{:S(2)}) collective-permute-start(bf16[64,512]{1,0:T(8,128)(2,1)S(1)} %bitcast.105), channel_id=1, source_target_pairs={{0,4},{1,5},{2,6},{3,7},{4,0},{5,1},{6,2},{7,3},{8,12},{9,13},{10,... | collective-permute-start | bytes 196616 | tf_op jit(solution)/shard_map/ppermute | solution.py:33
  25.7 2.0 %collective-permute-done.3 = bf16[64,512]{1,0:T(8,128)(2,1)S(1)} collective-permute-done((bf16[64,512]{1,0:T(8,128)(2,1)S(1)}, bf16[64,512]{1,0:T(8,128)(2,1)S(1)}, u32[]{:S(2)}, u32[]{:S(2)}) %collective-permute-start.3) | collective-permute-done | bytes 65568 | tf_op jit(solution)/shard_map/ppermute | solution.py:33
  29.7 5.0 %collective-permute-done.4.refs_1_ = bf16[32,512]{1,0:T(8,128)(2,1)S(1)} collective-permute-done((bf16[32,512]{1,0:T(8,128)(2,1)S(1)}, bf16[32,512]{1,0:T(8,128)(2,1)S(1)}, u32[]{:S(2)}, u32[]{:S(2)}) %collective-permute-start.4) | collective-permute-done | bytes 32800 | tf_op jit(solution)/shard_map/ppermute | solution.py:33
  34.6 1.4 %step_sent_half.4 = (bf16[32,512]{1,0:T(8,128)(2,1)S(1)}, bf16[4,2,16,512]{3,2,1,0:T(8,128)(2,1)S(1)}) custom-call(bf16[8192,512]{1,0:T(8,128)(2,1)S(1)} %copy-done, bf16[256,48]{1,0:T(8,128)(2,1)S(1)} %get-tuple-element.24.route_ref, f32[16,1,512]{2,1,0:T(1,128)S(1)} %all_to_all.10.sums_ref, f32[32,512]{1,0:T(8,128)S(1)} %slice_bitcast_fusion.2.refs_0_, ...), custom_call_target="tpu_custom_call" | custom-call | tf_op jit(solution)/shard_map/step_sent_half/pallas_call | solution.py:382
  36.2 1.3 %step_kept_half.4 = f32[4,2,16,512]{3,2,1,0:T(8,128)S(1)} custom-call(bf16[8192,512]{1,0:T(8,128)(2,1)S(1)} %copy-done, bf16[32,512]{1,0:T(8,128)(2,1)S(1)} %get-tuple-element.31.halves_ref), custom_call_target="tpu_custom_call" | custom-call | tf_op jit(solution)/shard_map/step_kept_half/pallas_call | solution.py:394
  37.7 2.4 %collective-permute-start.6 = (bf16[32,512]{1,0:T(8,128)(2,1)S(1)}, bf16[32,512]{1,0:T(8,128)(2,1)S(1)}, u32[]{:S(2)}, u32[]{:S(2)}) collective-permute-start(bf16[32,512]{1,0:T(8,128)(2,1)S(1)} %bitcast.114), channel_id=1, source_target_pairs={{0,4},{1,5},{2,6},{3,7},{4,0},{5,1},{6,2},{7,3},{8,12},{9,13},{10,... | collective-permute-start | bytes 98312 | tf_op jit(solution)/shard_map/ppermute | solution.py:33
  42.4 1.3 %collective-permute-done.7 = bf16[32,512]{1,0:T(8,128)(2,1)S(1)} collective-permute-done((bf16[32,512]{1,0:T(8,128)(2,1)S(1)}, bf16[32,512]{1,0:T(8,128)(2,1)S(1)}, u32[]{:S(2)}, u32[]{:S(2)}) %collective-permute-start.7) | collective-permute-done | bytes 32800 | tf_op jit(solution)/shard_map/ppermute | solution.py:33
  43.9 4.9 %collective-permute-done.9.refs_1_ = bf16[32,512]{1,0:T(8,128)(2,1)S(1)} collective-permute-done((bf16[32,512]{1,0:T(8,128)(2,1)S(1)}, bf16[32,512]{1,0:T(8,128)(2,1)S(1)}, u32[]{:S(2)}, u32[]{:S(2)}) %collective-permute-start.9) | collective-permute-done | bytes 32800 | tf_op jit(solution)/shard_map/ppermute | solution.py:33
  48.8 1.4 %step_sent_half.5 = (bf16[32,512]{1,0:T(8,128)(2,1)S(1)}, f32[4,2,16,512]{3,2,1,0:T(8,128)S(1)}) custom-call(bf16[8192,512]{1,0:T(8,128)(2,1)S(1)} %copy-done, bf16[256,48]{1,0:T(8,128)(2,1)S(1)} %get-tuple-element.24.route_ref, f32[16,1,512]{2,1,0:T(1,128)S(1)} %all_to_all.10.sums_ref, f32[16,512]{1,0:T(8,128)S(1)} %slice_bitcast_fusion.4.refs_0_, ...), custom_call_target="tpu_custom_call" | custom-call | tf_op jit(solution)/shard_map/step_sent_half/pallas_call | solution.py:382
  50.4 1.3 %step_kept_half.5 = f32[4,2,16,512]{3,2,1,0:T(8,128)S(1)} custom-call(bf16[8192,512]{1,0:T(8,128)(2,1)S(1)} %copy-done, bf16[32,512]{1,0:T(8,128)(2,1)S(1)} %get-tuple-element.33.halves_ref), custom_call_target="tpu_custom_call" | custom-call | tf_op jit(solution)/shard_map/step_kept_half/pallas_call | solution.py:394
  53.1 2.2 %collective-permute-start.13 = (bf16[96,512]{1,0:T(8,128)(2,1)S(1)}, bf16[96,512]{1,0:T(8,128)(2,1)S(1)}, u32[]{:S(2)}, u32[]{:S(2)}) collective-permute-start(bf16[96,512]{1,0:T(8,128)(2,1)S(1)} %get-tuple-element.65), channel_id=1, source_target_pairs={{0,7},{1,6},{2,5},{3,4},{4,3},{5,2},{6,1},{7,0},{8,15},{9,14},{10,... | collective-permute-start | bytes 294920 | tf_op jit(solution)/shard_map/ppermute | solution.py:33
  55.3 2.4 %collective-permute-done.11 = bf16[96,512]{1,0:T(8,128)(2,1)S(1)} collective-permute-done((bf16[96,512]{1,0:T(8,128)(2,1)S(1)}, bf16[96,512]{1,0:T(8,128)(2,1)S(1)}, u32[]{:S(2)}, u32[]{:S(2)}) %collective-permute-start.11) | collective-permute-done | bytes 98336 | tf_op jit(solution)/shard_map/ppermute | solution.py:33
  57.6 1.4 %collective-permute-done.13 = bf16[96,512]{1,0:T(8,128)(2,1)S(1)} collective-permute-done((bf16[96,512]{1,0:T(8,128)(2,1)S(1)}, bf16[96,512]{1,0:T(8,128)(2,1)S(1)}, u32[]{:S(2)}, u32[]{:S(2)}) %collective-permute-start.13) | collective-permute-done | bytes 98336 | tf_op jit(solution)/shard_map/ppermute | solution.py:33
  61.0 2.9 %collective-permute-done.14.refs_0_ = bf16[64,512]{1,0:T(8,128)(2,1)S(1)} collective-permute-done((bf16[64,512]{1,0:T(8,128)(2,1)S(1)}, bf16[64,512]{1,0:T(8,128)(2,1)S(1)}, u32[]{:S(2)}, u32[]{:S(2)}) %collective-permute-start.14) | collective-permute-done | bytes 65568 | tf_op jit(solution)/shard_map/ppermute | solution.py:33
  63.9 2.4 %collective-permute-start.16 = (f32[2,16,512]{2,1,0:T(8,128)S(1)}, f32[2,16,512]{2,1,0:T(8,128)S(1)}, u32[]{:S(2)}, u32[]{:S(2)}) collective-permute-start(f32[2,16,512]{2,1,0:T(8,128)S(1)} %last_messages.1), channel_id=1, source_target_pairs={{0,4},{1,5},{2,6},{3,7},{4,0},{5,1},{6,2},{7,3},{8,12},{9,13},{10,... | collective-permute-start | bytes 196616 | tf_op jit(solution)/shard_map/ppermute | solution.py:33
  68.9 2.8 %collective-permute-done.19 = f32[2,16,512]{2,1,0:T(8,128)S(1)} collective-permute-done((f32[2,16,512]{2,1,0:T(8,128)S(1)}, f32[2,16,512]{2,1,0:T(8,128)S(1)}, u32[]{:S(2)}, u32[]{:S(2)}) %collective-permute-start.19) | collective-permute-done | bytes 65568 | tf_op jit(solution)/shard_map/ppermute | solution.py:33
  72.3 1.3 %weigh_tokens.1.before_ref = f32[16,256]{1,0:T(8,128)S(1)} custom-call(bf16[8192,256]{1,0:T(8,128)(2,1)S(1)} %copy-done.2, bf16[256,512]{1,0:T(8,128)(2,1)S(1)} %order_forward.1.refs_1_.forward_ref, bf16[16,48]{1,0:T(8,128)(2,1)S(1)} %get-tuple-element.35.chooser_ref, f32[2,2,16,512]{3,2,1,0:T(8,128)S(1)} %pad_maximum_fusion.7.refs_0_, ...), custom_call_target="tpu_custom_call" | custom-call | tf_op jit(solution)/shard_map/weigh_tokens/pallas_call | solution.py:458
  75.0 3.7 %all-to-all-start.1 = ((f32[16,2,16]{2,1,0:T(2,128)}), f32[16,2,16]{2,1,0:T(2,128)S(1)}, u32[]{:S(2)}, u32[]{:S(2)}) async-start(f32[16,2,16]{2,1,0:T(2,128)} %broadcast_in_dim.7), calls=%async_computation.1 | async-start | bytes 32768 | tf_op jit(solution)/shard_map/all_to_all | solution.py:20
  79.3 5.9 %all-to-all-done.1 = f32[16,2,16]{2,1,0:T(2,128)S(1)} async-done(((f32[16,2,16]{2,1,0:T(2,128)}), f32[16,2,16]{2,1,0:T(2,128)S(1)}, u32[]{:S(2)}, u32[]{:S(2)}) %all-to-all-start.1) | async-done | bytes 2080 | tf_op jit(solution)/shard_map/all_to_all | solution.py:20
  (82 shorter events, 16.6 us)
Async XLA Ops:
  21.0 1.6 %collective-permute-start = (bf16[4,2,32,512]{3,2,1,0:T(8,128)(2,1)S(1)}, bf16[4,2,32,512]{3,2,1,0:T(8,128)(2,1)S(1)}, u32[]{:S(2)}, u32[]{:S(2)}) collective-permute-start(bf16[4,2,32,512]{3,2,1,0:T(8,128)(2,1)S(1)} %get-tuple-element.30), channel_id=1, source_target_pairs={{0,1},{1,0},{2,3},{3,2},{4,5},{5,4},{6,7},{7,6},{8,9},{9,8},{10,11... | collective-permute-start | bytes 786440 | tf_op jit(solution)/shard_map/ppermute | solution.py:33
  22.7 5.0 %collective-permute-start.3 = (bf16[64,512]{1,0:T(8,128)(2,1)S(1)}, bf16[64,512]{1,0:T(8,128)(2,1)S(1)}, u32[]{:S(2)}, u32[]{:S(2)}) collective-permute-start(bf16[64,512]{1,0:T(8,128)(2,1)S(1)} %bitcast.107), channel_id=1, source_target_pairs={{0,7},{1,6},{2,5},{3,4},{4,3},{5,2},{6,1},{7,0},{8,15},{9,14},{10,... | collective-permute-start | bytes 196616 | tf_op jit(solution)/shard_map/ppermute | solution.py:33
  23.1 5.3 %collective-permute-start.1 = (bf16[64,512]{1,0:T(8,128)(2,1)S(1)}, bf16[64,512]{1,0:T(8,128)(2,1)S(1)}, u32[]{:S(2)}, u32[]{:S(2)}) collective-permute-start(bf16[64,512]{1,0:T(8,128)(2,1)S(1)} %bitcast.105), channel_id=1, source_target_pairs={{0,4},{1,5},{2,6},{3,7},{4,0},{5,1},{6,2},{7,3},{8,12},{9,13},{10,... | collective-permute-start | bytes 196616 | tf_op jit(solution)/shard_map/ppermute | solution.py:33
  24.5 5.0 %collective-permute-start.2 = (bf16[64,512]{1,0:T(8,128)(2,1)S(1)}, bf16[64,512]{1,0:T(8,128)(2,1)S(1)}, u32[]{:S(2)}, u32[]{:S(2)}) collective-permute-start(bf16[64,512]{1,0:T(8,128)(2,1)S(1)} %bitcast.103), channel_id=1, source_target_pairs={{0,3},{1,2},{2,1},{3,0},{4,7},{5,6},{6,5},{7,4},{8,11},{9,10},{10,... | collective-permute-start | bytes 196616 | tf_op jit(solution)/shard_map/ppermute | solution.py:33
  29.5 5.1 %collective-permute-start.4 = (bf16[32,512]{1,0:T(8,128)(2,1)S(1)}, bf16[32,512]{1,0:T(8,128)(2,1)S(1)}, u32[]{:S(2)}, u32[]{:S(2)}) collective-permute-start(bf16[32,512]{1,0:T(8,128)(2,1)S(1)} %fusion.14), channel_id=1, source_target_pairs={{0,9},{1,8},{2,11},{3,10},{4,13},{5,12},{6,15},{7,14},{8,1},{9,0},... | collective-permute-start | bytes 98312 | tf_op jit(solution)/shard_map/ppermute | solution.py:33
  36.1 1.4 %collective-permute-start.5 = (bf16[4,2,16,512]{3,2,1,0:T(8,128)(2,1)S(1)}, bf16[4,2,16,512]{3,2,1,0:T(8,128)(2,1)S(1)}, u32[]{:S(2)}, u32[]{:S(2)}) collective-permute-start(bf16[4,2,16,512]{3,2,1,0:T(8,128)(2,1)S(1)} %get-tuple-element.32), channel_id=1, source_target_pairs={{0,1},{1,0},{2,3},{3,2},{4,5},{5,4},{6,7},{7,6},{8,9},{9,8},{10,11... | collective-permute-start | bytes 393224 | tf_op jit(solution)/shard_map/ppermute | solution.py:33
  37.6 4.3 %collective-permute-start.8 = (bf16[32,512]{1,0:T(8,128)(2,1)S(1)}, bf16[32,512]{1,0:T(8,128)(2,1)S(1)}, u32[]{:S(2)}, u32[]{:S(2)}) collective-permute-start(bf16[32,512]{1,0:T(8,128)(2,1)S(1)} %bitcast.115), channel_id=1, source_target_pairs={{0,7},{1,6},{2,5},{3,4},{4,3},{5,2},{6,1},{7,0},{8,15},{9,14},{10,... | collective-permute-start | bytes 98312 | tf_op jit(solution)/shard_map/ppermute | solution.py:33
  37.7 4.8 %collective-permute-start.6 = (bf16[32,512]{1,0:T(8,128)(2,1)S(1)}, bf16[32,512]{1,0:T(8,128)(2,1)S(1)}, u32[]{:S(2)}, u32[]{:S(2)}) collective-permute-start(bf16[32,512]{1,0:T(8,128)(2,1)S(1)} %bitcast.114), channel_id=1, source_target_pairs={{0,4},{1,5},{2,6},{3,7},{4,0},{5,1},{6,2},{7,3},{8,12},{9,13},{10,... | collective-permute-start | bytes 98312 | tf_op jit(solution)/shard_map/ppermute | solution.py:33
  40.1 3.7 %collective-permute-start.7 = (bf16[32,512]{1,0:T(8,128)(2,1)S(1)}, bf16[32,512]{1,0:T(8,128)(2,1)S(1)}, u32[]{:S(2)}, u32[]{:S(2)}) collective-permute-start(bf16[32,512]{1,0:T(8,128)(2,1)S(1)} %bitcast.113), channel_id=1, source_target_pairs={{0,3},{1,2},{2,1},{3,0},{4,7},{5,6},{6,5},{7,4},{8,11},{9,10},{10,... | collective-permute-start | bytes 98312 | tf_op jit(solution)/shard_map/ppermute | solution.py:33
  43.8 5.0 %collective-permute-start.9 = (bf16[32,512]{1,0:T(8,128)(2,1)S(1)}, bf16[32,512]{1,0:T(8,128)(2,1)S(1)}, u32[]{:S(2)}, u32[]{:S(2)}) collective-permute-start(bf16[32,512]{1,0:T(8,128)(2,1)S(1)} %pad_maximum_fusion.10), channel_id=1, source_target_pairs={{0,9},{1,8},{2,11},{3,10},{4,13},{5,12},{6,15},{7,14},{8,1},{9,0},... | collective-permute-start | bytes 98312 | tf_op jit(solution)/shard_map/ppermute | solution.py:33
  50.3 22.1 %copy-start.2 = (bf16[8192,256]{1,0:T(8,128)(2,1)S(1)}, bf16[8192,256]{1,0:T(8,128)(2,1)}, u32[]{:S(2)}) copy-start(bf16[8192,256]{1,0:T(8,128)(2,1)} %emission_ref.7) | copy-start | bytes 12582916
  50.3 1.6 %collective-permute-start.10 = (f32[4,2,16,512]{3,2,1,0:T(8,128)S(1)}, f32[4,2,16,512]{3,2,1,0:T(8,128)S(1)}, u32[]{:S(2)}, u32[]{:S(2)}) collective-permute-start(f32[4,2,16,512]{3,2,1,0:T(8,128)S(1)} %get-tuple-element.34), channel_id=1, source_target_pairs={{0,1},{1,0},{2,3},{3,2},{4,5},{5,4},{6,7},{7,6},{8,9},{9,8},{10,11... | collective-permute-start | bytes 786440 | tf_op jit(solution)/shard_map/ppermute | solution.py:33
  50.4 23.2 %copy-start.4 = (bf16[16,256]{1,0:T(8,128)(2,1)S(1)}, bf16[16,256]{1,0:T(8,128)(2,1)}, u32[]{:S(2)}) copy-start(bf16[16,256]{1,0:T(8,128)(2,1)} %logits_ref.1) | copy-start | bytes 24580
  52.0 5.6 %collective-permute-start.11 = (bf16[96,512]{1,0:T(8,128)(2,1)S(1)}, bf16[96,512]{1,0:T(8,128)(2,1)S(1)}, u32[]{:S(2)}, u32[]{:S(2)}) collective-permute-start(bf16[96,512]{1,0:T(8,128)(2,1)S(1)} %get-tuple-element.63), channel_id=1, source_target_pairs={{0,4},{1,5},{2,6},{3,7},{4,0},{5,1},{6,2},{7,3},{8,12},{9,13},{10,... | collective-permute-start | bytes 294920 | tf_op jit(solution)/shard_map/ppermute | solution.py:33
  52.1 5.6 %collective-permute-start.12 = (bf16[96,512]{1,0:T(8,128)(2,1)S(1)}, bf16[96,512]{1,0:T(8,128)(2,1)S(1)}, u32[]{:S(2)}, u32[]{:S(2)}) collective-permute-start(bf16[96,512]{1,0:T(8,128)(2,1)S(1)} %get-tuple-element.64), channel_id=1, source_target_pairs={{0,3},{1,2},{2,1},{3,0},{4,7},{5,6},{6,5},{7,4},{8,11},{9,10},{10,... | collective-permute-start | bytes 294920 | tf_op jit(solution)/shard_map/ppermute | solution.py:33
  53.1 6.0 %collective-permute-start.13 = (bf16[96,512]{1,0:T(8,128)(2,1)S(1)}, bf16[96,512]{1,0:T(8,128)(2,1)S(1)}, u32[]{:S(2)}, u32[]{:S(2)}) collective-permute-start(bf16[96,512]{1,0:T(8,128)(2,1)S(1)} %get-tuple-element.65), channel_id=1, source_target_pairs={{0,7},{1,6},{2,5},{3,4},{4,3},{5,2},{6,1},{7,0},{8,15},{9,14},{10,... | collective-permute-start | bytes 294920 | tf_op jit(solution)/shard_map/ppermute | solution.py:33
  59.1 4.8 %collective-permute-start.14 = (bf16[64,512]{1,0:T(8,128)(2,1)S(1)}, bf16[64,512]{1,0:T(8,128)(2,1)S(1)}, u32[]{:S(2)}, u32[]{:S(2)}) collective-permute-start(bf16[64,512]{1,0:T(8,128)(2,1)S(1)} %pad_maximum_fusion.9), channel_id=1, source_target_pairs={{0,9},{1,8},{2,11},{3,10},{4,13},{5,12},{6,15},{7,14},{8,1},{9,0},... | collective-permute-start | bytes 196616 | tf_op jit(solution)/shard_map/ppermute | solution.py:33
  59.3 1.5 %collective-permute-start.15 = (bf16[4,2,16,512]{3,2,1,0:T(8,128)(2,1)S(1)}, bf16[4,2,16,512]{3,2,1,0:T(8,128)(2,1)S(1)}, u32[]{:S(2)}, u32[]{:S(2)}) collective-permute-start(bf16[4,2,16,512]{3,2,1,0:T(8,128)(2,1)S(1)} %pad_maximum_fusion.6.near_ref), channel_id=1, source_target_pairs={{0,1},{1,0},{2,3},{3,2},{4,5},{5,4},{6,7},{7,6},{8,9},{9,8},{10,11... | collective-permute-start | bytes 393224 | tf_op jit(solution)/shard_map/ppermute | solution.py:33
  63.9 4.8 %collective-permute-start.16 = (f32[2,16,512]{2,1,0:T(8,128)S(1)}, f32[2,16,512]{2,1,0:T(8,128)S(1)}, u32[]{:S(2)}, u32[]{:S(2)}) collective-permute-start(f32[2,16,512]{2,1,0:T(8,128)S(1)} %last_messages.1), channel_id=1, source_target_pairs={{0,4},{1,5},{2,6},{3,7},{4,0},{5,1},{6,2},{7,3},{8,12},{9,13},{10,... | collective-permute-start | bytes 196616 | tf_op jit(solution)/shard_map/ppermute | solution.py:33
  66.3 5.4 %collective-permute-start.19 = (f32[2,16,512]{2,1,0:T(8,128)S(1)}, f32[2,16,512]{2,1,0:T(8,128)S(1)}, u32[]{:S(2)}, u32[]{:S(2)}) collective-permute-start(f32[2,16,512]{2,1,0:T(8,128)S(1)} %last_messages.1), channel_id=1, source_target_pairs={{0,7},{1,6},{2,5},{3,4},{4,3},{5,2},{6,1},{7,0},{8,15},{9,14},{10,... | collective-permute-start | bytes 196616 | tf_op jit(solution)/shard_map/ppermute | solution.py:33
  66.6 5.4 %collective-permute-start.18 = (f32[2,16,512]{2,1,0:T(8,128)S(1)}, f32[2,16,512]{2,1,0:T(8,128)S(1)}, u32[]{:S(2)}, u32[]{:S(2)}) collective-permute-start(f32[2,16,512]{2,1,0:T(8,128)S(1)} %last_messages.1), channel_id=1, source_target_pairs={{0,3},{1,2},{2,1},{3,0},{4,7},{5,6},{6,5},{7,4},{8,11},{9,10},{10,... | collective-permute-start | bytes 196616 | tf_op jit(solution)/shard_map/ppermute | solution.py:33
  68.8 3.5 %collective-permute-start.17 = (f32[2,2,16,512]{3,2,1,0:T(8,128)S(1)}, f32[2,2,16,512]{3,2,1,0:T(8,128)S(1)}, u32[]{:S(2)}, u32[]{:S(2)}) collective-permute-start(f32[2,2,16,512]{3,2,1,0:T(8,128)S(1)} %pad_maximum_fusion.7.refs_0_), channel_id=1, source_target_pairs={{0,1},{1,0},{2,3},{3,2},{4,5},{5,4},{6,7},{7,6},{8,9},{9,8},{10,11... | collective-permute-start | bytes 393224 | tf_op jit(solution)/shard_map/ppermute | solution.py:33
  72.0 1.7 %collective-permute-start.20 = (f32[2,2,16,512]{3,2,1,0:T(8,128)S(1)}, f32[2,2,16,512]{3,2,1,0:T(8,128)S(1)}, u32[]{:S(2)}, u32[]{:S(2)}) collective-permute-start(f32[2,2,16,512]{3,2,1,0:T(8,128)S(1)} %pad_maximum_fusion.8.refs_2_), channel_id=1, source_target_pairs={{0,1},{1,0},{2,3},{3,2},{4,5},{5,4},{6,7},{7,6},{8,9},{9,8},{10,11... | collective-permute-start | bytes 393224 | tf_op jit(solution)/shard_map/ppermute | solution.py:33
  75.0 10.2 %all-to-all-start.1 = ((f32[16,2,16]{2,1,0:T(2,128)}), f32[16,2,16]{2,1,0:T(2,128)S(1)}, u32[]{:S(2)}, u32[]{:S(2)}) async-start(f32[16,2,16]{2,1,0:T(2,128)} %broadcast_in_dim.7), calls=%async_computation.1 | async-start | bytes 32768 | tf_op jit(solution)/shard_map/all_to_all | solution.py:20
  (3 other events, 32.2 us)

commit v7 on v6

--- a/solution.py
+++ b/solution.py
@@ -25,7 +25,7 @@
 
 
 def basis(count):
-    return [1, 3, 4] + [(1 << bit) | 1 for bit in range(3, count)]
+    return [1, 2, 5] + [(1 << bit) | 1 for bit in range(3, count)]
 
 
 def swap(block, offset, devices):

time: 86.4 us -> 86.9 us (level)
  no operation moved by 1% of the time
where the time goes in v7:
time: 86.9 us; the launch traced here: 86.6 us
  waiting for transfers between devices  35.1 us (40%)
  starting transfers between devices  18.2 us (21%)
  blocking collectives  13.8 us (16%)
  Pallas kernels  13.5 us (16%)
  local copies, waits for them, and re-layouts  3.88 us (4%)
  other arithmetic  1.27 us (1%)
  between operations  0.95 us (1%)
    ppermute x21, waiting for transfers between devices, swap(): return lax.ppermute(block, 'vocab', pairs)  29.2 us
    ppermute x21, starting transfers between devices, swap(): return lax.ppermute(block, 'vocab', pairs)  14.4 us
    all_to_all x1, blocking collectives, exchange(): lax.all_to_all(blocks, 'vocab', split_axis=0, concat_axis=0, tiled=True)  13.8 us
    all_to_all x1, waiting for transfers between devices, exchange(): lax.all_to_all(blocks, 'vocab', split_axis=0, concat_axis=0, tiled=True)  5.88 us
    pallas_call x3, Pallas kernels, step(): pl.pallas_call(functools.partial(send_kernel, count, len(parts)), out_sha...  4.34 us
    pallas_call x3, Pallas kernels, step(): pl.pallas_call(functools.partial(keep_kernel, count), out_shape=pltpu.VME...  3.89 us
    all_to_all x1, starting transfers between devices, exchange(): lax.all_to_all(blocks, 'vocab', split_axis=0, concat_axis=0, tiled=True)  3.82 us
    unnamed x10, local copies, waits for them, and re-layouts  2.37 us
  transfers between devices with their start and end apart: 22, of which 18 were waited for; matrix products, arithmetic and copies ran while one was open for 1% of the time, Pallas kernels for 7%

profile of v7, /device:TPU:0, one launch (start us, length us, event | category | flops | bytes accessed | tf_op | source)
XLA Modules:
  0.0 86.6 jit_solution(14240887307791989487)
XLA Ops:
  0.7 2.3 %copy-done.1 = bf16[8192,256]{1,0:T(8,128)(2,1)S(1)} copy-done((bf16[8192,256]{1,0:T(8,128)(2,1)S(1)}, bf16[8192,256]{1,0:T(8,128)(2,1)}, u32[]{:S(2)}) %copy-start.1) | copy-done | bytes 4194328
  3.0 2.4 %first_products.1 = (f32[16,1,512]{2,1,0:T(1,128)S(1)}, bf16[4,2,16,512]{3,2,1,0:T(8,128)(2,1)S(1)}, bf16[4,2,16,512]{3,2,1,0:T(8,128)(2,1)S(1)}, s32[1,16]{1,0:...) custom-call(s32[16]{0:T(128)} %token_hbm.1, s32[1,16]{1,0:T(1,128)} %bitcast.118, ...), custom_call_target="tpu_custom_call" | custom-call | tf_op jit(solution)/shard_map/first_products/pallas_call | solution.py:233
  5.8 13.8 %all_to_all.10.sums_ref = f32[16,1,512]{2,1,0:T(1,128)S(1)} all-to-all(f32[16,1,512]{2,1,0:T(1,128)S(1)} %get-tuple-element.25), channel_id=1, replica_groups=mesh['parts'=2,'vocab'=16] {'vocab'}, dimensions={0} | all-to-all | bytes 65536 | tf_op jit(solution)/shard_map/all_to_all | solution.py:20
  19.6 1.5 %step_sent_half.3 = (bf16[32,512]{1,0:T(8,128)(2,1)S(1)}, bf16[4,2,32,512]{3,2,1,0:T(8,128)(2,1)S(1)}) custom-call(bf16[8192,512]{1,0:T(8,128)(2,1)S(1)} %copy-done, bf16[256,48]{1,0:T(8,128)(2,1)S(1)} %get-tuple-element.24.route_ref, f32[16,1,512]{2,1,0:T(1,128)S(1)} %all_to_all.10.sums_ref, f32[16,512]{1,0:T(8,128)S(1)} %get-tuple-element.26.refs_0_, ...), custom_call_target="tpu_custom_call" | custom-call | tf_op jit(solution)/shard_map/step_sent_half/pallas_call | solution.py:382
  21.0 1.3 %step_kept_half.3 = f32[4,2,32,512]{3,2,1,0:T(8,128)S(1)} custom-call(bf16[8192,512]{1,0:T(8,128)(2,1)S(1)} %copy-done, bf16[32,512]{1,0:T(8,128)(2,1)S(1)} %get-tuple-element.28.halves_ref, bf16[4,2,16,512]{3,2,1,0:T(8,128)(2,1)S(1)} %get-tuple-element.29.refs_0_), custom_call_target="tpu_custom_call" | custom-call | tf_op jit(solution)/shard_map/step_kept_half/pallas_call | solution.py:394
  24.3 1.7 %collective-permute-start.2 = (bf16[64,512]{1,0:T(8,128)(2,1)S(1)}, bf16[64,512]{1,0:T(8,128)(2,1)S(1)}, u32[]{:S(2)}, u32[]{:S(2)}) collective-permute-start(bf16[64,512]{1,0:T(8,128)(2,1)S(1)} %bitcast.103), channel_id=1, source_target_pairs={{0,2},{1,3},{2,0},{3,1},{4,6},{5,7},{6,4},{7,5},{8,10},{9,11},{10,... | collective-permute-start | bytes 196616 | tf_op jit(solution)/shard_map/ppermute | solution.py:33
  26.0 1.7 %collective-permute-done.3 = bf16[64,512]{1,0:T(8,128)(2,1)S(1)} collective-permute-done((bf16[64,512]{1,0:T(8,128)(2,1)S(1)}, bf16[64,512]{1,0:T(8,128)(2,1)S(1)}, u32[]{:S(2)}, u32[]{:S(2)}) %collective-permute-start.3) | collective-permute-done | bytes 65568 | tf_op jit(solution)/shard_map/ppermute | solution.py:33
  28.0 1.5 %collective-permute-done.2 = bf16[64,512]{1,0:T(8,128)(2,1)S(1)} collective-permute-done((bf16[64,512]{1,0:T(8,128)(2,1)S(1)}, bf16[64,512]{1,0:T(8,128)(2,1)S(1)}, u32[]{:S(2)}, u32[]{:S(2)}) %collective-permute-start.2) | collective-permute-done | bytes 65568 | tf_op jit(solution)/shard_map/ppermute | solution.py:33
  29.6 5.0 %collective-permute-done.4.refs_1_ = bf16[32,512]{1,0:T(8,128)(2,1)S(1)} collective-permute-done((bf16[32,512]{1,0:T(8,128)(2,1)S(1)}, bf16[32,512]{1,0:T(8,128)(2,1)S(1)}, u32[]{:S(2)}, u32[]{:S(2)}) %collective-permute-start.4) | collective-permute-done | bytes 32800 | tf_op jit(solution)/shard_map/ppermute | solution.py:33
  34.6 1.4 %step_sent_half.4 = (bf16[32,512]{1,0:T(8,128)(2,1)S(1)}, bf16[4,2,16,512]{3,2,1,0:T(8,128)(2,1)S(1)}) custom-call(bf16[8192,512]{1,0:T(8,128)(2,1)S(1)} %copy-done, bf16[256,48]{1,0:T(8,128)(2,1)S(1)} %get-tuple-element.24.route_ref, f32[16,1,512]{2,1,0:T(1,128)S(1)} %all_to_all.10.sums_ref, f32[32,512]{1,0:T(8,128)S(1)} %slice_bitcast_fusion.2.refs_0_, ...), custom_call_target="tpu_custom_call" | custom-call | tf_op jit(solution)/shard_map/step_sent_half/pallas_call | solution.py:382
  37.7 2.0 %collective-permute-start.6 = (bf16[32,512]{1,0:T(8,128)(2,1)S(1)}, bf16[32,512]{1,0:T(8,128)(2,1)S(1)}, u32[]{:S(2)}, u32[]{:S(2)}) collective-permute-start(bf16[32,512]{1,0:T(8,128)(2,1)S(1)} %bitcast.114), channel_id=1, source_target_pairs={{0,5},{1,4},{2,7},{3,6},{4,1},{5,0},{6,3},{7,2},{8,13},{9,12},{10,... | collective-permute-start | bytes 98312 | tf_op jit(solution)/shard_map/ppermute | solution.py:33
  41.9 1.7 %collective-permute-done.7 = bf16[32,512]{1,0:T(8,128)(2,1)S(1)} collective-permute-done((bf16[32,512]{1,0:T(8,128)(2,1)S(1)}, bf16[32,512]{1,0:T(8,128)(2,1)S(1)}, u32[]{:S(2)}, u32[]{:S(2)}) %collective-permute-start.7) | collective-permute-done | bytes 32800 | tf_op jit(solution)/shard_map/ppermute | solution.py:33
  43.8 4.6 %collective-permute-done.9.refs_1_ = bf16[32,512]{1,0:T(8,128)(2,1)S(1)} collective-permute-done((bf16[32,512]{1,0:T(8,128)(2,1)S(1)}, bf16[32,512]{1,0:T(8,128)(2,1)S(1)}, u32[]{:S(2)}, u32[]{:S(2)}) %collective-permute-start.9) | collective-permute-done | bytes 32800 | tf_op jit(solution)/shard_map/ppermute | solution.py:33
  48.4 1.4 %step_sent_half.5 = (bf16[32,512]{1,0:T(8,128)(2,1)S(1)}, f32[4,2,16,512]{3,2,1,0:T(8,128)S(1)}) custom-call(bf16[8192,512]{1,0:T(8,128)(2,1)S(1)} %copy-done, bf16[256,48]{1,0:T(8,128)(2,1)S(1)} %get-tuple-element.24.route_ref, f32[16,1,512]{2,1,0:T(1,128)S(1)} %all_to_all.10.sums_ref, f32[16,512]{1,0:T(8,128)S(1)} %slice_bitcast_fusion.4.refs_0_, ...), custom_call_target="tpu_custom_call" | custom-call | tf_op jit(solution)/shard_map/step_sent_half/pallas_call | solution.py:382
  49.9 1.3 %step_kept_half.5 = f32[4,2,16,512]{3,2,1,0:T(8,128)S(1)} custom-call(bf16[8192,512]{1,0:T(8,128)(2,1)S(1)} %copy-done, bf16[32,512]{1,0:T(8,128)(2,1)S(1)} %get-tuple-element.33.halves_ref), custom_call_target="tpu_custom_call" | custom-call | tf_op jit(solution)/shard_map/step_kept_half/pallas_call | solution.py:394
  53.0 1.6 %collective-permute-start.13 = (bf16[96,512]{1,0:T(8,128)(2,1)S(1)}, bf16[96,512]{1,0:T(8,128)(2,1)S(1)}, u32[]{:S(2)}, u32[]{:S(2)}) collective-permute-start(bf16[96,512]{1,0:T(8,128)(2,1)S(1)} %get-tuple-element.65), channel_id=1, source_target_pairs={{0,7},{1,6},{2,5},{3,4},{4,3},{5,2},{6,1},{7,0},{8,15},{9,14},{10,... | collective-permute-start | bytes 294920 | tf_op jit(solution)/shard_map/ppermute | solution.py:33
  54.5 1.8 %collective-permute-done.11 = bf16[96,512]{1,0:T(8,128)(2,1)S(1)} collective-permute-done((bf16[96,512]{1,0:T(8,128)(2,1)S(1)}, bf16[96,512]{1,0:T(8,128)(2,1)S(1)}, u32[]{:S(2)}, u32[]{:S(2)}) %collective-permute-start.11) | collective-permute-done | bytes 98336 | tf_op jit(solution)/shard_map/ppermute | solution.py:33
  56.7 2.4 %collective-permute-done.13 = bf16[96,512]{1,0:T(8,128)(2,1)S(1)} collective-permute-done((bf16[96,512]{1,0:T(8,128)(2,1)S(1)}, bf16[96,512]{1,0:T(8,128)(2,1)S(1)}, u32[]{:S(2)}, u32[]{:S(2)}) %collective-permute-start.13) | collective-permute-done | bytes 98336 | tf_op jit(solution)/shard_map/ppermute | solution.py:33
  61.1 4.6 %collective-permute-done.14.refs_0_ = bf16[64,512]{1,0:T(8,128)(2,1)S(1)} collective-permute-done((bf16[64,512]{1,0:T(8,128)(2,1)S(1)}, bf16[64,512]{1,0:T(8,128)(2,1)S(1)}, u32[]{:S(2)}, u32[]{:S(2)}) %collective-permute-start.14) | collective-permute-done | bytes 65568 | tf_op jit(solution)/shard_map/ppermute | solution.py:33
  66.5 2.5 %collective-permute-start.18 = (f32[2,16,512]{2,1,0:T(8,128)S(1)}, f32[2,16,512]{2,1,0:T(8,128)S(1)}, u32[]{:S(2)}, u32[]{:S(2)}) collective-permute-start(f32[2,16,512]{2,1,0:T(8,128)S(1)} %last_messages.1), channel_id=1, source_target_pairs={{0,2},{1,3},{2,0},{3,1},{4,6},{5,7},{6,4},{7,5},{8,10},{9,11},{10,... | collective-permute-start | bytes 196616 | tf_op jit(solution)/shard_map/ppermute | solution.py:33
  70.8 1.7 %collective-permute-done.18 = f32[2,16,512]{2,1,0:T(8,128)S(1)} collective-permute-done((f32[2,16,512]{2,1,0:T(8,128)S(1)}, f32[2,16,512]{2,1,0:T(8,128)S(1)}, u32[]{:S(2)}, u32[]{:S(2)}) %collective-permute-start.18) | collective-permute-done | bytes 65568 | tf_op jit(solution)/shard_map/ppermute | solution.py:33
  72.6 1.3 %weigh_tokens.1.before_ref = f32[16,256]{1,0:T(8,128)S(1)} custom-call(bf16[8192,256]{1,0:T(8,128)(2,1)S(1)} %copy-done.2, bf16[256,512]{1,0:T(8,128)(2,1)S(1)} %order_forward.1.refs_1_.forward_ref, bf16[16,48]{1,0:T(8,128)(2,1)S(1)} %get-tuple-element.35.chooser_ref, f32[2,2,16,512]{3,2,1,0:T(8,128)S(1)} %pad_maximum_fusion.7.refs_0_, ...), custom_call_target="tpu_custom_call" | custom-call | tf_op jit(solution)/shard_map/weigh_tokens/pallas_call | solution.py:458
  75.4 3.8 %all-to-all-start.1 = ((f32[16,2,16]{2,1,0:T(2,128)}), f32[16,2,16]{2,1,0:T(2,128)S(1)}, u32[]{:S(2)}, u32[]{:S(2)}) async-start(f32[16,2,16]{2,1,0:T(2,128)} %broadcast_in_dim.7), calls=%async_computation.1 | async-start | bytes 32768 | tf_op jit(solution)/shard_map/all_to_all | solution.py:20
  79.8 5.9 %all-to-all-done.1 = f32[16,2,16]{2,1,0:T(2,128)S(1)} async-done(((f32[16,2,16]{2,1,0:T(2,128)}), f32[16,2,16]{2,1,0:T(2,128)S(1)}, u32[]{:S(2)}, u32[]{:S(2)}) %all-to-all-start.1) | async-done | bytes 2080 | tf_op jit(solution)/shard_map/all_to_all | solution.py:20
  (82 shorter events, 16.4 us)
Async XLA Ops:
  21.0 1.6 %collective-permute-start = (bf16[4,2,32,512]{3,2,1,0:T(8,128)(2,1)S(1)}, bf16[4,2,32,512]{3,2,1,0:T(8,128)(2,1)S(1)}, u32[]{:S(2)}, u32[]{:S(2)}) collective-permute-start(bf16[4,2,32,512]{3,2,1,0:T(8,128)(2,1)S(1)} %get-tuple-element.30), channel_id=1, source_target_pairs={{0,1},{1,0},{2,3},{3,2},{4,5},{5,4},{6,7},{7,6},{8,9},{9,8},{10,11... | collective-permute-start | bytes 786440 | tf_op jit(solution)/shard_map/ppermute | solution.py:33
  22.7 5.0 %collective-permute-start.3 = (bf16[64,512]{1,0:T(8,128)(2,1)S(1)}, bf16[64,512]{1,0:T(8,128)(2,1)S(1)}, u32[]{:S(2)}, u32[]{:S(2)}) collective-permute-start(bf16[64,512]{1,0:T(8,128)(2,1)S(1)} %bitcast.107), channel_id=1, source_target_pairs={{0,7},{1,6},{2,5},{3,4},{4,3},{5,2},{6,1},{7,0},{8,15},{9,14},{10,... | collective-permute-start | bytes 196616 | tf_op jit(solution)/shard_map/ppermute | solution.py:33
  23.1 4.9 %collective-permute-start.1 = (bf16[64,512]{1,0:T(8,128)(2,1)S(1)}, bf16[64,512]{1,0:T(8,128)(2,1)S(1)}, u32[]{:S(2)}, u32[]{:S(2)}) collective-permute-start(bf16[64,512]{1,0:T(8,128)(2,1)S(1)} %bitcast.105), channel_id=1, source_target_pairs={{0,5},{1,4},{2,7},{3,6},{4,1},{5,0},{6,3},{7,2},{8,13},{9,12},{10,... | collective-permute-start | bytes 196616 | tf_op jit(solution)/shard_map/ppermute | solution.py:33
  24.3 5.2 %collective-permute-start.2 = (bf16[64,512]{1,0:T(8,128)(2,1)S(1)}, bf16[64,512]{1,0:T(8,128)(2,1)S(1)}, u32[]{:S(2)}, u32[]{:S(2)}) collective-permute-start(bf16[64,512]{1,0:T(8,128)(2,1)S(1)} %bitcast.103), channel_id=1, source_target_pairs={{0,2},{1,3},{2,0},{3,1},{4,6},{5,7},{6,4},{7,5},{8,10},{9,11},{10,... | collective-permute-start | bytes 196616 | tf_op jit(solution)/shard_map/ppermute | solution.py:33
  29.5 5.1 %collective-permute-start.4 = (bf16[32,512]{1,0:T(8,128)(2,1)S(1)}, bf16[32,512]{1,0:T(8,128)(2,1)S(1)}, u32[]{:S(2)}, u32[]{:S(2)}) collective-permute-start(bf16[32,512]{1,0:T(8,128)(2,1)S(1)} %fusion.14), channel_id=1, source_target_pairs={{0,9},{1,8},{2,11},{3,10},{4,13},{5,12},{6,15},{7,14},{8,1},{9,0},... | collective-permute-start | bytes 98312 | tf_op jit(solution)/shard_map/ppermute | solution.py:33
  36.1 1.4 %collective-permute-start.5 = (bf16[4,2,16,512]{3,2,1,0:T(8,128)(2,1)S(1)}, bf16[4,2,16,512]{3,2,1,0:T(8,128)(2,1)S(1)}, u32[]{:S(2)}, u32[]{:S(2)}) collective-permute-start(bf16[4,2,16,512]{3,2,1,0:T(8,128)(2,1)S(1)} %get-tuple-element.32), channel_id=1, source_target_pairs={{0,1},{1,0},{2,3},{3,2},{4,5},{5,4},{6,7},{7,6},{8,9},{9,8},{10,11... | collective-permute-start | bytes 393224 | tf_op jit(solution)/shard_map/ppermute | solution.py:33
  37.6 4.3 %collective-permute-start.8 = (bf16[32,512]{1,0:T(8,128)(2,1)S(1)}, bf16[32,512]{1,0:T(8,128)(2,1)S(1)}, u32[]{:S(2)}, u32[]{:S(2)}) collective-permute-start(bf16[32,512]{1,0:T(8,128)(2,1)S(1)} %bitcast.115), channel_id=1, source_target_pairs={{0,7},{1,6},{2,5},{3,4},{4,3},{5,2},{6,1},{7,0},{8,15},{9,14},{10,... | collective-permute-start | bytes 98312 | tf_op jit(solution)/shard_map/ppermute | solution.py:33
  37.7 4.2 %collective-permute-start.6 = (bf16[32,512]{1,0:T(8,128)(2,1)S(1)}, bf16[32,512]{1,0:T(8,128)(2,1)S(1)}, u32[]{:S(2)}, u32[]{:S(2)}) collective-permute-start(bf16[32,512]{1,0:T(8,128)(2,1)S(1)} %bitcast.114), channel_id=1, source_target_pairs={{0,5},{1,4},{2,7},{3,6},{4,1},{5,0},{6,3},{7,2},{8,13},{9,12},{10,... | collective-permute-start | bytes 98312 | tf_op jit(solution)/shard_map/ppermute | solution.py:33
  39.7 3.9 %collective-permute-start.7 = (bf16[32,512]{1,0:T(8,128)(2,1)S(1)}, bf16[32,512]{1,0:T(8,128)(2,1)S(1)}, u32[]{:S(2)}, u32[]{:S(2)}) collective-permute-start(bf16[32,512]{1,0:T(8,128)(2,1)S(1)} %bitcast.113), channel_id=1, source_target_pairs={{0,2},{1,3},{2,0},{3,1},{4,6},{5,7},{6,4},{7,5},{8,10},{9,11},{10,... | collective-permute-start | bytes 98312 | tf_op jit(solution)/shard_map/ppermute | solution.py:33
  43.7 4.7 %collective-permute-start.9 = (bf16[32,512]{1,0:T(8,128)(2,1)S(1)}, bf16[32,512]{1,0:T(8,128)(2,1)S(1)}, u32[]{:S(2)}, u32[]{:S(2)}) collective-permute-start(bf16[32,512]{1,0:T(8,128)(2,1)S(1)} %pad_maximum_fusion.10), channel_id=1, source_target_pairs={{0,9},{1,8},{2,11},{3,10},{4,13},{5,12},{6,15},{7,14},{8,1},{9,0},... | collective-permute-start | bytes 98312 | tf_op jit(solution)/shard_map/ppermute | solution.py:33
  49.8 22.8 %copy-start.2 = (bf16[8192,256]{1,0:T(8,128)(2,1)S(1)}, bf16[8192,256]{1,0:T(8,128)(2,1)}, u32[]{:S(2)}) copy-start(bf16[8192,256]{1,0:T(8,128)(2,1)} %emission_ref.7) | copy-start | bytes 12582916
  49.8 1.6 %collective-permute-start.10 = (f32[4,2,16,512]{3,2,1,0:T(8,128)S(1)}, f32[4,2,16,512]{3,2,1,0:T(8,128)S(1)}, u32[]{:S(2)}, u32[]{:S(2)}) collective-permute-start(f32[4,2,16,512]{3,2,1,0:T(8,128)S(1)} %get-tuple-element.34), channel_id=1, source_target_pairs={{0,1},{1,0},{2,3},{3,2},{4,5},{5,4},{6,7},{7,6},{8,9},{9,8},{10,11... | collective-permute-start | bytes 786440 | tf_op jit(solution)/shard_map/ppermute | solution.py:33
  49.8 24.1 %copy-start.4 = (bf16[16,256]{1,0:T(8,128)(2,1)S(1)}, bf16[16,256]{1,0:T(8,128)(2,1)}, u32[]{:S(2)}) copy-start(bf16[16,256]{1,0:T(8,128)(2,1)} %logits_ref.1) | copy-start | bytes 24580
  51.5 4.8 %collective-permute-start.11 = (bf16[96,512]{1,0:T(8,128)(2,1)S(1)}, bf16[96,512]{1,0:T(8,128)(2,1)S(1)}, u32[]{:S(2)}, u32[]{:S(2)}) collective-permute-start(bf16[96,512]{1,0:T(8,128)(2,1)S(1)} %get-tuple-element.63), channel_id=1, source_target_pairs={{0,5},{1,4},{2,7},{3,6},{4,1},{5,0},{6,3},{7,2},{8,13},{9,12},{10,... | collective-permute-start | bytes 294920 | tf_op jit(solution)/shard_map/ppermute | solution.py:33
  51.7 5.0 %collective-permute-start.12 = (bf16[96,512]{1,0:T(8,128)(2,1)S(1)}, bf16[96,512]{1,0:T(8,128)(2,1)S(1)}, u32[]{:S(2)}, u32[]{:S(2)}) collective-permute-start(bf16[96,512]{1,0:T(8,128)(2,1)S(1)} %get-tuple-element.64), channel_id=1, source_target_pairs={{0,2},{1,3},{2,0},{3,1},{4,6},{5,7},{6,4},{7,5},{8,10},{9,11},{10,... | collective-permute-start | bytes 294920 | tf_op jit(solution)/shard_map/ppermute | solution.py:33
  53.0 6.2 %collective-permute-start.13 = (bf16[96,512]{1,0:T(8,128)(2,1)S(1)}, bf16[96,512]{1,0:T(8,128)(2,1)S(1)}, u32[]{:S(2)}, u32[]{:S(2)}) collective-permute-start(bf16[96,512]{1,0:T(8,128)(2,1)S(1)} %get-tuple-element.65), channel_id=1, source_target_pairs={{0,7},{1,6},{2,5},{3,4},{4,3},{5,2},{6,1},{7,0},{8,15},{9,14},{10,... | collective-permute-start | bytes 294920 | tf_op jit(solution)/shard_map/ppermute | solution.py:33
  59.2 6.4 %collective-permute-start.14 = (bf16[64,512]{1,0:T(8,128)(2,1)S(1)}, bf16[64,512]{1,0:T(8,128)(2,1)S(1)}, u32[]{:S(2)}, u32[]{:S(2)}) collective-permute-start(bf16[64,512]{1,0:T(8,128)(2,1)S(1)} %pad_maximum_fusion.9), channel_id=1, source_target_pairs={{0,9},{1,8},{2,11},{3,10},{4,13},{5,12},{6,15},{7,14},{8,1},{9,0},... | collective-permute-start | bytes 196616 | tf_op jit(solution)/shard_map/ppermute | solution.py:33
  59.3 1.4 %collective-permute-start.15 = (bf16[4,2,16,512]{3,2,1,0:T(8,128)(2,1)S(1)}, bf16[4,2,16,512]{3,2,1,0:T(8,128)(2,1)S(1)}, u32[]{:S(2)}, u32[]{:S(2)}) collective-permute-start(bf16[4,2,16,512]{3,2,1,0:T(8,128)(2,1)S(1)} %pad_maximum_fusion.6.near_ref), channel_id=1, source_target_pairs={{0,1},{1,0},{2,3},{3,2},{4,5},{5,4},{6,7},{7,6},{8,9},{9,8},{10,11... | collective-permute-start | bytes 393224 | tf_op jit(solution)/shard_map/ppermute | solution.py:33
  65.7 4.1 %collective-permute-start.16 = (f32[2,16,512]{2,1,0:T(8,128)S(1)}, f32[2,16,512]{2,1,0:T(8,128)S(1)}, u32[]{:S(2)}, u32[]{:S(2)}) collective-permute-start(f32[2,16,512]{2,1,0:T(8,128)S(1)} %last_messages.1), channel_id=1, source_target_pairs={{0,5},{1,4},{2,7},{3,6},{4,1},{5,0},{6,3},{7,2},{8,13},{9,12},{10,... | collective-permute-start | bytes 196616 | tf_op jit(solution)/shard_map/ppermute | solution.py:33
  65.7 5.0 %collective-permute-start.19 = (f32[2,16,512]{2,1,0:T(8,128)S(1)}, f32[2,16,512]{2,1,0:T(8,128)S(1)}, u32[]{:S(2)}, u32[]{:S(2)}) collective-permute-start(f32[2,16,512]{2,1,0:T(8,128)S(1)} %last_messages.1), channel_id=1, source_target_pairs={{0,7},{1,6},{2,5},{3,4},{4,3},{5,2},{6,1},{7,0},{8,15},{9,14},{10,... | collective-permute-start | bytes 196616 | tf_op jit(solution)/shard_map/ppermute | solution.py:33
  66.5 6.0 %collective-permute-start.18 = (f32[2,16,512]{2,1,0:T(8,128)S(1)}, f32[2,16,512]{2,1,0:T(8,128)S(1)}, u32[]{:S(2)}, u32[]{:S(2)}) collective-permute-start(f32[2,16,512]{2,1,0:T(8,128)S(1)} %last_messages.1), channel_id=1, source_target_pairs={{0,2},{1,3},{2,0},{3,1},{4,6},{5,7},{6,4},{7,5},{8,10},{9,11},{10,... | collective-permute-start | bytes 196616 | tf_op jit(solution)/shard_map/ppermute | solution.py:33
  69.8 2.8 %collective-permute-start.17 = (f32[2,2,16,512]{3,2,1,0:T(8,128)S(1)}, f32[2,2,16,512]{3,2,1,0:T(8,128)S(1)}, u32[]{:S(2)}, u32[]{:S(2)}) collective-permute-start(f32[2,2,16,512]{3,2,1,0:T(8,128)S(1)} %pad_maximum_fusion.7.refs_0_), channel_id=1, source_target_pairs={{0,1},{1,0},{2,3},{3,2},{4,5},{5,4},{6,7},{7,6},{8,9},{9,8},{10,11... | collective-permute-start | bytes 393224 | tf_op jit(solution)/shard_map/ppermute | solution.py:33
  72.5 1.5 %collective-permute-start.20 = (f32[2,2,16,512]{3,2,1,0:T(8,128)S(1)}, f32[2,2,16,512]{3,2,1,0:T(8,128)S(1)}, u32[]{:S(2)}, u32[]{:S(2)}) collective-permute-start(f32[2,2,16,512]{3,2,1,0:T(8,128)S(1)} %pad_maximum_fusion.8.refs_2_), channel_id=1, source_target_pairs={{0,1},{1,0},{2,3},{3,2},{4,5},{5,4},{6,7},{7,6},{8,9},{9,8},{10,11... | collective-permute-start | bytes 393224 | tf_op jit(solution)/shard_map/ppermute | solution.py:33
  75.4 10.3 %all-to-all-start.1 = ((f32[16,2,16]{2,1,0:T(2,128)}), f32[16,2,16]{2,1,0:T(2,128)S(1)}, u32[]{:S(2)}, u32[]{:S(2)}) async-start(f32[16,2,16]{2,1,0:T(2,128)} %broadcast_in_dim.7), calls=%async_computation.1 | async-start | bytes 32768 | tf_op jit(solution)/shard_map/all_to_all | solution.py:20
  (3 other events, 32.6 us)

commit v8 on v4

--- a/solution.py
+++ b/solution.py
@@ -9,6 +9,7 @@
 
 BLK = 256
 STEPS = 3
+CHUNKS = 4
 LIMIT = 16 * 1024 * 1024
 VMEM = pl.BlockSpec(memory_space=pltpu.VMEM)
 SMEM = pl.BlockSpec(memory_space=pltpu.SMEM)
@@ -184,9 +185,9 @@
 
 
 def products_kernel(
-    count, token_hbm, state_hbm, allow_hbm, table_hbm, start_hbm, emission_ref,
-    sums_ref, kept_ref, sent_ref, state_ref, allow_ref, table_ref, messages_ref,
-    token_ref, columns_ref, sems,
+    count, token_hbm, state_hbm, allow_hbm, table_hbm, start_hbm, emission_hbm,
+    sums_ref, kept_ref, sent_ref, state_ref, allow_ref, table_ref, messages_ref, emission_ref,
+    token_ref, columns_ref, sems, chunk_sems,
 ):
     device = lax.axis_index("vocab")
     devices = 1 << count
@@ -199,7 +200,14 @@
     copies = [
         pltpu.make_async_copy(source, to, sems.at[k]) for k, (source, to) in enumerate(pairs)
     ]
-    for copy in copies:
+    size = emission_ref.shape[0] // CHUNKS
+    chunks = []
+    for k in range(CHUNKS):
+        span = pl.ds(k * size, size)
+        chunks.append(
+            pltpu.make_async_copy(emission_hbm.at[span], emission_ref.at[span], chunk_sems.at[k])
+        )
+    for copy in copies[:1] + chunks + copies[1:]:
         copy.start()
     shape = (devices * devices // 2, devices * devices)
     to, source = (lax.broadcasted_iota(jnp.int32, shape, axis) for axis in (0, 1))
@@ -215,6 +223,8 @@
     onehot = (tokens == lax.broadcasted_iota(jnp.int32, shape, 1)).astype(jnp.bfloat16)
     left = jnp.concatenate([onehot, jnp.ones((16, BLK), jnp.bfloat16)], axis=0)
     for k in range(devices):
+        if k * rows % size == 0:
+            chunks[k * rows // size].wait()
         product = dot_rows(left, emission_ref[pl.ds(k * rows, rows)])
         columns_ref[pl.ds(k * devices, devices)] = product[:devices].astype(jnp.bfloat16)
         sums_ref[k] = product[devices : devices + 1]
@@ -234,17 +244,19 @@
         functools.partial(products_kernel, count),
         out_shape=[jax.ShapeDtypeStruct((devices, 1, rows), jnp.float32), half, half]
         + [pltpu.VMEM(array.shape, array.dtype) for array in small]
-        + [pltpu.VMEM((beta_start.shape[1], rows), jnp.float32)],
-        in_specs=[ANY] * len(operands) + [VMEM],
-        out_specs=[VMEM] * 7,
+        + [pltpu.VMEM((beta_start.shape[1], rows), jnp.float32)]
+        + [pltpu.VMEM(emission.shape, emission.dtype)],
+        in_specs=[ANY] * (len(operands) + 1),
+        out_specs=[VMEM] * 8,
         scratch_shapes=[
             pltpu.SMEM(last_token.shape, jnp.int32),
             pltpu.VMEM((devices * devices, rows), jnp.bfloat16),
             pltpu.SemaphoreType.DMA((len(operands),)),
+            pltpu.SemaphoreType.DMA((CHUNKS,)),
         ],
         compiler_params=PARAMS,
         name="first_products",
-    )(*(in_hbm(operand) for operand in operands), emission)
+    )(*(in_hbm(operand) for operand in operands + (emission,)))
 
 
 def in_hbm(array):
@@ -498,10 +510,10 @@
     prompts = prompt_state.shape[0]
     count = devices.bit_length() - 1
     if devices == 1 << count and count > 2 and own_rows % 128 == 0 and prompts == devices:
-        sums, columns, columns_out, state, allow, table, messages = first_products(
+        sums, columns, columns_out, state, allow, table, messages, held = first_products(
             last_token, prompt_state, allow_list, trans_table, beta_start, emission, count
         )
-        route, chooser, sums = tables(state, allow, table, emission, sums, count)
+        route, chooser, sums = tables(state, allow, table, held, sums, count)
         sums = exchange(sums)
         parts, kept_rows, sent_rows = [messages], (columns,), (columns_out,)
         for window_step in range(STEPS):

time: 86 us -> 84.7 us (0.985)
  local copies, waits for them, and re-layouts: 3.87 us -> 1.54 us
  Pallas kernels: 13.6 us -> 14.5 us
    unnamed x10 -> x8, local copies, waits for them, and re-layouts: 2.35 us -> 0.02 us
    pallas_call x1, Pallas kernels: 2.38 us -> 3.35 us  [first_products(): pl.pallas_call(functools.partial(products_kernel, count), out_shape=[jax....]
where the time goes in v8:
time: 84.7 us; the launch traced here: 84.4 us
  waiting for transfers between devices  34.9 us (41%)
  starting transfers between devices  17.5 us (21%)
  Pallas kernels  14.5 us (17%)
  blocking collectives  13.8 us (16%)
  local copies, waits for them, and re-layouts  1.54 us (2%)
  other arithmetic  1.29 us (2%)
  between operations  0.91 us (1%)
    ppermute x20, waiting for transfers between devices, swap(): return lax.ppermute(block, 'vocab', pairs)  29 us
    ppermute x20, starting transfers between devices, swap(): return lax.ppermute(block, 'vocab', pairs)  14 us
    all_to_all x1, blocking collectives, exchange(): lax.all_to_all(blocks, 'vocab', split_axis=0, concat_axis=0, tiled=True)  13.8 us
    all_to_all x1, waiting for transfers between devices, exchange(): lax.all_to_all(blocks, 'vocab', split_axis=0, concat_axis=0, tiled=True)  5.84 us
    pallas_call x3, Pallas kernels, step(): pl.pallas_call(functools.partial(send_kernel, count, len(parts)), out_sha...  4.34 us
    pallas_call x3, Pallas kernels, step(): pl.pallas_call(functools.partial(keep_kernel, count), out_shape=pltpu.VME...  3.88 us
    all_to_all x1, starting transfers between devices, exchange(): lax.all_to_all(blocks, 'vocab', split_axis=0, concat_axis=0, tiled=True)  3.49 us
    pallas_call x1, Pallas kernels, first_products(): pl.pallas_call(functools.partial(products_kernel, count), out_shape=[jax....  3.35 us
  transfers between devices with their start and end apart: 21, of which 18 were waited for; matrix products, arithmetic and copies ran while one was open for 1% of the time, Pallas kernels for 6%

profile of v8, /device:TPU:0, one launch (start us, length us, event | category | flops | bytes accessed | tf_op | source)
XLA Modules:
  0.0 84.4 jit_solution(16212961229981428045)
XLA Ops:
  0.6 3.3 %first_products.1 = (f32[16,1,512]{2,1,0:T(1,128)S(1)}, bf16[4,2,16,512]{3,2,1,0:T(8,128)(2,1)S(1)}, bf16[4,2,16,512]{3,2,1,0:T(8,128)(2,1)S(1)}, s32[1,16]{1,0:...) custom-call(s32[16]{0:T(128)} %token_hbm.1, ...), custom_call_target="tpu_custom_call" | custom-call | tf_op jit(solution)/shard_map/first_products/pallas_call | solution.py:243
  4.4 13.8 %all_to_all.10.sums_ref = f32[16,1,512]{2,1,0:T(1,128)S(1)} all-to-all(f32[16,1,512]{2,1,0:T(1,128)S(1)} %get-tuple-element.27), channel_id=1, replica_groups=mesh['parts'=2,'vocab'=16] {'vocab'}, dimensions={0} | all-to-all | bytes 65536 | tf_op jit(solution)/shard_map/all_to_all | solution.py:21
  18.3 1.4 %step_sent_half.3 = (bf16[32,512]{1,0:T(8,128)(2,1)S(1)}, bf16[4,2,32,512]{3,2,1,0:T(8,128)(2,1)S(1)}) custom-call(bf16[8192,512]{1,0:T(8,128)(2,1)S(1)} %copy-done, bf16[256,48]{1,0:T(8,128)(2,1)S(1)} %get-tuple-element.26.route_ref, f32[16,1,512]{2,1,0:T(1,128)S(1)} %all_to_all.10.sums_ref, f32[16,512]{1,0:T(8,128)S(1)} %get-tuple-element.28.refs_0_, ...), custom_call_target="tpu_custom_call" | custom-call | tf_op jit(solution)/shard_map/step_sent_half/pallas_call | solution.py:394
  19.7 1.3 %step_kept_half.3 = f32[4,2,32,512]{3,2,1,0:T(8,128)S(1)} custom-call(bf16[8192,512]{1,0:T(8,128)(2,1)S(1)} %copy-done, bf16[32,512]{1,0:T(8,128)(2,1)S(1)} %get-tuple-element.30.halves_ref, bf16[4,2,16,512]{3,2,1,0:T(8,128)(2,1)S(1)} %get-tuple-element.31.refs_0_), custom_call_target="tpu_custom_call" | custom-call | tf_op jit(solution)/shard_map/step_kept_half/pallas_call | solution.py:406
  22.9 1.8 %collective-permute-start.2 = (bf16[64,512]{1,0:T(8,128)(2,1)S(1)}, bf16[64,512]{1,0:T(8,128)(2,1)S(1)}, u32[]{:S(2)}, u32[]{:S(2)}) collective-permute-start(bf16[64,512]{1,0:T(8,128)(2,1)S(1)} %bitcast.103), channel_id=1, source_target_pairs={{0,3},{1,2},{2,1},{3,0},{4,7},{5,6},{6,5},{7,4},{8,11},{9,10},{10,... | collective-permute-start | bytes 196616 | tf_op jit(solution)/shard_map/ppermute | solution.py:34
  24.7 2.6 %collective-permute-done.3 = bf16[64,512]{1,0:T(8,128)(2,1)S(1)} collective-permute-done((bf16[64,512]{1,0:T(8,128)(2,1)S(1)}, bf16[64,512]{1,0:T(8,128)(2,1)S(1)}, u32[]{:S(2)}, u32[]{:S(2)}) %collective-permute-start.3) | collective-permute-done | bytes 65568 | tf_op jit(solution)/shard_map/ppermute | solution.py:34
  28.0 5.0 %collective-permute-done.4.refs_1_ = bf16[32,512]{1,0:T(8,128)(2,1)S(1)} collective-permute-done((bf16[32,512]{1,0:T(8,128)(2,1)S(1)}, bf16[32,512]{1,0:T(8,128)(2,1)S(1)}, u32[]{:S(2)}, u32[]{:S(2)}) %collective-permute-start.4) | collective-permute-done | bytes 32800 | tf_op jit(solution)/shard_map/ppermute | solution.py:34
  33.0 1.5 %step_sent_half.4 = (bf16[32,512]{1,0:T(8,128)(2,1)S(1)}, bf16[4,2,16,512]{3,2,1,0:T(8,128)(2,1)S(1)}) custom-call(bf16[8192,512]{1,0:T(8,128)(2,1)S(1)} %copy-done, bf16[256,48]{1,0:T(8,128)(2,1)S(1)} %get-tuple-element.26.route_ref, f32[16,1,512]{2,1,0:T(1,128)S(1)} %all_to_all.10.sums_ref, f32[32,512]{1,0:T(8,128)S(1)} %slice_bitcast_fusion.2.refs_0_, ...), custom_call_target="tpu_custom_call" | custom-call | tf_op jit(solution)/shard_map/step_sent_half/pallas_call | solution.py:394
  34.6 1.3 %step_kept_half.4 = f32[4,2,16,512]{3,2,1,0:T(8,128)S(1)} custom-call(bf16[8192,512]{1,0:T(8,128)(2,1)S(1)} %copy-done, bf16[32,512]{1,0:T(8,128)(2,1)S(1)} %get-tuple-element.33.halves_ref), custom_call_target="tpu_custom_call" | custom-call | tf_op jit(solution)/shard_map/step_kept_half/pallas_call | solution.py:406
  36.1 1.6 %collective-permute-start.6 = (bf16[32,512]{1,0:T(8,128)(2,1)S(1)}, bf16[32,512]{1,0:T(8,128)(2,1)S(1)}, u32[]{:S(2)}, u32[]{:S(2)}) collective-permute-start(bf16[32,512]{1,0:T(8,128)(2,1)S(1)} %bitcast.114), channel_id=1, source_target_pairs={{0,5},{1,4},{2,7},{3,6},{4,1},{5,0},{6,3},{7,2},{8,13},{9,12},{10,... | collective-permute-start | bytes 98312 | tf_op jit(solution)/shard_map/ppermute | solution.py:34
  37.7 1.6 %collective-permute-start.7 = (bf16[32,512]{1,0:T(8,128)(2,1)S(1)}, bf16[32,512]{1,0:T(8,128)(2,1)S(1)}, u32[]{:S(2)}, u32[]{:S(2)}) collective-permute-start(bf16[32,512]{1,0:T(8,128)(2,1)S(1)} %bitcast.113), channel_id=1, source_target_pairs={{0,3},{1,2},{2,1},{3,0},{4,7},{5,6},{6,5},{7,4},{8,11},{9,10},{10,... | collective-permute-start | bytes 98312 | tf_op jit(solution)/shard_map/ppermute | solution.py:34
  39.4 1.7 %collective-permute-done.8 = bf16[32,512]{1,0:T(8,128)(2,1)S(1)} collective-permute-done((bf16[32,512]{1,0:T(8,128)(2,1)S(1)}, bf16[32,512]{1,0:T(8,128)(2,1)S(1)}, u32[]{:S(2)}, u32[]{:S(2)}) %collective-permute-start.8) | collective-permute-done | bytes 32800 | tf_op jit(solution)/shard_map/ppermute | solution.py:34
  41.4 5.0 %collective-permute-done.9.refs_1_ = bf16[32,512]{1,0:T(8,128)(2,1)S(1)} collective-permute-done((bf16[32,512]{1,0:T(8,128)(2,1)S(1)}, bf16[32,512]{1,0:T(8,128)(2,1)S(1)}, u32[]{:S(2)}, u32[]{:S(2)}) %collective-permute-start.9) | collective-permute-done | bytes 32800 | tf_op jit(solution)/shard_map/ppermute | solution.py:34
  46.4 1.4 %step_sent_half.5 = (bf16[32,512]{1,0:T(8,128)(2,1)S(1)}, f32[4,2,16,512]{3,2,1,0:T(8,128)S(1)}) custom-call(bf16[8192,512]{1,0:T(8,128)(2,1)S(1)} %copy-done, bf16[256,48]{1,0:T(8,128)(2,1)S(1)} %get-tuple-element.26.route_ref, f32[16,1,512]{2,1,0:T(1,128)S(1)} %all_to_all.10.sums_ref, f32[16,512]{1,0:T(8,128)S(1)} %slice_bitcast_fusion.4.refs_0_, ...), custom_call_target="tpu_custom_call" | custom-call | tf_op jit(solution)/shard_map/step_sent_half/pallas_call | solution.py:394
  48.0 1.3 %step_kept_half.5 = f32[4,2,16,512]{3,2,1,0:T(8,128)S(1)} custom-call(bf16[8192,512]{1,0:T(8,128)(2,1)S(1)} %copy-done, bf16[32,512]{1,0:T(8,128)(2,1)S(1)} %get-tuple-element.35.halves_ref), custom_call_target="tpu_custom_call" | custom-call | tf_op jit(solution)/shard_map/step_kept_half/pallas_call | solution.py:406
  50.8 2.0 %collective-permute-start.13 = (bf16[96,512]{1,0:T(8,128)(2,1)S(1)}, bf16[96,512]{1,0:T(8,128)(2,1)S(1)}, u32[]{:S(2)}, u32[]{:S(2)}) collective-permute-start(bf16[96,512]{1,0:T(8,128)(2,1)S(1)} %get-tuple-element.67), channel_id=1, source_target_pairs={{0,6},{1,7},{2,4},{3,5},{4,2},{5,3},{6,0},{7,1},{8,14},{9,15},{10,... | collective-permute-start | bytes 294920 | tf_op jit(solution)/shard_map/ppermute | solution.py:34
  52.9 1.5 %collective-permute-done.11 = bf16[96,512]{1,0:T(8,128)(2,1)S(1)} collective-permute-done((bf16[96,512]{1,0:T(8,128)(2,1)S(1)}, bf16[96,512]{1,0:T(8,128)(2,1)S(1)}, u32[]{:S(2)}, u32[]{:S(2)}) %collective-permute-start.11) | collective-permute-done | bytes 98336 | tf_op jit(solution)/shard_map/ppermute | solution.py:34
  54.4 3.1 %collective-permute-done.13 = bf16[96,512]{1,0:T(8,128)(2,1)S(1)} collective-permute-done((bf16[96,512]{1,0:T(8,128)(2,1)S(1)}, bf16[96,512]{1,0:T(8,128)(2,1)S(1)}, u32[]{:S(2)}, u32[]{:S(2)}) %collective-permute-start.13) | collective-permute-done | bytes 98336 | tf_op jit(solution)/shard_map/ppermute | solution.py:34
  57.8 1.3 %collective-permute-done.15.far_ref = bf16[4,2,16,512]{3,2,1,0:T(8,128)(2,1)S(1)} collective-permute-done((bf16[4,2,16,512]{3,2,1,0:T(8,128)(2,1)S(1)}, bf16[4,2,16,512]{3,2,1,0:T(8,128)(2,1)S(1)}, u32[]{:S(2)}, u32[]{:S(2)}) %collective-permute-start.15) | collective-permute-done | bytes 131104 | tf_op jit(solution)/shard_map/ppermute | solution.py:34
  59.4 4.8 %collective-permute-done.14.refs_0_ = bf16[64,512]{1,0:T(8,128)(2,1)S(1)} collective-permute-done((bf16[64,512]{1,0:T(8,128)(2,1)S(1)}, bf16[64,512]{1,0:T(8,128)(2,1)S(1)}, u32[]{:S(2)}, u32[]{:S(2)}) %collective-permute-start.14) | collective-permute-done | bytes 65568 | tf_op jit(solution)/shard_map/ppermute | solution.py:34
  64.8 2.7 %collective-permute-start.16 = (f32[2,16,512]{2,1,0:T(8,128)S(1)}, f32[2,16,512]{2,1,0:T(8,128)S(1)}, u32[]{:S(2)}, u32[]{:S(2)}) collective-permute-start(f32[2,16,512]{2,1,0:T(8,128)S(1)} %last_messages.1), channel_id=1, source_target_pairs={{0,5},{1,4},{2,7},{3,6},{4,1},{5,0},{6,3},{7,2},{8,13},{9,12},{10,... | collective-permute-start | bytes 196616 | tf_op jit(solution)/shard_map/ppermute | solution.py:34
  67.5 2.4 %collective-permute-done.18 = f32[2,16,512]{2,1,0:T(8,128)S(1)} collective-permute-done((f32[2,16,512]{2,1,0:T(8,128)S(1)}, f32[2,16,512]{2,1,0:T(8,128)S(1)}, u32[]{:S(2)}, u32[]{:S(2)}) %collective-permute-start.18) | collective-permute-done | bytes 65568 | tf_op jit(solution)/shard_map/ppermute | solution.py:34
  73.5 3.5 %all-to-all-start.1 = ((f32[16,2,16]{2,1,0:T(2,128)}), f32[16,2,16]{2,1,0:T(2,128)S(1)}, u32[]{:S(2)}, u32[]{:S(2)}) async-start(f32[16,2,16]{2,1,0:T(2,128)} %broadcast_in_dim.7), calls=%async_computation.1 | async-start | bytes 32768 | tf_op jit(solution)/shard_map/all_to_all | solution.py:21
  77.6 5.8 %all-to-all-done.1 = f32[16,2,16]{2,1,0:T(2,128)S(1)} async-done(((f32[16,2,16]{2,1,0:T(2,128)}), f32[16,2,16]{2,1,0:T(2,128)S(1)}, u32[]{:S(2)}, u32[]{:S(2)}) %all-to-all-start.1) | async-done | bytes 2080 | tf_op jit(solution)/shard_map/all_to_all | solution.py:21
  (77 shorter events, 11.8 us)
Async XLA Ops:
  0.6 17.6 %copy-start = (bf16[8192,512]{1,0:T(8,128)(2,1)S(1)}, bf16[8192,512]{1,0:T(8,128)(2,1)}, u32[]{:S(2)}) copy-start(bf16[8192,512]{1,0:T(8,128)(2,1)} %transition_ref.11) | copy-start | bytes 25165828
  19.7 1.6 %collective-permute-start = (bf16[4,2,32,512]{3,2,1,0:T(8,128)(2,1)S(1)}, bf16[4,2,32,512]{3,2,1,0:T(8,128)(2,1)S(1)}, u32[]{:S(2)}, u32[]{:S(2)}) collective-permute-start(bf16[4,2,32,512]{3,2,1,0:T(8,128)(2,1)S(1)} %get-tuple-element.32), channel_id=1, source_target_pairs={{0,1},{1,0},{2,3},{3,2},{4,5},{5,4},{6,7},{7,6},{8,9},{9,8},{10,11... | collective-permute-start | bytes 786440 | tf_op jit(solution)/shard_map/ppermute | solution.py:34
  21.4 5.9 %collective-permute-start.3 = (bf16[64,512]{1,0:T(8,128)(2,1)S(1)}, bf16[64,512]{1,0:T(8,128)(2,1)S(1)}, u32[]{:S(2)}, u32[]{:S(2)}) collective-permute-start(bf16[64,512]{1,0:T(8,128)(2,1)S(1)} %bitcast.105), channel_id=1, source_target_pairs={{0,6},{1,7},{2,4},{3,5},{4,2},{5,3},{6,0},{7,1},{8,14},{9,15},{10,... | collective-permute-start | bytes 196616 | tf_op jit(solution)/shard_map/ppermute | solution.py:34
  21.8 5.4 %collective-permute-start.1 = (bf16[64,512]{1,0:T(8,128)(2,1)S(1)}, bf16[64,512]{1,0:T(8,128)(2,1)S(1)}, u32[]{:S(2)}, u32[]{:S(2)}) collective-permute-start(bf16[64,512]{1,0:T(8,128)(2,1)S(1)} %bitcast.104), channel_id=1, source_target_pairs={{0,5},{1,4},{2,7},{3,6},{4,1},{5,0},{6,3},{7,2},{8,13},{9,12},{10,... | collective-permute-start | bytes 196616 | tf_op jit(solution)/shard_map/ppermute | solution.py:34
  22.9 4.9 %collective-permute-start.2 = (bf16[64,512]{1,0:T(8,128)(2,1)S(1)}, bf16[64,512]{1,0:T(8,128)(2,1)S(1)}, u32[]{:S(2)}, u32[]{:S(2)}) collective-permute-start(bf16[64,512]{1,0:T(8,128)(2,1)S(1)} %bitcast.103), channel_id=1, source_target_pairs={{0,3},{1,2},{2,1},{3,0},{4,7},{5,6},{6,5},{7,4},{8,11},{9,10},{10,... | collective-permute-start | bytes 196616 | tf_op jit(solution)/shard_map/ppermute | solution.py:34
  27.8 5.2 %collective-permute-start.4 = (bf16[32,512]{1,0:T(8,128)(2,1)S(1)}, bf16[32,512]{1,0:T(8,128)(2,1)S(1)}, u32[]{:S(2)}, u32[]{:S(2)}) collective-permute-start(bf16[32,512]{1,0:T(8,128)(2,1)S(1)} %fusion.14), channel_id=1, source_target_pairs={{0,9},{1,8},{2,11},{3,10},{4,13},{5,12},{6,15},{7,14},{8,1},{9,0},... | collective-permute-start | bytes 98312 | tf_op jit(solution)/shard_map/ppermute | solution.py:34
  34.5 1.4 %collective-permute-start.5 = (bf16[4,2,16,512]{3,2,1,0:T(8,128)(2,1)S(1)}, bf16[4,2,16,512]{3,2,1,0:T(8,128)(2,1)S(1)}, u32[]{:S(2)}, u32[]{:S(2)}) collective-permute-start(bf16[4,2,16,512]{3,2,1,0:T(8,128)(2,1)S(1)} %get-tuple-element.34), channel_id=1, source_target_pairs={{0,1},{1,0},{2,3},{3,2},{4,5},{5,4},{6,7},{7,6},{8,9},{9,8},{10,11... | collective-permute-start | bytes 393224 | tf_op jit(solution)/shard_map/ppermute | solution.py:34
  36.0 5.1 %collective-permute-start.8 = (bf16[32,512]{1,0:T(8,128)(2,1)S(1)}, bf16[32,512]{1,0:T(8,128)(2,1)S(1)}, u32[]{:S(2)}, u32[]{:S(2)}) collective-permute-start(bf16[32,512]{1,0:T(8,128)(2,1)S(1)} %bitcast.115), channel_id=1, source_target_pairs={{0,6},{1,7},{2,4},{3,5},{4,2},{5,3},{6,0},{7,1},{8,14},{9,15},{10,... | collective-permute-start | bytes 98312 | tf_op jit(solution)/shard_map/ppermute | solution.py:34
  36.1 5.0 %collective-permute-start.6 = (bf16[32,512]{1,0:T(8,128)(2,1)S(1)}, bf16[32,512]{1,0:T(8,128)(2,1)S(1)}, u32[]{:S(2)}, u32[]{:S(2)}) collective-permute-start(bf16[32,512]{1,0:T(8,128)(2,1)S(1)} %bitcast.114), channel_id=1, source_target_pairs={{0,5},{1,4},{2,7},{3,6},{4,1},{5,0},{6,3},{7,2},{8,13},{9,12},{10,... | collective-permute-start | bytes 98312 | tf_op jit(solution)/shard_map/ppermute | solution.py:34
  37.7 3.6 %collective-permute-start.7 = (bf16[32,512]{1,0:T(8,128)(2,1)S(1)}, bf16[32,512]{1,0:T(8,128)(2,1)S(1)}, u32[]{:S(2)}, u32[]{:S(2)}) collective-permute-start(bf16[32,512]{1,0:T(8,128)(2,1)S(1)} %bitcast.113), channel_id=1, source_target_pairs={{0,3},{1,2},{2,1},{3,0},{4,7},{5,6},{6,5},{7,4},{8,11},{9,10},{10,... | collective-permute-start | bytes 98312 | tf_op jit(solution)/shard_map/ppermute | solution.py:34
  41.3 5.1 %collective-permute-start.9 = (bf16[32,512]{1,0:T(8,128)(2,1)S(1)}, bf16[32,512]{1,0:T(8,128)(2,1)S(1)}, u32[]{:S(2)}, u32[]{:S(2)}) collective-permute-start(bf16[32,512]{1,0:T(8,128)(2,1)S(1)} %pad_maximum_fusion.9), channel_id=1, source_target_pairs={{0,9},{1,8},{2,11},{3,10},{4,13},{5,12},{6,15},{7,14},{8,1},{9,0},... | collective-permute-start | bytes 98312 | tf_op jit(solution)/shard_map/ppermute | solution.py:34
  47.9 1.6 %collective-permute-start.10 = (f32[4,2,16,512]{3,2,1,0:T(8,128)S(1)}, f32[4,2,16,512]{3,2,1,0:T(8,128)S(1)}, u32[]{:S(2)}, u32[]{:S(2)}) collective-permute-start(f32[4,2,16,512]{3,2,1,0:T(8,128)S(1)} %get-tuple-element.36), channel_id=1, source_target_pairs={{0,1},{1,0},{2,3},{3,2},{4,5},{5,4},{6,7},{7,6},{8,9},{9,8},{10,11... | collective-permute-start | bytes 786440 | tf_op jit(solution)/shard_map/ppermute | solution.py:34
  49.3 21.0 %copy-start.1 = (bf16[8192,256]{1,0:T(8,128)(2,1)S(1)}, bf16[8192,256]{1,0:T(8,128)(2,1)}, u32[]{:S(2)}) copy-start(bf16[8192,256]{1,0:T(8,128)(2,1)} %emission_ref.3) | copy-start | bytes 12582916
  49.5 22.2 %copy-start.3 = (bf16[16,256]{1,0:T(8,128)(2,1)S(1)}, bf16[16,256]{1,0:T(8,128)(2,1)}, u32[]{:S(2)}) copy-start(bf16[16,256]{1,0:T(8,128)(2,1)} %logits_ref.1) | copy-start | bytes 24580
  49.6 4.8 %collective-permute-start.11 = (bf16[96,512]{1,0:T(8,128)(2,1)S(1)}, bf16[96,512]{1,0:T(8,128)(2,1)S(1)}, u32[]{:S(2)}, u32[]{:S(2)}) collective-permute-start(bf16[96,512]{1,0:T(8,128)(2,1)S(1)} %get-tuple-element.65), channel_id=1, source_target_pairs={{0,5},{1,4},{2,7},{3,6},{4,1},{5,0},{6,3},{7,2},{8,13},{9,12},{10,... | collective-permute-start | bytes 294920 | tf_op jit(solution)/shard_map/ppermute | solution.py:34
  49.7 4.8 %collective-permute-start.12 = (bf16[96,512]{1,0:T(8,128)(2,1)S(1)}, bf16[96,512]{1,0:T(8,128)(2,1)S(1)}, u32[]{:S(2)}, u32[]{:S(2)}) collective-permute-start(bf16[96,512]{1,0:T(8,128)(2,1)S(1)} %get-tuple-element.66), channel_id=1, source_target_pairs={{0,3},{1,2},{2,1},{3,0},{4,7},{5,6},{6,5},{7,4},{8,11},{9,10},{10,... | collective-permute-start | bytes 294920 | tf_op jit(solution)/shard_map/ppermute | solution.py:34
  50.8 6.7 %collective-permute-start.13 = (bf16[96,512]{1,0:T(8,128)(2,1)S(1)}, bf16[96,512]{1,0:T(8,128)(2,1)S(1)}, u32[]{:S(2)}, u32[]{:S(2)}) collective-permute-start(bf16[96,512]{1,0:T(8,128)(2,1)S(1)} %get-tuple-element.67), channel_id=1, source_target_pairs={{0,6},{1,7},{2,4},{3,5},{4,2},{5,3},{6,0},{7,1},{8,14},{9,15},{10,... | collective-permute-start | bytes 294920 | tf_op jit(solution)/shard_map/ppermute | solution.py:34
  57.5 6.7 %collective-permute-start.14 = (bf16[64,512]{1,0:T(8,128)(2,1)S(1)}, bf16[64,512]{1,0:T(8,128)(2,1)S(1)}, u32[]{:S(2)}, u32[]{:S(2)}) collective-permute-start(bf16[64,512]{1,0:T(8,128)(2,1)S(1)} %pad_maximum_fusion.8), channel_id=1, source_target_pairs={{0,9},{1,8},{2,11},{3,10},{4,13},{5,12},{6,15},{7,14},{8,1},{9,0},... | collective-permute-start | bytes 196616 | tf_op jit(solution)/shard_map/ppermute | solution.py:34
  57.7 1.4 %collective-permute-start.15 = (bf16[4,2,16,512]{3,2,1,0:T(8,128)(2,1)S(1)}, bf16[4,2,16,512]{3,2,1,0:T(8,128)(2,1)S(1)}, u32[]{:S(2)}, u32[]{:S(2)}) collective-permute-start(bf16[4,2,16,512]{3,2,1,0:T(8,128)(2,1)S(1)} %pad_maximum_fusion.7.near_ref), channel_id=1, source_target_pairs={{0,1},{1,0},{2,3},{3,2},{4,5},{5,4},{6,7},{7,6},{8,9},{9,8},{10,11... | collective-permute-start | bytes 393224 | tf_op jit(solution)/shard_map/ppermute | solution.py:34
  64.2 5.7 %collective-permute-start.18 = (f32[2,16,512]{2,1,0:T(8,128)S(1)}, f32[2,16,512]{2,1,0:T(8,128)S(1)}, u32[]{:S(2)}, u32[]{:S(2)}) collective-permute-start(f32[2,16,512]{2,1,0:T(8,128)S(1)} %last_messages.1), channel_id=1, source_target_pairs={{0,6},{1,7},{2,4},{3,5},{4,2},{5,3},{6,0},{7,1},{8,14},{9,15},{10,... | collective-permute-start | bytes 196616 | tf_op jit(solution)/shard_map/ppermute | solution.py:34
  64.4 5.6 %collective-permute-start.17 = (f32[2,16,512]{2,1,0:T(8,128)S(1)}, f32[2,16,512]{2,1,0:T(8,128)S(1)}, u32[]{:S(2)}, u32[]{:S(2)}) collective-permute-start(f32[2,16,512]{2,1,0:T(8,128)S(1)} %last_messages.1), channel_id=1, source_target_pairs={{0,3},{1,2},{2,1},{3,0},{4,7},{5,6},{6,5},{7,4},{8,11},{9,10},{10,... | collective-permute-start | bytes 196616 | tf_op jit(solution)/shard_map/ppermute | solution.py:34
  64.8 5.3 %collective-permute-start.16 = (f32[2,16,512]{2,1,0:T(8,128)S(1)}, f32[2,16,512]{2,1,0:T(8,128)S(1)}, u32[]{:S(2)}, u32[]{:S(2)}) collective-permute-start(f32[2,16,512]{2,1,0:T(8,128)S(1)} %last_messages.1), channel_id=1, source_target_pairs={{0,5},{1,4},{2,7},{3,6},{4,1},{5,0},{6,3},{7,2},{8,13},{9,12},{10,... | collective-permute-start | bytes 196616 | tf_op jit(solution)/shard_map/ppermute | solution.py:34
  70.1 1.6 %collective-permute-start.19 = (f32[4,2,16,512]{3,2,1,0:T(8,128)S(1)}, f32[4,2,16,512]{3,2,1,0:T(8,128)S(1)}, u32[]{:S(2)}, u32[]{:S(2)}) collective-permute-start(f32[4,2,16,512]{3,2,1,0:T(8,128)S(1)} %pad_maximum_fusion.parts_ref), channel_id=1, source_target_pairs={{0,1},{1,0},{2,3},{3,2},{4,5},{5,4},{6,7},{7,6},{8,9},{9,8},{10,11... | collective-permute-start | bytes 786440 | tf_op jit(solution)/shard_map/ppermute | solution.py:34
  73.5 10.0 %all-to-all-start.1 = ((f32[16,2,16]{2,1,0:T(2,128)}), f32[16,2,16]{2,1,0:T(2,128)S(1)}, u32[]{:S(2)}, u32[]{:S(2)}) async-start(f32[16,2,16]{2,1,0:T(2,128)} %broadcast_in_dim.7), calls=%async_computation.1 | async-start | bytes 32768 | tf_op jit(solution)/shard_map/all_to_all | solution.py:21
  (1 other events, 4.6 us)

commit v9 on v8

--- a/solution.py
+++ b/solution.py
@@ -9,7 +9,7 @@
 
 BLK = 256
 STEPS = 3
-CHUNKS = 4
+CUTS = (0, 6, 12, 15, 16)
 LIMIT = 16 * 1024 * 1024
 VMEM = pl.BlockSpec(memory_space=pltpu.VMEM)
 SMEM = pl.BlockSpec(memory_space=pltpu.SMEM)
@@ -128,11 +128,11 @@
     return near, swap(near, 1, devices)
 
 
-def column_of(scalars_ref, shape):
+def column_of(scalars_ref, shape, order):
     row = lax.broadcasted_iota(jnp.int32, shape, 0)
     column = jnp.zeros(shape, jnp.int32)
-    for k in range(shape[0]):
-        column = jnp.where(row == k, scalars_ref[k], column)
+    for k, place in enumerate(order):
+        column = jnp.where(row == k, scalars_ref[place], column)
     return column
 
 
@@ -200,31 +200,33 @@
     copies = [
         pltpu.make_async_copy(source, to, sems.at[k]) for k, (source, to) in enumerate(pairs)
     ]
-    size = emission_ref.shape[0] // CHUNKS
-    chunks = []
-    for k in range(CHUNKS):
-        span = pl.ds(k * size, size)
-        chunks.append(
-            pltpu.make_async_copy(emission_hbm.at[span], emission_ref.at[span], chunk_sems.at[k])
-        )
-    for copy in copies[:1] + chunks + copies[1:]:
+    chunks = {}
+    cuts = [cut * devices // CUTS[-1] for cut in CUTS]
+    for k, (low, high) in enumerate(zip(cuts, cuts[1:])):
+        span = pl.ds(low * rows, (high - low) * rows)
+        if high > low:
+            chunks[low] = pltpu.make_async_copy(
+                emission_hbm.at[span], emission_ref.at[span], chunk_sems.at[k]
+            )
+    for copy in copies[:1] + list(chunks.values()) + copies[1:]:
         copy.start()
     shape = (devices * devices // 2, devices * devices)
     to, source = (lax.broadcasted_iota(jnp.int32, shape, axis) for axis in (0, 1))
     same_block = (to & (devices - 1)) == (source >> count)
     orders = []
     for first in range(2):
-        prompt = partner_at((to >> count) + first * (devices // 2), count)
+        prompt = (to >> count) + first * (devices // 2)
         onehot = same_block & ((source & (devices - 1)) == prompt)
         orders.append(onehot.astype(jnp.bfloat16))
     copies[0].wait()
     shape = (devices, BLK)
-    tokens = column_of(token_ref, shape) - device * BLK
+    partners = [partner for first in range(2) for _, partner in half_places(count, first)]
+    tokens = column_of(token_ref, shape, [device ^ partner for partner in partners]) - device * BLK
     onehot = (tokens == lax.broadcasted_iota(jnp.int32, shape, 1)).astype(jnp.bfloat16)
     left = jnp.concatenate([onehot, jnp.ones((16, BLK), jnp.bfloat16)], axis=0)
     for k in range(devices):
-        if k * rows % size == 0:
-            chunks[k * rows // size].wait()
+        if k in chunks:
+            chunks[k].wait()
         product = dot_rows(left, emission_ref[pl.ds(k * rows, rows)])
         columns_ref[pl.ds(k * devices, devices)] = product[:devices].astype(jnp.bfloat16)
         sums_ref[k] = product[devices : devices + 1]
@@ -252,7 +254,7 @@
             pltpu.SMEM(last_token.shape, jnp.int32),
             pltpu.VMEM((devices * devices, rows), jnp.bfloat16),
             pltpu.SemaphoreType.DMA((len(operands),)),
-            pltpu.SemaphoreType.DMA((CHUNKS,)),
+            pltpu.SemaphoreType.DMA((len(CUTS) - 1,)),
         ],
         compiler_params=PARAMS,
         name="first_products",

time: 84.7 us -> 84.9 us (level)
  no operation moved by 1% of the time
where the time goes in v9:
time: 84.9 us; the launch traced here: 84.6 us
  waiting for transfers between devices  34.9 us (41%)
  starting transfers between devices  17.5 us (21%)
  Pallas kernels  14.7 us (17%)
  blocking collectives  13.8 us (16%)
  local copies, waits for them, and re-layouts  1.54 us (2%)
  other arithmetic  1.29 us (2%)
  between operations  0.91 us (1%)
    ppermute x20, waiting for transfers between devices, swap(): return lax.ppermute(block, 'vocab', pairs)  29.1 us
    ppermute x20, starting transfers between devices, swap(): return lax.ppermute(block, 'vocab', pairs)  14 us
    all_to_all x1, blocking collectives, exchange(): lax.all_to_all(blocks, 'vocab', split_axis=0, concat_axis=0, tiled=True)  13.8 us
    all_to_all x1, waiting for transfers between devices, exchange(): lax.all_to_all(blocks, 'vocab', split_axis=0, concat_axis=0, tiled=True)  5.84 us
    pallas_call x3, Pallas kernels, step(): pl.pallas_call(functools.partial(send_kernel, count, len(parts)), out_sha...  4.34 us
    pallas_call x3, Pallas kernels, step(): pl.pallas_call(functools.partial(keep_kernel, count), out_shape=pltpu.VME...  3.88 us
    pallas_call x1, Pallas kernels, first_products(): pl.pallas_call(functools.partial(products_kernel, count), out_shape=[jax....  3.53 us
    all_to_all x1, starting transfers between devices, exchange(): lax.all_to_all(blocks, 'vocab', split_axis=0, concat_axis=0, tiled=True)  3.49 us
  transfers between devices with their start and end apart: 21, of which 18 were waited for; matrix products, arithmetic and copies ran while one was open for 1% of the time, Pallas kernels for 6%

profile of v9, /device:TPU:0, one launch (start us, length us, event | category | flops | bytes accessed | tf_op | source)
XLA Modules:
  0.0 84.6 jit_solution(12441046679582447099)
XLA Ops:
  0.6 3.5 %first_products.1 = (f32[16,1,512]{2,1,0:T(1,128)S(1)}, bf16[4,2,16,512]{3,2,1,0:T(8,128)(2,1)S(1)}, bf16[4,2,16,512]{3,2,1,0:T(8,128)(2,1)S(1)}, s32[1,16]{1,0:...) custom-call(s32[16]{0:T(128)} %token_hbm.1, ...), custom_call_target="tpu_custom_call" | custom-call | tf_op jit(solution)/shard_map/first_products/pallas_call | solution.py:245
  4.6 13.8 %all_to_all.10.sums_ref = f32[16,1,512]{2,1,0:T(1,128)S(1)} all-to-all(f32[16,1,512]{2,1,0:T(1,128)S(1)} %get-tuple-element.27), channel_id=1, replica_groups=mesh['parts'=2,'vocab'=16] {'vocab'}, dimensions={0} | all-to-all | bytes 65536 | tf_op jit(solution)/shard_map/all_to_all | solution.py:21
  18.4 1.4 %step_sent_half.3 = (bf16[32,512]{1,0:T(8,128)(2,1)S(1)}, bf16[4,2,32,512]{3,2,1,0:T(8,128)(2,1)S(1)}) custom-call(bf16[8192,512]{1,0:T(8,128)(2,1)S(1)} %copy-done, bf16[256,48]{1,0:T(8,128)(2,1)S(1)} %get-tuple-element.26.route_ref, f32[16,1,512]{2,1,0:T(1,128)S(1)} %all_to_all.10.sums_ref, f32[16,512]{1,0:T(8,128)S(1)} %get-tuple-element.28.refs_0_, ...), custom_call_target="tpu_custom_call" | custom-call | tf_op jit(solution)/shard_map/step_sent_half/pallas_call | solution.py:396
  19.9 1.3 %step_kept_half.3 = f32[4,2,32,512]{3,2,1,0:T(8,128)S(1)} custom-call(bf16[8192,512]{1,0:T(8,128)(2,1)S(1)} %copy-done, bf16[32,512]{1,0:T(8,128)(2,1)S(1)} %get-tuple-element.30.halves_ref, bf16[4,2,16,512]{3,2,1,0:T(8,128)(2,1)S(1)} %get-tuple-element.31.refs_0_), custom_call_target="tpu_custom_call" | custom-call | tf_op jit(solution)/shard_map/step_kept_half/pallas_call | solution.py:408
  23.0 1.8 %collective-permute-start.2 = (bf16[64,512]{1,0:T(8,128)(2,1)S(1)}, bf16[64,512]{1,0:T(8,128)(2,1)S(1)}, u32[]{:S(2)}, u32[]{:S(2)}) collective-permute-start(bf16[64,512]{1,0:T(8,128)(2,1)S(1)} %bitcast.103), channel_id=1, source_target_pairs={{0,3},{1,2},{2,1},{3,0},{4,7},{5,6},{6,5},{7,4},{8,11},{9,10},{10,... | collective-permute-start | bytes 196616 | tf_op jit(solution)/shard_map/ppermute | solution.py:34
  24.8 2.6 %collective-permute-done.3 = bf16[64,512]{1,0:T(8,128)(2,1)S(1)} collective-permute-done((bf16[64,512]{1,0:T(8,128)(2,1)S(1)}, bf16[64,512]{1,0:T(8,128)(2,1)S(1)}, u32[]{:S(2)}, u32[]{:S(2)}) %collective-permute-start.3) | collective-permute-done | bytes 65568 | tf_op jit(solution)/shard_map/ppermute | solution.py:34
  28.2 5.0 %collective-permute-done.4.refs_1_ = bf16[32,512]{1,0:T(8,128)(2,1)S(1)} collective-permute-done((bf16[32,512]{1,0:T(8,128)(2,1)S(1)}, bf16[32,512]{1,0:T(8,128)(2,1)S(1)}, u32[]{:S(2)}, u32[]{:S(2)}) %collective-permute-start.4) | collective-permute-done | bytes 32800 | tf_op jit(solution)/shard_map/ppermute | solution.py:34
  33.2 1.4 %step_sent_half.4 = (bf16[32,512]{1,0:T(8,128)(2,1)S(1)}, bf16[4,2,16,512]{3,2,1,0:T(8,128)(2,1)S(1)}) custom-call(bf16[8192,512]{1,0:T(8,128)(2,1)S(1)} %copy-done, bf16[256,48]{1,0:T(8,128)(2,1)S(1)} %get-tuple-element.26.route_ref, f32[16,1,512]{2,1,0:T(1,128)S(1)} %all_to_all.10.sums_ref, f32[32,512]{1,0:T(8,128)S(1)} %slice_bitcast_fusion.2.refs_0_, ...), custom_call_target="tpu_custom_call" | custom-call | tf_op jit(solution)/shard_map/step_sent_half/pallas_call | solution.py:396
  34.8 1.3 %step_kept_half.4 = f32[4,2,16,512]{3,2,1,0:T(8,128)S(1)} custom-call(bf16[8192,512]{1,0:T(8,128)(2,1)S(1)} %copy-done, bf16[32,512]{1,0:T(8,128)(2,1)S(1)} %get-tuple-element.33.halves_ref), custom_call_target="tpu_custom_call" | custom-call | tf_op jit(solution)/shard_map/step_kept_half/pallas_call | solution.py:408
  36.3 1.6 %collective-permute-start.6 = (bf16[32,512]{1,0:T(8,128)(2,1)S(1)}, bf16[32,512]{1,0:T(8,128)(2,1)S(1)}, u32[]{:S(2)}, u32[]{:S(2)}) collective-permute-start(bf16[32,512]{1,0:T(8,128)(2,1)S(1)} %bitcast.114), channel_id=1, source_target_pairs={{0,5},{1,4},{2,7},{3,6},{4,1},{5,0},{6,3},{7,2},{8,13},{9,12},{10,... | collective-permute-start | bytes 98312 | tf_op jit(solution)/shard_map/ppermute | solution.py:34
  37.9 1.6 %collective-permute-start.7 = (bf16[32,512]{1,0:T(8,128)(2,1)S(1)}, bf16[32,512]{1,0:T(8,128)(2,1)S(1)}, u32[]{:S(2)}, u32[]{:S(2)}) collective-permute-start(bf16[32,512]{1,0:T(8,128)(2,1)S(1)} %bitcast.113), channel_id=1, source_target_pairs={{0,3},{1,2},{2,1},{3,0},{4,7},{5,6},{6,5},{7,4},{8,11},{9,10},{10,... | collective-permute-start | bytes 98312 | tf_op jit(solution)/shard_map/ppermute | solution.py:34
  39.6 1.7 %collective-permute-done.8 = bf16[32,512]{1,0:T(8,128)(2,1)S(1)} collective-permute-done((bf16[32,512]{1,0:T(8,128)(2,1)S(1)}, bf16[32,512]{1,0:T(8,128)(2,1)S(1)}, u32[]{:S(2)}, u32[]{:S(2)}) %collective-permute-start.8) | collective-permute-done | bytes 32800 | tf_op jit(solution)/shard_map/ppermute | solution.py:34
  41.6 5.0 %collective-permute-done.9.refs_1_ = bf16[32,512]{1,0:T(8,128)(2,1)S(1)} collective-permute-done((bf16[32,512]{1,0:T(8,128)(2,1)S(1)}, bf16[32,512]{1,0:T(8,128)(2,1)S(1)}, u32[]{:S(2)}, u32[]{:S(2)}) %collective-permute-start.9) | collective-permute-done | bytes 32800 | tf_op jit(solution)/shard_map/ppermute | solution.py:34
  46.6 1.4 %step_sent_half.5 = (bf16[32,512]{1,0:T(8,128)(2,1)S(1)}, f32[4,2,16,512]{3,2,1,0:T(8,128)S(1)}) custom-call(bf16[8192,512]{1,0:T(8,128)(2,1)S(1)} %copy-done, bf16[256,48]{1,0:T(8,128)(2,1)S(1)} %get-tuple-element.26.route_ref, f32[16,1,512]{2,1,0:T(1,128)S(1)} %all_to_all.10.sums_ref, f32[16,512]{1,0:T(8,128)S(1)} %slice_bitcast_fusion.4.refs_0_, ...), custom_call_target="tpu_custom_call" | custom-call | tf_op jit(solution)/shard_map/step_sent_half/pallas_call | solution.py:396
  48.2 1.3 %step_kept_half.5 = f32[4,2,16,512]{3,2,1,0:T(8,128)S(1)} custom-call(bf16[8192,512]{1,0:T(8,128)(2,1)S(1)} %copy-done, bf16[32,512]{1,0:T(8,128)(2,1)S(1)} %get-tuple-element.35.halves_ref), custom_call_target="tpu_custom_call" | custom-call | tf_op jit(solution)/shard_map/step_kept_half/pallas_call | solution.py:408
  51.0 2.0 %collective-permute-start.13 = (bf16[96,512]{1,0:T(8,128)(2,1)S(1)}, bf16[96,512]{1,0:T(8,128)(2,1)S(1)}, u32[]{:S(2)}, u32[]{:S(2)}) collective-permute-start(bf16[96,512]{1,0:T(8,128)(2,1)S(1)} %get-tuple-element.67), channel_id=1, source_target_pairs={{0,6},{1,7},{2,4},{3,5},{4,2},{5,3},{6,0},{7,1},{8,14},{9,15},{10,... | collective-permute-start | bytes 294920 | tf_op jit(solution)/shard_map/ppermute | solution.py:34
  53.1 1.5 %collective-permute-done.11 = bf16[96,512]{1,0:T(8,128)(2,1)S(1)} collective-permute-done((bf16[96,512]{1,0:T(8,128)(2,1)S(1)}, bf16[96,512]{1,0:T(8,128)(2,1)S(1)}, u32[]{:S(2)}, u32[]{:S(2)}) %collective-permute-start.11) | collective-permute-done | bytes 98336 | tf_op jit(solution)/shard_map/ppermute | solution.py:34
  54.6 3.0 %collective-permute-done.13 = bf16[96,512]{1,0:T(8,128)(2,1)S(1)} collective-permute-done((bf16[96,512]{1,0:T(8,128)(2,1)S(1)}, bf16[96,512]{1,0:T(8,128)(2,1)S(1)}, u32[]{:S(2)}, u32[]{:S(2)}) %collective-permute-start.13) | collective-permute-done | bytes 98336 | tf_op jit(solution)/shard_map/ppermute | solution.py:34
  58.0 1.3 %collective-permute-done.15.far_ref = bf16[4,2,16,512]{3,2,1,0:T(8,128)(2,1)S(1)} collective-permute-done((bf16[4,2,16,512]{3,2,1,0:T(8,128)(2,1)S(1)}, bf16[4,2,16,512]{3,2,1,0:T(8,128)(2,1)S(1)}, u32[]{:S(2)}, u32[]{:S(2)}) %collective-permute-start.15) | collective-permute-done | bytes 131104 | tf_op jit(solution)/shard_map/ppermute | solution.py:34
  59.6 4.8 %collective-permute-done.14.refs_0_ = bf16[64,512]{1,0:T(8,128)(2,1)S(1)} collective-permute-done((bf16[64,512]{1,0:T(8,128)(2,1)S(1)}, bf16[64,512]{1,0:T(8,128)(2,1)S(1)}, u32[]{:S(2)}, u32[]{:S(2)}) %collective-permute-start.14) | collective-permute-done | bytes 65568 | tf_op jit(solution)/shard_map/ppermute | solution.py:34
  65.0 2.7 %collective-permute-start.16 = (f32[2,16,512]{2,1,0:T(8,128)S(1)}, f32[2,16,512]{2,1,0:T(8,128)S(1)}, u32[]{:S(2)}, u32[]{:S(2)}) collective-permute-start(f32[2,16,512]{2,1,0:T(8,128)S(1)} %last_messages.1), channel_id=1, source_target_pairs={{0,5},{1,4},{2,7},{3,6},{4,1},{5,0},{6,3},{7,2},{8,13},{9,12},{10,... | collective-permute-start | bytes 196616 | tf_op jit(solution)/shard_map/ppermute | solution.py:34
  67.7 2.4 %collective-permute-done.18 = f32[2,16,512]{2,1,0:T(8,128)S(1)} collective-permute-done((f32[2,16,512]{2,1,0:T(8,128)S(1)}, f32[2,16,512]{2,1,0:T(8,128)S(1)}, u32[]{:S(2)}, u32[]{:S(2)}) %collective-permute-start.18) | collective-permute-done | bytes 65568 | tf_op jit(solution)/shard_map/ppermute | solution.py:34
  73.7 3.5 %all-to-all-start.1 = ((f32[16,2,16]{2,1,0:T(2,128)}), f32[16,2,16]{2,1,0:T(2,128)S(1)}, u32[]{:S(2)}, u32[]{:S(2)}) async-start(f32[16,2,16]{2,1,0:T(2,128)} %broadcast_in_dim.7), calls=%async_computation.1 | async-start | bytes 32768 | tf_op jit(solution)/shard_map/all_to_all | solution.py:21
  77.8 5.8 %all-to-all-done.1 = f32[16,2,16]{2,1,0:T(2,128)S(1)} async-done(((f32[16,2,16]{2,1,0:T(2,128)}), f32[16,2,16]{2,1,0:T(2,128)S(1)}, u32[]{:S(2)}, u32[]{:S(2)}) %all-to-all-start.1) | async-done | bytes 2080 | tf_op jit(solution)/shard_map/all_to_all | solution.py:21
  (77 shorter events, 11.8 us)
Async XLA Ops:
  0.6 17.8 %copy-start = (bf16[8192,512]{1,0:T(8,128)(2,1)S(1)}, bf16[8192,512]{1,0:T(8,128)(2,1)}, u32[]{:S(2)}) copy-start(bf16[8192,512]{1,0:T(8,128)(2,1)} %transition_ref.11) | copy-start | bytes 25165828
  19.9 1.6 %collective-permute-start = (bf16[4,2,32,512]{3,2,1,0:T(8,128)(2,1)S(1)}, bf16[4,2,32,512]{3,2,1,0:T(8,128)(2,1)S(1)}, u32[]{:S(2)}, u32[]{:S(2)}) collective-permute-start(bf16[4,2,32,512]{3,2,1,0:T(8,128)(2,1)S(1)} %get-tuple-element.32), channel_id=1, source_target_pairs={{0,1},{1,0},{2,3},{3,2},{4,5},{5,4},{6,7},{7,6},{8,9},{9,8},{10,11... | collective-permute-start | bytes 786440 | tf_op jit(solution)/shard_map/ppermute | solution.py:34
  21.6 5.9 %collective-permute-start.3 = (bf16[64,512]{1,0:T(8,128)(2,1)S(1)}, bf16[64,512]{1,0:T(8,128)(2,1)S(1)}, u32[]{:S(2)}, u32[]{:S(2)}) collective-permute-start(bf16[64,512]{1,0:T(8,128)(2,1)S(1)} %bitcast.105), channel_id=1, source_target_pairs={{0,6},{1,7},{2,4},{3,5},{4,2},{5,3},{6,0},{7,1},{8,14},{9,15},{10,... | collective-permute-start | bytes 196616 | tf_op jit(solution)/shard_map/ppermute | solution.py:34
  22.0 5.4 %collective-permute-start.1 = (bf16[64,512]{1,0:T(8,128)(2,1)S(1)}, bf16[64,512]{1,0:T(8,128)(2,1)S(1)}, u32[]{:S(2)}, u32[]{:S(2)}) collective-permute-start(bf16[64,512]{1,0:T(8,128)(2,1)S(1)} %bitcast.104), channel_id=1, source_target_pairs={{0,5},{1,4},{2,7},{3,6},{4,1},{5,0},{6,3},{7,2},{8,13},{9,12},{10,... | collective-permute-start | bytes 196616 | tf_op jit(solution)/shard_map/ppermute | solution.py:34
  23.0 4.9 %collective-permute-start.2 = (bf16[64,512]{1,0:T(8,128)(2,1)S(1)}, bf16[64,512]{1,0:T(8,128)(2,1)S(1)}, u32[]{:S(2)}, u32[]{:S(2)}) collective-permute-start(bf16[64,512]{1,0:T(8,128)(2,1)S(1)} %bitcast.103), channel_id=1, source_target_pairs={{0,3},{1,2},{2,1},{3,0},{4,7},{5,6},{6,5},{7,4},{8,11},{9,10},{10,... | collective-permute-start | bytes 196616 | tf_op jit(solution)/shard_map/ppermute | solution.py:34
  28.0 5.2 %collective-permute-start.4 = (bf16[32,512]{1,0:T(8,128)(2,1)S(1)}, bf16[32,512]{1,0:T(8,128)(2,1)S(1)}, u32[]{:S(2)}, u32[]{:S(2)}) collective-permute-start(bf16[32,512]{1,0:T(8,128)(2,1)S(1)} %fusion.14), channel_id=1, source_target_pairs={{0,9},{1,8},{2,11},{3,10},{4,13},{5,12},{6,15},{7,14},{8,1},{9,0},... | collective-permute-start | bytes 98312 | tf_op jit(solution)/shard_map/ppermute | solution.py:34
  34.7 1.4 %collective-permute-start.5 = (bf16[4,2,16,512]{3,2,1,0:T(8,128)(2,1)S(1)}, bf16[4,2,16,512]{3,2,1,0:T(8,128)(2,1)S(1)}, u32[]{:S(2)}, u32[]{:S(2)}) collective-permute-start(bf16[4,2,16,512]{3,2,1,0:T(8,128)(2,1)S(1)} %get-tuple-element.34), channel_id=1, source_target_pairs={{0,1},{1,0},{2,3},{3,2},{4,5},{5,4},{6,7},{7,6},{8,9},{9,8},{10,11... | collective-permute-start | bytes 393224 | tf_op jit(solution)/shard_map/ppermute | solution.py:34
  36.2 5.1 %collective-permute-start.8 = (bf16[32,512]{1,0:T(8,128)(2,1)S(1)}, bf16[32,512]{1,0:T(8,128)(2,1)S(1)}, u32[]{:S(2)}, u32[]{:S(2)}) collective-permute-start(bf16[32,512]{1,0:T(8,128)(2,1)S(1)} %bitcast.115), channel_id=1, source_target_pairs={{0,6},{1,7},{2,4},{3,5},{4,2},{5,3},{6,0},{7,1},{8,14},{9,15},{10,... | collective-permute-start | bytes 98312 | tf_op jit(solution)/shard_map/ppermute | solution.py:34
  36.3 5.0 %collective-permute-start.6 = (bf16[32,512]{1,0:T(8,128)(2,1)S(1)}, bf16[32,512]{1,0:T(8,128)(2,1)S(1)}, u32[]{:S(2)}, u32[]{:S(2)}) collective-permute-start(bf16[32,512]{1,0:T(8,128)(2,1)S(1)} %bitcast.114), channel_id=1, source_target_pairs={{0,5},{1,4},{2,7},{3,6},{4,1},{5,0},{6,3},{7,2},{8,13},{9,12},{10,... | collective-permute-start | bytes 98312 | tf_op jit(solution)/shard_map/ppermute | solution.py:34
  37.9 3.6 %collective-permute-start.7 = (bf16[32,512]{1,0:T(8,128)(2,1)S(1)}, bf16[32,512]{1,0:T(8,128)(2,1)S(1)}, u32[]{:S(2)}, u32[]{:S(2)}) collective-permute-start(bf16[32,512]{1,0:T(8,128)(2,1)S(1)} %bitcast.113), channel_id=1, source_target_pairs={{0,3},{1,2},{2,1},{3,0},{4,7},{5,6},{6,5},{7,4},{8,11},{9,10},{10,... | collective-permute-start | bytes 98312 | tf_op jit(solution)/shard_map/ppermute | solution.py:34
  41.5 5.1 %collective-permute-start.9 = (bf16[32,512]{1,0:T(8,128)(2,1)S(1)}, bf16[32,512]{1,0:T(8,128)(2,1)S(1)}, u32[]{:S(2)}, u32[]{:S(2)}) collective-permute-start(bf16[32,512]{1,0:T(8,128)(2,1)S(1)} %pad_maximum_fusion.9), channel_id=1, source_target_pairs={{0,9},{1,8},{2,11},{3,10},{4,13},{5,12},{6,15},{7,14},{8,1},{9,0},... | collective-permute-start | bytes 98312 | tf_op jit(solution)/shard_map/ppermute | solution.py:34
  48.1 1.6 %collective-permute-start.10 = (f32[4,2,16,512]{3,2,1,0:T(8,128)S(1)}, f32[4,2,16,512]{3,2,1,0:T(8,128)S(1)}, u32[]{:S(2)}, u32[]{:S(2)}) collective-permute-start(f32[4,2,16,512]{3,2,1,0:T(8,128)S(1)} %get-tuple-element.36), channel_id=1, source_target_pairs={{0,1},{1,0},{2,3},{3,2},{4,5},{5,4},{6,7},{7,6},{8,9},{9,8},{10,11... | collective-permute-start | bytes 786440 | tf_op jit(solution)/shard_map/ppermute | solution.py:34
  49.5 21.0 %copy-start.1 = (bf16[8192,256]{1,0:T(8,128)(2,1)S(1)}, bf16[8192,256]{1,0:T(8,128)(2,1)}, u32[]{:S(2)}) copy-start(bf16[8192,256]{1,0:T(8,128)(2,1)} %emission_ref.3) | copy-start | bytes 12582916
  49.7 22.2 %copy-start.3 = (bf16[16,256]{1,0:T(8,128)(2,1)S(1)}, bf16[16,256]{1,0:T(8,128)(2,1)}, u32[]{:S(2)}) copy-start(bf16[16,256]{1,0:T(8,128)(2,1)} %logits_ref.1) | copy-start | bytes 24580
  49.8 4.8 %collective-permute-start.11 = (bf16[96,512]{1,0:T(8,128)(2,1)S(1)}, bf16[96,512]{1,0:T(8,128)(2,1)S(1)}, u32[]{:S(2)}, u32[]{:S(2)}) collective-permute-start(bf16[96,512]{1,0:T(8,128)(2,1)S(1)} %get-tuple-element.65), channel_id=1, source_target_pairs={{0,5},{1,4},{2,7},{3,6},{4,1},{5,0},{6,3},{7,2},{8,13},{9,12},{10,... | collective-permute-start | bytes 294920 | tf_op jit(solution)/shard_map/ppermute | solution.py:34
  49.9 4.8 %collective-permute-start.12 = (bf16[96,512]{1,0:T(8,128)(2,1)S(1)}, bf16[96,512]{1,0:T(8,128)(2,1)S(1)}, u32[]{:S(2)}, u32[]{:S(2)}) collective-permute-start(bf16[96,512]{1,0:T(8,128)(2,1)S(1)} %get-tuple-element.66), channel_id=1, source_target_pairs={{0,3},{1,2},{2,1},{3,0},{4,7},{5,6},{6,5},{7,4},{8,11},{9,10},{10,... | collective-permute-start | bytes 294920 | tf_op jit(solution)/shard_map/ppermute | solution.py:34
  51.0 6.7 %collective-permute-start.13 = (bf16[96,512]{1,0:T(8,128)(2,1)S(1)}, bf16[96,512]{1,0:T(8,128)(2,1)S(1)}, u32[]{:S(2)}, u32[]{:S(2)}) collective-permute-start(bf16[96,512]{1,0:T(8,128)(2,1)S(1)} %get-tuple-element.67), channel_id=1, source_target_pairs={{0,6},{1,7},{2,4},{3,5},{4,2},{5,3},{6,0},{7,1},{8,14},{9,15},{10,... | collective-permute-start | bytes 294920 | tf_op jit(solution)/shard_map/ppermute | solution.py:34
  57.7 6.7 %collective-permute-start.14 = (bf16[64,512]{1,0:T(8,128)(2,1)S(1)}, bf16[64,512]{1,0:T(8,128)(2,1)S(1)}, u32[]{:S(2)}, u32[]{:S(2)}) collective-permute-start(bf16[64,512]{1,0:T(8,128)(2,1)S(1)} %pad_maximum_fusion.8), channel_id=1, source_target_pairs={{0,9},{1,8},{2,11},{3,10},{4,13},{5,12},{6,15},{7,14},{8,1},{9,0},... | collective-permute-start | bytes 196616 | tf_op jit(solution)/shard_map/ppermute | solution.py:34
  57.9 1.4 %collective-permute-start.15 = (bf16[4,2,16,512]{3,2,1,0:T(8,128)(2,1)S(1)}, bf16[4,2,16,512]{3,2,1,0:T(8,128)(2,1)S(1)}, u32[]{:S(2)}, u32[]{:S(2)}) collective-permute-start(bf16[4,2,16,512]{3,2,1,0:T(8,128)(2,1)S(1)} %pad_maximum_fusion.7.near_ref), channel_id=1, source_target_pairs={{0,1},{1,0},{2,3},{3,2},{4,5},{5,4},{6,7},{7,6},{8,9},{9,8},{10,11... | collective-permute-start | bytes 393224 | tf_op jit(solution)/shard_map/ppermute | solution.py:34
  64.4 5.7 %collective-permute-start.18 = (f32[2,16,512]{2,1,0:T(8,128)S(1)}, f32[2,16,512]{2,1,0:T(8,128)S(1)}, u32[]{:S(2)}, u32[]{:S(2)}) collective-permute-start(f32[2,16,512]{2,1,0:T(8,128)S(1)} %last_messages.1), channel_id=1, source_target_pairs={{0,6},{1,7},{2,4},{3,5},{4,2},{5,3},{6,0},{7,1},{8,14},{9,15},{10,... | collective-permute-start | bytes 196616 | tf_op jit(solution)/shard_map/ppermute | solution.py:34
  64.6 5.6 %collective-permute-start.17 = (f32[2,16,512]{2,1,0:T(8,128)S(1)}, f32[2,16,512]{2,1,0:T(8,128)S(1)}, u32[]{:S(2)}, u32[]{:S(2)}) collective-permute-start(f32[2,16,512]{2,1,0:T(8,128)S(1)} %last_messages.1), channel_id=1, source_target_pairs={{0,3},{1,2},{2,1},{3,0},{4,7},{5,6},{6,5},{7,4},{8,11},{9,10},{10,... | collective-permute-start | bytes 196616 | tf_op jit(solution)/shard_map/ppermute | solution.py:34
  65.0 5.3 %collective-permute-start.16 = (f32[2,16,512]{2,1,0:T(8,128)S(1)}, f32[2,16,512]{2,1,0:T(8,128)S(1)}, u32[]{:S(2)}, u32[]{:S(2)}) collective-permute-start(f32[2,16,512]{2,1,0:T(8,128)S(1)} %last_messages.1), channel_id=1, source_target_pairs={{0,5},{1,4},{2,7},{3,6},{4,1},{5,0},{6,3},{7,2},{8,13},{9,12},{10,... | collective-permute-start | bytes 196616 | tf_op jit(solution)/shard_map/ppermute | solution.py:34
  70.3 1.6 %collective-permute-start.19 = (f32[4,2,16,512]{3,2,1,0:T(8,128)S(1)}, f32[4,2,16,512]{3,2,1,0:T(8,128)S(1)}, u32[]{:S(2)}, u32[]{:S(2)}) collective-permute-start(f32[4,2,16,512]{3,2,1,0:T(8,128)S(1)} %pad_maximum_fusion.parts_ref), channel_id=1, source_target_pairs={{0,1},{1,0},{2,3},{3,2},{4,5},{5,4},{6,7},{7,6},{8,9},{9,8},{10,11... | collective-permute-start | bytes 786440 | tf_op jit(solution)/shard_map/ppermute | solution.py:34
  73.7 10.0 %all-to-all-start.1 = ((f32[16,2,16]{2,1,0:T(2,128)}), f32[16,2,16]{2,1,0:T(2,128)S(1)}, u32[]{:S(2)}, u32[]{:S(2)}) async-start(f32[16,2,16]{2,1,0:T(2,128)} %broadcast_in_dim.7), calls=%async_computation.1 | async-start | bytes 32768 | tf_op jit(solution)/shard_map/all_to_all | solution.py:21
  (1 other events, 4.6 us)

commit v10 on v8

--- a/solution.py
+++ b/solution.py
@@ -207,7 +207,7 @@
         chunks.append(
             pltpu.make_async_copy(emission_hbm.at[span], emission_ref.at[span], chunk_sems.at[k])
         )
-    for copy in copies[:1] + chunks + copies[1:]:
+    for copy in copies + chunks:
         copy.start()
     shape = (devices * devices // 2, devices * devices)
     to, source = (lax.broadcasted_iota(jnp.int32, shape, axis) for axis in (0, 1))

time: 84.7 us -> 84.7 us (level)
  no operation moved by 1% of the time
where the time goes in v10:
time: 84.7 us; the launch traced here: 84.5 us
  waiting for transfers between devices  34.9 us (41%)
  starting transfers between devices  17.5 us (21%)
  Pallas kernels  14.5 us (17%)
  blocking collectives  13.8 us (16%)
  local copies, waits for them, and re-layouts  1.54 us (2%)
  other arithmetic  1.29 us (2%)
  between operations  0.91 us (1%)
    ppermute x20, waiting for transfers between devices, swap(): return lax.ppermute(block, 'vocab', pairs)  29 us
    ppermute x20, starting transfers between devices, swap(): return lax.ppermute(block, 'vocab', pairs)  14 us
    all_to_all x1, blocking collectives, exchange(): lax.all_to_all(blocks, 'vocab', split_axis=0, concat_axis=0, tiled=True)  13.8 us
    all_to_all x1, waiting for transfers between devices, exchange(): lax.all_to_all(blocks, 'vocab', split_axis=0, concat_axis=0, tiled=True)  5.84 us
    pallas_call x3, Pallas kernels, step(): pl.pallas_call(functools.partial(send_kernel, count, len(parts)), out_sha...  4.34 us
    pallas_call x3, Pallas kernels, step(): pl.pallas_call(functools.partial(keep_kernel, count), out_shape=pltpu.VME...  3.88 us
    all_to_all x1, starting transfers between devices, exchange(): lax.all_to_all(blocks, 'vocab', split_axis=0, concat_axis=0, tiled=True)  3.49 us
    pallas_call x1, Pallas kernels, first_products(): pl.pallas_call(functools.partial(products_kernel, count), out_shape=[jax....  3.36 us
  transfers between devices with their start and end apart: 21, of which 18 were waited for; matrix products, arithmetic and copies ran while one was open for 1% of the time, Pallas kernels for 6%

profile of v10, /device:TPU:0, one launch (start us, length us, event | category | flops | bytes accessed | tf_op | source)
XLA Modules:
  0.0 84.5 jit_solution(3857176263422193124)
XLA Ops:
  0.6 3.4 %first_products.1 = (f32[16,1,512]{2,1,0:T(1,128)S(1)}, bf16[4,2,16,512]{3,2,1,0:T(8,128)(2,1)S(1)}, bf16[4,2,16,512]{3,2,1,0:T(8,128)(2,1)S(1)}, s32[1,16]{1,0:...) custom-call(s32[16]{0:T(128)} %token_hbm.1, ...), custom_call_target="tpu_custom_call" | custom-call | tf_op jit(solution)/shard_map/first_products/pallas_call | solution.py:243
  4.5 13.8 %all_to_all.10.sums_ref = f32[16,1,512]{2,1,0:T(1,128)S(1)} all-to-all(f32[16,1,512]{2,1,0:T(1,128)S(1)} %get-tuple-element.27), channel_id=1, replica_groups=mesh['parts'=2,'vocab'=16] {'vocab'}, dimensions={0} | all-to-all | bytes 65536 | tf_op jit(solution)/shard_map/all_to_all | solution.py:21
  18.3 1.4 %step_sent_half.3 = (bf16[32,512]{1,0:T(8,128)(2,1)S(1)}, bf16[4,2,32,512]{3,2,1,0:T(8,128)(2,1)S(1)}) custom-call(bf16[8192,512]{1,0:T(8,128)(2,1)S(1)} %copy-done, bf16[256,48]{1,0:T(8,128)(2,1)S(1)} %get-tuple-element.26.route_ref, f32[16,1,512]{2,1,0:T(1,128)S(1)} %all_to_all.10.sums_ref, f32[16,512]{1,0:T(8,128)S(1)} %get-tuple-element.28.refs_0_, ...), custom_call_target="tpu_custom_call" | custom-call | tf_op jit(solution)/shard_map/step_sent_half/pallas_call | solution.py:394
  19.7 1.3 %step_kept_half.3 = f32[4,2,32,512]{3,2,1,0:T(8,128)S(1)} custom-call(bf16[8192,512]{1,0:T(8,128)(2,1)S(1)} %copy-done, bf16[32,512]{1,0:T(8,128)(2,1)S(1)} %get-tuple-element.30.halves_ref, bf16[4,2,16,512]{3,2,1,0:T(8,128)(2,1)S(1)} %get-tuple-element.31.refs_0_), custom_call_target="tpu_custom_call" | custom-call | tf_op jit(solution)/shard_map/step_kept_half/pallas_call | solution.py:406
  22.9 1.8 %collective-permute-start.2 = (bf16[64,512]{1,0:T(8,128)(2,1)S(1)}, bf16[64,512]{1,0:T(8,128)(2,1)S(1)}, u32[]{:S(2)}, u32[]{:S(2)}) collective-permute-start(bf16[64,512]{1,0:T(8,128)(2,1)S(1)} %bitcast.103), channel_id=1, source_target_pairs={{0,3},{1,2},{2,1},{3,0},{4,7},{5,6},{6,5},{7,4},{8,11},{9,10},{10,... | collective-permute-start | bytes 196616 | tf_op jit(solution)/shard_map/ppermute | solution.py:34
  24.7 2.6 %collective-permute-done.3 = bf16[64,512]{1,0:T(8,128)(2,1)S(1)} collective-permute-done((bf16[64,512]{1,0:T(8,128)(2,1)S(1)}, bf16[64,512]{1,0:T(8,128)(2,1)S(1)}, u32[]{:S(2)}, u32[]{:S(2)}) %collective-permute-start.3) | collective-permute-done | bytes 65568 | tf_op jit(solution)/shard_map/ppermute | solution.py:34
  28.1 5.0 %collective-permute-done.4.refs_1_ = bf16[32,512]{1,0:T(8,128)(2,1)S(1)} collective-permute-done((bf16[32,512]{1,0:T(8,128)(2,1)S(1)}, bf16[32,512]{1,0:T(8,128)(2,1)S(1)}, u32[]{:S(2)}, u32[]{:S(2)}) %collective-permute-start.4) | collective-permute-done | bytes 32800 | tf_op jit(solution)/shard_map/ppermute | solution.py:34
  33.0 1.5 %step_sent_half.4 = (bf16[32,512]{1,0:T(8,128)(2,1)S(1)}, bf16[4,2,16,512]{3,2,1,0:T(8,128)(2,1)S(1)}) custom-call(bf16[8192,512]{1,0:T(8,128)(2,1)S(1)} %copy-done, bf16[256,48]{1,0:T(8,128)(2,1)S(1)} %get-tuple-element.26.route_ref, f32[16,1,512]{2,1,0:T(1,128)S(1)} %all_to_all.10.sums_ref, f32[32,512]{1,0:T(8,128)S(1)} %slice_bitcast_fusion.2.refs_0_, ...), custom_call_target="tpu_custom_call" | custom-call | tf_op jit(solution)/shard_map/step_sent_half/pallas_call | solution.py:394
  34.6 1.3 %step_kept_half.4 = f32[4,2,16,512]{3,2,1,0:T(8,128)S(1)} custom-call(bf16[8192,512]{1,0:T(8,128)(2,1)S(1)} %copy-done, bf16[32,512]{1,0:T(8,128)(2,1)S(1)} %get-tuple-element.33.halves_ref), custom_call_target="tpu_custom_call" | custom-call | tf_op jit(solution)/shard_map/step_kept_half/pallas_call | solution.py:406
  36.1 1.6 %collective-permute-start.6 = (bf16[32,512]{1,0:T(8,128)(2,1)S(1)}, bf16[32,512]{1,0:T(8,128)(2,1)S(1)}, u32[]{:S(2)}, u32[]{:S(2)}) collective-permute-start(bf16[32,512]{1,0:T(8,128)(2,1)S(1)} %bitcast.114), channel_id=1, source_target_pairs={{0,5},{1,4},{2,7},{3,6},{4,1},{5,0},{6,3},{7,2},{8,13},{9,12},{10,... | collective-permute-start | bytes 98312 | tf_op jit(solution)/shard_map/ppermute | solution.py:34
  37.7 1.6 %collective-permute-start.7 = (bf16[32,512]{1,0:T(8,128)(2,1)S(1)}, bf16[32,512]{1,0:T(8,128)(2,1)S(1)}, u32[]{:S(2)}, u32[]{:S(2)}) collective-permute-start(bf16[32,512]{1,0:T(8,128)(2,1)S(1)} %bitcast.113), channel_id=1, source_target_pairs={{0,3},{1,2},{2,1},{3,0},{4,7},{5,6},{6,5},{7,4},{8,11},{9,10},{10,... | collective-permute-start | bytes 98312 | tf_op jit(solution)/shard_map/ppermute | solution.py:34
  39.4 1.7 %collective-permute-done.8 = bf16[32,512]{1,0:T(8,128)(2,1)S(1)} collective-permute-done((bf16[32,512]{1,0:T(8,128)(2,1)S(1)}, bf16[32,512]{1,0:T(8,128)(2,1)S(1)}, u32[]{:S(2)}, u32[]{:S(2)}) %collective-permute-start.8) | collective-permute-done | bytes 32800 | tf_op jit(solution)/shard_map/ppermute | solution.py:34
  41.4 5.0 %collective-permute-done.9.refs_1_ = bf16[32,512]{1,0:T(8,128)(2,1)S(1)} collective-permute-done((bf16[32,512]{1,0:T(8,128)(2,1)S(1)}, bf16[32,512]{1,0:T(8,128)(2,1)S(1)}, u32[]{:S(2)}, u32[]{:S(2)}) %collective-permute-start.9) | collective-permute-done | bytes 32800 | tf_op jit(solution)/shard_map/ppermute | solution.py:34
  46.4 1.4 %step_sent_half.5 = (bf16[32,512]{1,0:T(8,128)(2,1)S(1)}, f32[4,2,16,512]{3,2,1,0:T(8,128)S(1)}) custom-call(bf16[8192,512]{1,0:T(8,128)(2,1)S(1)} %copy-done, bf16[256,48]{1,0:T(8,128)(2,1)S(1)} %get-tuple-element.26.route_ref, f32[16,1,512]{2,1,0:T(1,128)S(1)} %all_to_all.10.sums_ref, f32[16,512]{1,0:T(8,128)S(1)} %slice_bitcast_fusion.4.refs_0_, ...), custom_call_target="tpu_custom_call" | custom-call | tf_op jit(solution)/shard_map/step_sent_half/pallas_call | solution.py:394
  48.0 1.3 %step_kept_half.5 = f32[4,2,16,512]{3,2,1,0:T(8,128)S(1)} custom-call(bf16[8192,512]{1,0:T(8,128)(2,1)S(1)} %copy-done, bf16[32,512]{1,0:T(8,128)(2,1)S(1)} %get-tuple-element.35.halves_ref), custom_call_target="tpu_custom_call" | custom-call | tf_op jit(solution)/shard_map/step_kept_half/pallas_call | solution.py:406
  50.8 2.0 %collective-permute-start.13 = (bf16[96,512]{1,0:T(8,128)(2,1)S(1)}, bf16[96,512]{1,0:T(8,128)(2,1)S(1)}, u32[]{:S(2)}, u32[]{:S(2)}) collective-permute-start(bf16[96,512]{1,0:T(8,128)(2,1)S(1)} %get-tuple-element.67), channel_id=1, source_target_pairs={{0,6},{1,7},{2,4},{3,5},{4,2},{5,3},{6,0},{7,1},{8,14},{9,15},{10,... | collective-permute-start | bytes 294920 | tf_op jit(solution)/shard_map/ppermute | solution.py:34
  52.9 1.5 %collective-permute-done.11 = bf16[96,512]{1,0:T(8,128)(2,1)S(1)} collective-permute-done((bf16[96,512]{1,0:T(8,128)(2,1)S(1)}, bf16[96,512]{1,0:T(8,128)(2,1)S(1)}, u32[]{:S(2)}, u32[]{:S(2)}) %collective-permute-start.11) | collective-permute-done | bytes 98336 | tf_op jit(solution)/shard_map/ppermute | solution.py:34
  54.4 3.1 %collective-permute-done.13 = bf16[96,512]{1,0:T(8,128)(2,1)S(1)} collective-permute-done((bf16[96,512]{1,0:T(8,128)(2,1)S(1)}, bf16[96,512]{1,0:T(8,128)(2,1)S(1)}, u32[]{:S(2)}, u32[]{:S(2)}) %collective-permute-start.13) | collective-permute-done | bytes 98336 | tf_op jit(solution)/shard_map/ppermute | solution.py:34
  57.8 1.3 %collective-permute-done.15.far_ref = bf16[4,2,16,512]{3,2,1,0:T(8,128)(2,1)S(1)} collective-permute-done((bf16[4,2,16,512]{3,2,1,0:T(8,128)(2,1)S(1)}, bf16[4,2,16,512]{3,2,1,0:T(8,128)(2,1)S(1)}, u32[]{:S(2)}, u32[]{:S(2)}) %collective-permute-start.15) | collective-permute-done | bytes 131104 | tf_op jit(solution)/shard_map/ppermute | solution.py:34
  59.4 4.8 %collective-permute-done.14.refs_0_ = bf16[64,512]{1,0:T(8,128)(2,1)S(1)} collective-permute-done((bf16[64,512]{1,0:T(8,128)(2,1)S(1)}, bf16[64,512]{1,0:T(8,128)(2,1)S(1)}, u32[]{:S(2)}, u32[]{:S(2)}) %collective-permute-start.14) | collective-permute-done | bytes 65568 | tf_op jit(solution)/shard_map/ppermute | solution.py:34
  64.8 2.7 %collective-permute-start.16 = (f32[2,16,512]{2,1,0:T(8,128)S(1)}, f32[2,16,512]{2,1,0:T(8,128)S(1)}, u32[]{:S(2)}, u32[]{:S(2)}) collective-permute-start(f32[2,16,512]{2,1,0:T(8,128)S(1)} %last_messages.1), channel_id=1, source_target_pairs={{0,5},{1,4},{2,7},{3,6},{4,1},{5,0},{6,3},{7,2},{8,13},{9,12},{10,... | collective-permute-start | bytes 196616 | tf_op jit(solution)/shard_map/ppermute | solution.py:34
  67.5 2.4 %collective-permute-done.18 = f32[2,16,512]{2,1,0:T(8,128)S(1)} collective-permute-done((f32[2,16,512]{2,1,0:T(8,128)S(1)}, f32[2,16,512]{2,1,0:T(8,128)S(1)}, u32[]{:S(2)}, u32[]{:S(2)}) %collective-permute-start.18) | collective-permute-done | bytes 65568 | tf_op jit(solution)/shard_map/ppermute | solution.py:34
  73.5 3.5 %all-to-all-start.1 = ((f32[16,2,16]{2,1,0:T(2,128)}), f32[16,2,16]{2,1,0:T(2,128)S(1)}, u32[]{:S(2)}, u32[]{:S(2)}) async-start(f32[16,2,16]{2,1,0:T(2,128)} %broadcast_in_dim.7), calls=%async_computation.1 | async-start | bytes 32768 | tf_op jit(solution)/shard_map/all_to_all | solution.py:21
  77.6 5.8 %all-to-all-done.1 = f32[16,2,16]{2,1,0:T(2,128)S(1)} async-done(((f32[16,2,16]{2,1,0:T(2,128)}), f32[16,2,16]{2,1,0:T(2,128)S(1)}, u32[]{:S(2)}, u32[]{:S(2)}) %all-to-all-start.1) | async-done | bytes 2080 | tf_op jit(solution)/shard_map/all_to_all | solution.py:21
  (77 shorter events, 11.8 us)
Async XLA Ops:
  0.6 17.6 %copy-start = (bf16[8192,512]{1,0:T(8,128)(2,1)S(1)}, bf16[8192,512]{1,0:T(8,128)(2,1)}, u32[]{:S(2)}) copy-start(bf16[8192,512]{1,0:T(8,128)(2,1)} %transition_ref.11) | copy-start | bytes 25165828
  19.7 1.6 %collective-permute-start = (bf16[4,2,32,512]{3,2,1,0:T(8,128)(2,1)S(1)}, bf16[4,2,32,512]{3,2,1,0:T(8,128)(2,1)S(1)}, u32[]{:S(2)}, u32[]{:S(2)}) collective-permute-start(bf16[4,2,32,512]{3,2,1,0:T(8,128)(2,1)S(1)} %get-tuple-element.32), channel_id=1, source_target_pairs={{0,1},{1,0},{2,3},{3,2},{4,5},{5,4},{6,7},{7,6},{8,9},{9,8},{10,11... | collective-permute-start | bytes 786440 | tf_op jit(solution)/shard_map/ppermute | solution.py:34
  21.4 5.9 %collective-permute-start.3 = (bf16[64,512]{1,0:T(8,128)(2,1)S(1)}, bf16[64,512]{1,0:T(8,128)(2,1)S(1)}, u32[]{:S(2)}, u32[]{:S(2)}) collective-permute-start(bf16[64,512]{1,0:T(8,128)(2,1)S(1)} %bitcast.105), channel_id=1, source_target_pairs={{0,6},{1,7},{2,4},{3,5},{4,2},{5,3},{6,0},{7,1},{8,14},{9,15},{10,... | collective-permute-start | bytes 196616 | tf_op jit(solution)/shard_map/ppermute | solution.py:34
  21.9 5.4 %collective-permute-start.1 = (bf16[64,512]{1,0:T(8,128)(2,1)S(1)}, bf16[64,512]{1,0:T(8,128)(2,1)S(1)}, u32[]{:S(2)}, u32[]{:S(2)}) collective-permute-start(bf16[64,512]{1,0:T(8,128)(2,1)S(1)} %bitcast.104), channel_id=1, source_target_pairs={{0,5},{1,4},{2,7},{3,6},{4,1},{5,0},{6,3},{7,2},{8,13},{9,12},{10,... | collective-permute-start | bytes 196616 | tf_op jit(solution)/shard_map/ppermute | solution.py:34
  22.9 4.9 %collective-permute-start.2 = (bf16[64,512]{1,0:T(8,128)(2,1)S(1)}, bf16[64,512]{1,0:T(8,128)(2,1)S(1)}, u32[]{:S(2)}, u32[]{:S(2)}) collective-permute-start(bf16[64,512]{1,0:T(8,128)(2,1)S(1)} %bitcast.103), channel_id=1, source_target_pairs={{0,3},{1,2},{2,1},{3,0},{4,7},{5,6},{6,5},{7,4},{8,11},{9,10},{10,... | collective-permute-start | bytes 196616 | tf_op jit(solution)/shard_map/ppermute | solution.py:34
  27.8 5.2 %collective-permute-start.4 = (bf16[32,512]{1,0:T(8,128)(2,1)S(1)}, bf16[32,512]{1,0:T(8,128)(2,1)S(1)}, u32[]{:S(2)}, u32[]{:S(2)}) collective-permute-start(bf16[32,512]{1,0:T(8,128)(2,1)S(1)} %fusion.14), channel_id=1, source_target_pairs={{0,9},{1,8},{2,11},{3,10},{4,13},{5,12},{6,15},{7,14},{8,1},{9,0},... | collective-permute-start | bytes 98312 | tf_op jit(solution)/shard_map/ppermute | solution.py:34
  34.5 1.4 %collective-permute-start.5 = (bf16[4,2,16,512]{3,2,1,0:T(8,128)(2,1)S(1)}, bf16[4,2,16,512]{3,2,1,0:T(8,128)(2,1)S(1)}, u32[]{:S(2)}, u32[]{:S(2)}) collective-permute-start(bf16[4,2,16,512]{3,2,1,0:T(8,128)(2,1)S(1)} %get-tuple-element.34), channel_id=1, source_target_pairs={{0,1},{1,0},{2,3},{3,2},{4,5},{5,4},{6,7},{7,6},{8,9},{9,8},{10,11... | collective-permute-start | bytes 393224 | tf_op jit(solution)/shard_map/ppermute | solution.py:34
  36.0 5.1 %collective-permute-start.8 = (bf16[32,512]{1,0:T(8,128)(2,1)S(1)}, bf16[32,512]{1,0:T(8,128)(2,1)S(1)}, u32[]{:S(2)}, u32[]{:S(2)}) collective-permute-start(bf16[32,512]{1,0:T(8,128)(2,1)S(1)} %bitcast.115), channel_id=1, source_target_pairs={{0,6},{1,7},{2,4},{3,5},{4,2},{5,3},{6,0},{7,1},{8,14},{9,15},{10,... | collective-permute-start | bytes 98312 | tf_op jit(solution)/shard_map/ppermute | solution.py:34
  36.1 5.0 %collective-permute-start.6 = (bf16[32,512]{1,0:T(8,128)(2,1)S(1)}, bf16[32,512]{1,0:T(8,128)(2,1)S(1)}, u32[]{:S(2)}, u32[]{:S(2)}) collective-permute-start(bf16[32,512]{1,0:T(8,128)(2,1)S(1)} %bitcast.114), channel_id=1, source_target_pairs={{0,5},{1,4},{2,7},{3,6},{4,1},{5,0},{6,3},{7,2},{8,13},{9,12},{10,... | collective-permute-start | bytes 98312 | tf_op jit(solution)/shard_map/ppermute | solution.py:34
  37.7 3.6 %collective-permute-start.7 = (bf16[32,512]{1,0:T(8,128)(2,1)S(1)}, bf16[32,512]{1,0:T(8,128)(2,1)S(1)}, u32[]{:S(2)}, u32[]{:S(2)}) collective-permute-start(bf16[32,512]{1,0:T(8,128)(2,1)S(1)} %bitcast.113), channel_id=1, source_target_pairs={{0,3},{1,2},{2,1},{3,0},{4,7},{5,6},{6,5},{7,4},{8,11},{9,10},{10,... | collective-permute-start | bytes 98312 | tf_op jit(solution)/shard_map/ppermute | solution.py:34
  41.3 5.1 %collective-permute-start.9 = (bf16[32,512]{1,0:T(8,128)(2,1)S(1)}, bf16[32,512]{1,0:T(8,128)(2,1)S(1)}, u32[]{:S(2)}, u32[]{:S(2)}) collective-permute-start(bf16[32,512]{1,0:T(8,128)(2,1)S(1)} %pad_maximum_fusion.9), channel_id=1, source_target_pairs={{0,9},{1,8},{2,11},{3,10},{4,13},{5,12},{6,15},{7,14},{8,1},{9,0},... | collective-permute-start | bytes 98312 | tf_op jit(solution)/shard_map/ppermute | solution.py:34
  47.9 1.6 %collective-permute-start.10 = (f32[4,2,16,512]{3,2,1,0:T(8,128)S(1)}, f32[4,2,16,512]{3,2,1,0:T(8,128)S(1)}, u32[]{:S(2)}, u32[]{:S(2)}) collective-permute-start(f32[4,2,16,512]{3,2,1,0:T(8,128)S(1)} %get-tuple-element.36), channel_id=1, source_target_pairs={{0,1},{1,0},{2,3},{3,2},{4,5},{5,4},{6,7},{7,6},{8,9},{9,8},{10,11... | collective-permute-start | bytes 786440 | tf_op jit(solution)/shard_map/ppermute | solution.py:34
  49.3 21.0 %copy-start.1 = (bf16[8192,256]{1,0:T(8,128)(2,1)S(1)}, bf16[8192,256]{1,0:T(8,128)(2,1)}, u32[]{:S(2)}) copy-start(bf16[8192,256]{1,0:T(8,128)(2,1)} %emission_ref.3) | copy-start | bytes 12582916
  49.5 22.2 %copy-start.3 = (bf16[16,256]{1,0:T(8,128)(2,1)S(1)}, bf16[16,256]{1,0:T(8,128)(2,1)}, u32[]{:S(2)}) copy-start(bf16[16,256]{1,0:T(8,128)(2,1)} %logits_ref.1) | copy-start | bytes 24580
  49.6 4.8 %collective-permute-start.11 = (bf16[96,512]{1,0:T(8,128)(2,1)S(1)}, bf16[96,512]{1,0:T(8,128)(2,1)S(1)}, u32[]{:S(2)}, u32[]{:S(2)}) collective-permute-start(bf16[96,512]{1,0:T(8,128)(2,1)S(1)} %get-tuple-element.65), channel_id=1, source_target_pairs={{0,5},{1,4},{2,7},{3,6},{4,1},{5,0},{6,3},{7,2},{8,13},{9,12},{10,... | collective-permute-start | bytes 294920 | tf_op jit(solution)/shard_map/ppermute | solution.py:34
  49.7 4.8 %collective-permute-start.12 = (bf16[96,512]{1,0:T(8,128)(2,1)S(1)}, bf16[96,512]{1,0:T(8,128)(2,1)S(1)}, u32[]{:S(2)}, u32[]{:S(2)}) collective-permute-start(bf16[96,512]{1,0:T(8,128)(2,1)S(1)} %get-tuple-element.66), channel_id=1, source_target_pairs={{0,3},{1,2},{2,1},{3,0},{4,7},{5,6},{6,5},{7,4},{8,11},{9,10},{10,... | collective-permute-start | bytes 294920 | tf_op jit(solution)/shard_map/ppermute | solution.py:34
  50.8 6.7 %collective-permute-start.13 = (bf16[96,512]{1,0:T(8,128)(2,1)S(1)}, bf16[96,512]{1,0:T(8,128)(2,1)S(1)}, u32[]{:S(2)}, u32[]{:S(2)}) collective-permute-start(bf16[96,512]{1,0:T(8,128)(2,1)S(1)} %get-tuple-element.67), channel_id=1, source_target_pairs={{0,6},{1,7},{2,4},{3,5},{4,2},{5,3},{6,0},{7,1},{8,14},{9,15},{10,... | collective-permute-start | bytes 294920 | tf_op jit(solution)/shard_map/ppermute | solution.py:34
  57.6 6.7 %collective-permute-start.14 = (bf16[64,512]{1,0:T(8,128)(2,1)S(1)}, bf16[64,512]{1,0:T(8,128)(2,1)S(1)}, u32[]{:S(2)}, u32[]{:S(2)}) collective-permute-start(bf16[64,512]{1,0:T(8,128)(2,1)S(1)} %pad_maximum_fusion.8), channel_id=1, source_target_pairs={{0,9},{1,8},{2,11},{3,10},{4,13},{5,12},{6,15},{7,14},{8,1},{9,0},... | collective-permute-start | bytes 196616 | tf_op jit(solution)/shard_map/ppermute | solution.py:34
  57.7 1.4 %collective-permute-start.15 = (bf16[4,2,16,512]{3,2,1,0:T(8,128)(2,1)S(1)}, bf16[4,2,16,512]{3,2,1,0:T(8,128)(2,1)S(1)}, u32[]{:S(2)}, u32[]{:S(2)}) collective-permute-start(bf16[4,2,16,512]{3,2,1,0:T(8,128)(2,1)S(1)} %pad_maximum_fusion.7.near_ref), channel_id=1, source_target_pairs={{0,1},{1,0},{2,3},{3,2},{4,5},{5,4},{6,7},{7,6},{8,9},{9,8},{10,11... | collective-permute-start | bytes 393224 | tf_op jit(solution)/shard_map/ppermute | solution.py:34
  64.2 5.7 %collective-permute-start.18 = (f32[2,16,512]{2,1,0:T(8,128)S(1)}, f32[2,16,512]{2,1,0:T(8,128)S(1)}, u32[]{:S(2)}, u32[]{:S(2)}) collective-permute-start(f32[2,16,512]{2,1,0:T(8,128)S(1)} %last_messages.1), channel_id=1, source_target_pairs={{0,6},{1,7},{2,4},{3,5},{4,2},{5,3},{6,0},{7,1},{8,14},{9,15},{10,... | collective-permute-start | bytes 196616 | tf_op jit(solution)/shard_map/ppermute | solution.py:34
  64.4 5.6 %collective-permute-start.17 = (f32[2,16,512]{2,1,0:T(8,128)S(1)}, f32[2,16,512]{2,1,0:T(8,128)S(1)}, u32[]{:S(2)}, u32[]{:S(2)}) collective-permute-start(f32[2,16,512]{2,1,0:T(8,128)S(1)} %last_messages.1), channel_id=1, source_target_pairs={{0,3},{1,2},{2,1},{3,0},{4,7},{5,6},{6,5},{7,4},{8,11},{9,10},{10,... | collective-permute-start | bytes 196616 | tf_op jit(solution)/shard_map/ppermute | solution.py:34
  64.8 5.3 %collective-permute-start.16 = (f32[2,16,512]{2,1,0:T(8,128)S(1)}, f32[2,16,512]{2,1,0:T(8,128)S(1)}, u32[]{:S(2)}, u32[]{:S(2)}) collective-permute-start(f32[2,16,512]{2,1,0:T(8,128)S(1)} %last_messages.1), channel_id=1, source_target_pairs={{0,5},{1,4},{2,7},{3,6},{4,1},{5,0},{6,3},{7,2},{8,13},{9,12},{10,... | collective-permute-start | bytes 196616 | tf_op jit(solution)/shard_map/ppermute | solution.py:34
  70.1 1.6 %collective-permute-start.19 = (f32[4,2,16,512]{3,2,1,0:T(8,128)S(1)}, f32[4,2,16,512]{3,2,1,0:T(8,128)S(1)}, u32[]{:S(2)}, u32[]{:S(2)}) collective-permute-start(f32[4,2,16,512]{3,2,1,0:T(8,128)S(1)} %pad_maximum_fusion.parts_ref), channel_id=1, source_target_pairs={{0,1},{1,0},{2,3},{3,2},{4,5},{5,4},{6,7},{7,6},{8,9},{9,8},{10,11... | collective-permute-start | bytes 786440 | tf_op jit(solution)/shard_map/ppermute | solution.py:34
  73.5 10.0 %all-to-all-start.1 = ((f32[16,2,16]{2,1,0:T(2,128)}), f32[16,2,16]{2,1,0:T(2,128)S(1)}, u32[]{:S(2)}, u32[]{:S(2)}) async-start(f32[16,2,16]{2,1,0:T(2,128)} %broadcast_in_dim.7), calls=%async_computation.1 | async-start | bytes 32768 | tf_op jit(solution)/shard_map/all_to_all | solution.py:21
  (1 other events, 4.6 us)
